TPU v7x, 512 devices: a whole 4x4x16 slice. The times are simulated.
512 devices in a mesh: dp: 16 (over z), seq: 4 (over y_hi, core), tensor: 8 (over y_lo, x).
Axes of the slice: x: 4, y: 4 (y_hi: 2, y_lo: 2; y = y_hi * 2 + y_lo), z: 16, core: 2. Of those that a mesh axis runs over, the one named last changes fastest.
Arguments:
- student_hidden: bfloat16 [4, 64, 16, 4096], P('seq', None, None, 'tensor'), may hold values from -1.5 to 1.5
- teacher_hidden: bfloat16 [4, 64, 16, 16384], P('seq', None, 'dp', 'tensor'), may hold values from -24 to 24
- proj_weight: bfloat16 [4096, 16384], P('tensor', 'dp'), may hold values from -0.375 to 0.375
Outputs:
- loss_value: float32 [], replicated
- grad_weight: float32 [4096, 16384], P('tensor', 'dp')
- grad_input: bfloat16 [4, 64, 16, 4096], P('seq', 'dp', None, 'tensor')
All inputs are finite; a program needn't handle non-finite values.
Results may differ from a plain program's by a relative error of at most 0.0028.
The roundings to bfloat16 on the way count: a program that leaves them out, or rounds other values in their place, can miss the bound.
Values may be sent and summed in bfloat16 or wider, within the bound.
No kernel may reach another device: no remote copies, remote signals or barrier semaphores. Data moves between devices by JAX's collectives and lax.ppermute only.
A program may use at most 128 MiB of HBM per device.

v0:
```python
import jax
import jax.numpy as jnp
from jax import lax
from jax.sharding import PartitionSpec as P

scale_epsilon = 1e-06
grad_factor = 0.25


def quantize(values):
    wide_values = values.astype(jnp.float32)
    largest = jnp.max(jnp.abs(wide_values), axis=3)
    token_scale = largest + scale_epsilon
    quantized = (wide_values / token_scale[..., None]).astype(jnp.bfloat16)
    return (quantized, token_scale)


def body(student_hidden, teacher_hidden, proj_weight):
    width_local = student_hidden.shape[3]
    flat_rows = student_hidden.reshape(-1, width_local)
    row_count = flat_rows.shape[0]
    tensor_count = lax.axis_size("tensor")
    received = lax.all_gather(teacher_hidden, "tensor", axis=3, tiled=True)
    quantized, token_scale = quantize(received)
    columns = lax.all_to_all(quantized, "dp", split_axis=3, concat_axis=2, tiled=True)
    scales_all = lax.all_gather(token_scale, "dp", axis=2, tiled=True)
    target = columns.astype(jnp.float32).reshape(-1, columns.shape[3])
    scale_rows = scales_all.reshape(-1, 1)
    total_tokens = row_count * lax.axis_size("seq")
    total_width = proj_weight.shape[1] * lax.axis_size("dp")
    partial_sums = jnp.dot(flat_rows, proj_weight, preferred_element_type=jnp.float32)
    prediction = lax.psum(partial_sums, "tensor")
    difference = prediction / scale_rows - target
    per_device = row_count // tensor_count
    own_rows = lax.dynamic_slice_in_dim(
        difference, lax.axis_index("tensor") * per_device, per_device, 0
    )
    local_sum = jnp.sum(own_rows * own_rows)
    grad_full = (difference / scale_rows * grad_factor).astype(jnp.bfloat16)
    loss_value = lax.psum(local_sum, ("dp", "seq", "tensor")) / (total_tokens * total_width)
    weight_term = lax.dot_general(
        flat_rows, grad_full, (((0,), (0,)), ((), ())), preferred_element_type=jnp.float32
    )
    grad_weight = lax.psum(weight_term, "seq")
    grad_input = lax.psum_scatter(
        lax.dot_general(
            grad_full, proj_weight, (((1,), (1,)), ((), ())), preferred_element_type=jnp.float32
        ),
        "dp",
        scatter_dimension=0,
        tiled=True,
    ).astype(jnp.bfloat16)
    grad_input = grad_input.reshape(1, -1, student_hidden.shape[2], width_local)
    return (loss_value, grad_weight, grad_input)


def solution(mesh):
    placed = (P("seq", None, None, "tensor"), P("seq", None, "dp", "tensor"), P("tensor", "dp"))
    return jax.shard_map(
        body,
        mesh=mesh,
        in_specs=placed,
        out_specs=(P(), P("tensor", "dp"), P("seq", "dp", None, "tensor")),
        check_vma=False,
    )
```

profile of v0, /device:TPU:2, one launch (start us, length us, event | category | flops | bytes accessed | tf_op | source)
XLA Modules:
  0.0 497.2 jit_solution(15448332772953075648)
XLA Ops:
  7.2 0.0 copy-start
  7.2 0.0 all-gather.2.cloned.1.call-start
  7.2 0.7 all-gather.2.cloned.1.call-update
  7.9 53.6 %all-gather.2.cloned.1.call-done = bf16[1,64,1,16384]{3,1,2,0:T(8,128)(2,1)} async-done(((bf16[1,64,1,2048]{3,1,2,0:T(8,128)(2,1)}), bf16[1,64,1,16384]{3,1,2,0:T(8,128)(2,1)}) %all-gather.2.cloned.1.call-update) | async-done | bytes 2097168 | tf_op jit(solution)/shard_map/all_gather | solution.py:23
  61.5 2.0 fusion
  63.5 2.0 fusion.1
  65.5 12.8 %copy.21 = bf16[1,64,1,16384]{1,2,0,3:T(2,128)(2,1)} copy(bf16[1,64,1,16384]{3,1,2,0:T(8,128)(2,1)S(1)} %fusion.1) | data formatting | bytes 4194304 | tf_op jit(solution)/shard_map/convert_element_type | solution.py:14
  78.4 0.5 broadcast.15
  78.9 90.8 %reduce.1 = bf16[16384,64]{1,0:T(8,128)(2,1)} reduce(bf16[16384,1,1,64]{3,2,1,0:T(2,128)(2,1)} %bitcast.22, bf16[]{:T(256)} %broadcast.15), dimensions={1,2}, to_apply=%bitcast.12.reduce_sub_computation | reduce | bytes 4194306
  169.7 7.5 %reshape.44 = bf16[16,2,32768]{2,1,0:T(2,128)(2,1)} reshape(bf16[16384,64]{1,0:T(8,128)(2,1)} %reduce.1) | data formatting | bytes 4194304
  177.2 12.3 %all-to-all-start = ((bf16[16,2,32768]{2,1,0:T(2,128)(2,1)}), bf16[16,2,32768]{2,1,0:T(2,128)(2,1)S(1)}, u32[]{:S(2)}, u32[]{:S(2)}) async-start(bf16[16,2,32768]{2,1,0:T(2,128)(2,1)} %reshape.44), calls=%async_computation | async-start | bytes 4194304 | tf_op jit(solution)/shard_map/all_to_all | solution.py:25
  189.5 0.0 all-reduce.3.cloned.1.call-start
  189.5 0.0 copy-done
  189.5 4.4 fusion.3
  194.0 0.0 all-reduce.3.cloned.1.call-update
  194.0 0.0 all-reduce.5.cloned.1.call-start
  194.1 108.0 %all_gather.7 = f32[1,64,16]{1,0,2:T(1,128)S(1)} all-gather(f32[1,64,1]{1,0,2:T(1,128)S(1)} %get-tuple-element.21), channel_id=1, replica_groups=mesh['dp'=16,'seq'=4,'tensor'=8] {'dp'}, dimensions={2}, use_global_device_ids=true | all-gather | bytes 4352 | tf_op jit(solution)/shard_map/all_gather | solution.py:26
  302.1 0.1 copy.20
  302.2 0.1 div.27
  302.2 0.0 all-to-all-done
  302.2 8.4 %reshape.45 = bf16[16384,1,1,64]{3,2,1,0:T(2,128)(2,1)} reshape(bf16[16,2,32768]{2,1,0:T(2,128)(2,1)S(1)} %all-to-all-done) | data formatting | bytes 4194304
  310.7 15.5 %copy.22 = bf16[1,64,1,16384]{3,1,2,0:T(8,128)(2,1)S(1)} copy(bf16[1,64,1,16384]{1,2,0,3:T(2,128)(2,1)} %bitcast.23) | data formatting | bytes 4194304 | tf_op jit(solution)/shard_map/all_to_all | solution.py:25
  326.2 2.8 reshape.43
  329.0 0.0 all-reduce.3.cloned.1.call-done
  329.0 7.1 %multiply_convert_fusion = (bf16[1024,1024]{1,0:T(8,128)(2,1)S(1)}, f32[1024,1024]{1,0:T(8,128)}) fusion(f32[1024]{0:T(1024)S(1)} %div.27, f32[1024,1024]{1,0:T(8,128)} %reshape.43, f32[1024,1024]{1,0:T(8,128)} %all-reduce.3.cloned.1.call-done), kind=kLoop, calls=%fused_computation.4 | loop fusion | flops 5242880 | bytes 14684160 | tf_op jit(solution)/shard_map/convert_element_type | solution.py:39
  336.0 2.6 convolution_bitcast_fusion
  338.6 0.0 all-reduce.5.cloned.1.call-update
  338.7 0.2 reduce-scatter.2.cloned.1.call-start
  338.9 3.9 fusion.4
  342.7 0.0 reduce-scatter.2.cloned.1.call-update
  342.8 1.8 multiply_reduce_fusion
  344.6 115.7 %psum.22 = f32[]{:T(128)} all-reduce(f32[]{:T(128)} %multiply_reduce_fusion), channel_id=1, replica_groups=mesh['dp'=16,'seq'=4,'tensor'=8] {'dp','seq','tensor'}, use_global_device_ids=true, to_apply=%region_3.0 | all-reduce | flops 1 | bytes 8 | tf_op jit(solution)/shard_map/psum | solution.py:40
  460.9 0.0 all-reduce.5.cloned.1.call-done
  460.9 2.9 copy.23
  463.8 24.1 %reduce-scatter.2.cloned.1.call-done = f32[64,512]{1,0:T(8,128)} async-done(((f32[1024,512]{1,0:T(8,128)}), f32[64,512]{1,0:T(8,128)}) %reduce-scatter.2.cloned.1.call-update) | async-done | bytes 131088 | tf_op jit(solution)/shard_map/reduce_scatter | solution.py:45
  488.0 1.5 convert_element_type.26
  (1 shorter events, 0.0 us)
Async XLA Ops:
  7.2 182.4 %copy-start = (bf16[1,64,16,512]{3,2,1,0:T(8,128)(2,1)S(1)}, bf16[1,64,16,512]{3,2,1,0:T(8,128)(2,1)}, u32[]{:S(2)}) copy-start(bf16[1,64,16,512]{3,2,1,0:T(8,128)(2,1)} %param.3) | copy-start | bytes 3145732
  7.2 54.3 %all-gather.2.cloned.1.call-start = ((), (), s32[]{:S(2)}) async-start(), calls=%async_computation.3 | async-start | bytes 2359296 | tf_op jit(solution)/shard_map/all_gather | solution.py:23
  177.2 125.1 %all-to-all-start = ((bf16[16,2,32768]{2,1,0:T(2,128)(2,1)}), bf16[16,2,32768]{2,1,0:T(2,128)(2,1)S(1)}, u32[]{:S(2)}, u32[]{:S(2)}) async-start(bf16[16,2,32768]{2,1,0:T(2,128)(2,1)} %reshape.44), calls=%async_computation | async-start | bytes 4194304 | tf_op jit(solution)/shard_map/all_to_all | solution.py:25
  189.5 139.5 %all-reduce.3.cloned.1.call-start = ((), (), s32[]{:S(2)}) async-start(), calls=%async_computation.2 | async-start | bytes 8388608 | tf_op jit(solution)/shard_map/psum | solution.py:32
  194.0 266.9 %all-reduce.5.cloned.1.call-start = ((), (), s32[]{:S(2)}) async-start(), calls=%async_computation.4 | async-start | bytes 4194304 | tf_op jit(solution)/shard_map/psum | solution.py:44
  338.7 149.3 %reduce-scatter.2.cloned.1.call-start = ((), (), s32[]{:S(2)}) async-start(), calls=%async_computation.5 | async-start | bytes 2228224 | tf_op jit(solution)/shard_map/reduce_scatter | solution.py:45
Sparse Core Ops, SparseCore 0:
  10.1 51.3 all-gather.1
  194.1 119.9 all-reduce.2
  338.8 73.2 all-reduce.4
  414.9 72.9 reduce-scatter.1
where the time goes:
time: 498 us; the launch traced here: 497 us
  blocking collectives  224 us (45%)
  other arithmetic  105 us (21%)
  waiting for transfers between devices  78.5 us (16%)
  local copies, waits for them, and re-layouts  50.7 us (10%)
  between operations  15.6 us (3%)
  starting transfers between devices  12.6 us (3%)
  matrix products  10.9 us (2%)
    psum x1, blocking collectives, body(): lax.psum(local_sum, ('dp', 'seq', 'tensor')) / (total_tokens * total_width)  116 us
    all_gather x1, blocking collectives, body(): scales_all = lax.all_gather(token_scale, 'dp', axis=2, tiled=True)  108 us
    unnamed x1, other arithmetic  90.8 us
    all_gather x1, waiting for transfers between devices, body(): received = lax.all_gather(teacher_hidden, 'tensor', axis=3, tiled=True)  53.6 us
    reduce_scatter x1, waiting for transfers between devices, body(): lax.psum_scatter(lax.dot_general(grad_full, proj_weight, (((1,), (1,)), (...  24.1 us
    unnamed x6, local copies, waits for them, and re-layouts  19.4 us
    all_to_all x1, local copies, waits for them, and re-layouts, body(): lax.all_to_all(quantized, 'dp', split_axis=3, concat_axis=2, tiled=True)  15.5 us
    convert_element_type x1, local copies, waits for them, and re-layouts, quantize(): quantized = (wide_values / token_scale[..., None]).astype(jnp.bfloat16)  12.8 us
  transfers between devices with their start and end apart: 5, of which 2 were waited for; matrix products, arithmetic and copies ran while one was open for 8% of the time, Pallas kernels for 0%

commit v1 on v0

v1 whole, which is shorter than its diff:
```python
import jax
import jax.numpy as jnp
from jax import lax
from jax.experimental import pallas as pl
from jax.experimental.pallas import tpu as pltpu
from jax.sharding import PartitionSpec as P

scale_epsilon = 1e-06
grad_factor = 0.25
LANES = 128
META = 16
TOP = 14.0
bf16, f16, f32 = jnp.bfloat16, jnp.float16, jnp.float32


def call(kernel, out_shape, flops, nbytes, **kw):
    return pl.pallas_call(
        kernel,
        out_shape=out_shape,
        cost_estimate=pl.CostEstimate(flops=flops, bytes_accessed=nbytes, transcendentals=0),
        compiler_params=pltpu.CompilerParams(vmem_limit_bytes=40 * 1024 * 1024),
        **kw,
    )


def all_to_all(x, axis):
    return lax.all_to_all(x, axis, 0, 0)


def exponent_of(largest):
    return jnp.clip(jnp.ceil(jnp.log2(jnp.maximum(largest, 1e-30))), -100.0, 100.0)


def pack_teacher(x_ref, o_ref):
    rows = x_ref[...].astype(f32)
    largest = jnp.max(jnp.max(jnp.abs(rows).reshape(8, 8, -1), axis=0), axis=1, keepdims=True)
    half = rows.shape[1] // 2
    wide = jnp.broadcast_to(jnp.concatenate([largest, largest], axis=0), (16, LANES)).astype(bf16)
    for t in range(8):
        block = rows[8 * t : 8 * t + 8]
        both = jnp.concatenate([block[:, :half], block[:, half:]], axis=0)
        o_ref[16 * t : 16 * t + 16, :half] = both.astype(bf16)
        o_ref[16 * t : 16 * t + 16, half:] = wide


def forward(s_ref, w_ref, o_ref):
    partial = jnp.dot(s_ref[...], w_ref[...], preferred_element_type=f32)
    power = exponent_of(jnp.max(jnp.abs(partial), axis=1, keepdims=True))
    scaled = partial * jnp.exp2(TOP - power)
    rows, width = scaled.shape
    for c in range(width // LANES):
        o_ref[0, c * rows : (c + 1) * rows, :] = scaled[:, c * LANES : (c + 1) * LANES]
    meta = jnp.transpose(jnp.broadcast_to(power, (rows, LANES)))
    o_ref[0, width // LANES * rows :, :] = meta[:META]


def token_grad(pred_ref, tgt_ref, o_ref, held):
    blocks, rows, _ = pred_ref.shape

    @pl.when(pl.program_id(0) == 0)
    def _():
        r = lax.broadcasted_iota(jnp.int32, (rows, rows), 0)
        q = lax.broadcasted_iota(jnp.int32, (rows, rows), 1)
        order = jnp.where(q == (r % 16) * 8 + r // 16, 1.0, 0.0).astype(bf16)
        target = jnp.dot(order, tgt_ref[...], preferred_element_type=f32)
        token_scale = target[:, blocks * LANES : blocks * LANES + 1] + scale_epsilon
        total = jnp.zeros((rows, LANES), f32)
        for c in range(blocks):
            quantized = (target[:, c * LANES : (c + 1) * LANES] / token_scale).astype(bf16)
            difference = pred_ref[c] / token_scale - quantized.astype(f32)
            total = total + difference * difference
            held[c * rows : (c + 1) * rows, :] = ((difference / token_scale) * grad_factor).astype(bf16)
        loss = jnp.sum(jnp.sum(total, axis=0, keepdims=True), axis=1, keepdims=True)
        high = loss.astype(bf16).astype(f32)
        middle = (loss - high).astype(bf16).astype(f32)
        low = loss - high - middle
        row = lax.broadcasted_iota(jnp.int32, (META, LANES), 0)
        pieces = jnp.where(row == 0, high, jnp.where(row == 1, middle, jnp.where(row == 2, low, 0.0)))
        held[blocks * rows :, :] = pieces.astype(bf16)

    o_ref[0] = held[...]


def input_grad(g_ref, w_ref, o_ref, loss_ref):
    rows = 128

    @pl.when(pl.program_id(0) == 0)
    def _():
        loss_ref[...] = jnp.zeros_like(loss_ref)

    pieces = g_ref[0, 8 * rows :, :].astype(f32)
    loss_ref[...] += jnp.sum(pieces, axis=0, keepdims=True)
    grad = jnp.concatenate([g_ref[0, c * rows : (c + 1) * rows, :] for c in range(8)], axis=1)
    partial = lax.dot_general(grad, w_ref[...], (((1,), (1,)), ((), ())), preferred_element_type=f32)
    for n in range(2):
        chunk = partial[64 * n : 64 * n + 64]
        largest = jnp.max(jnp.max(jnp.abs(chunk), axis=0, keepdims=True), axis=1, keepdims=True)
        power = exponent_of(largest)
        scaled = chunk * jnp.exp2(TOP - power)
        for c in range(4):
            o_ref[n, 64 * c : 64 * c + 64, :] = scaled[:, c * LANES : (c + 1) * LANES]
        o_ref[n, 256:, :] = jnp.broadcast_to(power, (META, LANES))


def weight_grad(core_ref, s_ref, g_ref, after_ref, send_ref, keep_ref):
    del after_ref
    tokens, width = s_ref.shape
    half = width // 2
    rows = 128
    grad = jnp.concatenate(
        [g_ref[:, c * rows : (c + 1) * rows, :].reshape(tokens, LANES) for c in range(2)], axis=1
    )
    core = core_ref[0]
    for ref, which in ((send_ref, 1 - core), (keep_ref, core)):
        part = s_ref[:, pl.ds(pl.multiple_of(which * half, half), half)]
        ref[...] = lax.dot_general(part, grad, (((0,), (0,)), ((), ())), preferred_element_type=f32)


def body(student_hidden, teacher_hidden, proj_weight):
    width_local = student_hidden.shape[3]
    student = student_hidden.reshape(-1, width_local)
    tokens, columns = student.shape[0], proj_weight.shape[1]
    tensor_count, dp_count, seq_count = (lax.axis_size(a) for a in ("tensor", "dp", "seq"))
    own = tokens // tensor_count
    blocks = columns // LANES

    with jax.named_scope("teacher"):
        spread = all_to_all(teacher_hidden.reshape(8, 8, -1), "tensor")
        packed = call(
            pack_teacher,
            jax.ShapeDtypeStruct((128, columns + LANES), bf16),
            0,
            600_000,
        )(spread.reshape(64, -1))
        target = all_to_all(packed.reshape(16, 8, -1), "dp").reshape(own, -1)

    with jax.named_scope("prediction"):
        size = blocks * own + META
        partial = call(
            forward,
            jax.ShapeDtypeStruct((tensor_count, size, LANES), f32),
            2 * tokens * width_local * columns,
            6_000_000,
            grid=(tensor_count,),
            in_specs=[
                pl.BlockSpec((own, width_local), lambda i: (i, 0)),
                pl.BlockSpec((width_local, columns), lambda i: (0, 0)),
            ],
            out_specs=pl.BlockSpec((1, size, LANES), lambda i: (i, 0, 0)),
        )(student, proj_weight)
        parts = all_to_all(partial.astype(f16), "tensor").astype(f32)
        unscale = jnp.exp2(parts[:, blocks * own, :] - TOP)
        data = parts[:, : blocks * own, :].reshape(tensor_count, blocks, own, LANES)
        prediction = jnp.sum(data * unscale[:, None, :, None], axis=0)

    with jax.named_scope("gradient"):
        grad_own = call(
            token_grad,
            jax.ShapeDtypeStruct((tensor_count, size, LANES), bf16),
            2 * own * own * columns,
            3_000_000,
            grid=(tensor_count,),
            in_specs=[
                pl.BlockSpec((blocks, own, LANES), lambda i: (0, 0, 0)),
                pl.BlockSpec((own, columns + LANES), lambda i: (0, 0)),
            ],
            out_specs=pl.BlockSpec((1, size, LANES), lambda i: (i, 0, 0)),
            scratch_shapes=[pltpu.VMEM((size, LANES), bf16)],
        )(prediction, target)
        grad = all_to_all(grad_own, "tensor")

    with jax.named_scope("input_grad"):
        chunk = 64 * 4 + META
        term, loss = call(
            input_grad,
            (jax.ShapeDtypeStruct((dp_count, chunk, LANES), f32), jax.ShapeDtypeStruct((1, LANES), f32)),
            2 * tokens * width_local * columns,
            5_000_000,
            grid=(tensor_count,),
            in_specs=[
                pl.BlockSpec((1, size, LANES), lambda i: (i, 0, 0)),
                pl.BlockSpec((width_local, columns), lambda i: (0, 0)),
            ],
            out_specs=(
                pl.BlockSpec((2, chunk, LANES), lambda i: (i, 0, 0)),
                pl.BlockSpec((1, LANES), lambda i: (0, 0)),
            ),
        )(grad, proj_weight)
        terms = all_to_all(term.astype(f16), "dp").astype(f32)
        unscale = jnp.exp2(terms[:, 256:257, 0:1] - TOP)
        summed = jnp.sum(terms[:, :256, :] * unscale, axis=0)
        grad_input = jnp.transpose(summed.reshape(4, 64, LANES), (1, 0, 2)).astype(bf16)
        grad_input = grad_input.reshape(1, 4, 16, width_local)

    with jax.named_scope("weight_grad"):
        seq_index = lax.axis_index("seq")
        core = seq_index % 2
        other_core = [(i, i ^ 1) for i in range(seq_count)]
        other_y = [(i, i ^ 2) for i in range(seq_count)]
        half = jax.ShapeDtypeStruct((width_local // 2, columns), f32)
        send, keep = call(
            weight_grad,
            (half, half),
            2 * tokens * width_local * columns,
            5_000_000,
            grid=(4,),
            in_specs=[
                pl.BlockSpec(memory_space=pltpu.SMEM),
                pl.BlockSpec((tokens, width_local), lambda i: (0, 0)),
                pl.BlockSpec((tensor_count, 2 * own, LANES), lambda i: (0, i, 0)),
                pl.BlockSpec((1, LANES), lambda i: (0, 0)),
            ],
            out_specs=(
                pl.BlockSpec((width_local // 2, 2 * LANES), lambda i: (0, i)),
                pl.BlockSpec((width_local // 2, 2 * LANES), lambda i: (0, i)),
            ),
        )(core.reshape(1).astype(jnp.int32), student, grad, loss)
        pair = (keep + lax.ppermute(send, "seq", other_core)).astype(bf16)
        mine = pair.astype(f32) + lax.ppermute(pair, "seq", other_y).astype(f32)
        theirs = lax.ppermute(mine, "seq", other_core)
        grad_weight = jnp.where(
            core == 0,
            jnp.concatenate([mine, theirs], axis=0),
            jnp.concatenate([theirs, mine], axis=0),
        )

    with jax.named_scope("loss"):
        for axis, step in (("dp", 1), ("dp", 2), ("dp", 4), ("dp", 8), ("seq", 1), ("seq", 2)):
            moves = [(i, i ^ step) for i in range(lax.axis_size(axis))]
            loss = loss + lax.ppermute(loss, axis, moves)
        loss_value = loss[0, 0] / (tokens * seq_count * columns * dp_count)
    return (loss_value, grad_weight, grad_input)


def solution(mesh):
    placed = (P("seq", None, None, "tensor"), P("seq", None, "dp", "tensor"), P("tensor", "dp"))
    return jax.shard_map(
        body,
        mesh=mesh,
        in_specs=placed,
        out_specs=(P(), P("tensor", "dp"), P("seq", "dp", None, "tensor")),
        check_vma=False,
    )
```

time: 498 us -> 218 us (0.44)
  the two profiles are of different devices: /device:TPU:2 before, /device:TPU:1 now
where the time goes in v1:
time: 218 us; the launch traced here: 217 us
  starting transfers between devices  95.1 us (44%)
  waiting for transfers between devices  71.9 us (33%)
  blocking collectives  24.2 us (11%)
  Pallas kernels  12.7 us (6%)
  other arithmetic  8.11 us (4%)
  local copies, waits for them, and re-layouts  3.18 us (1%)
    all_to_all x4, starting transfers between devices, all_to_all(): return lax.all_to_all(x, axis, 0, 0)  42.7 us
    ppermute x6, starting transfers between devices, body(): loss = loss + lax.ppermute(loss, axis, moves)  40.4 us
    all_to_all x4, waiting for transfers between devices, all_to_all(): return lax.all_to_all(x, axis, 0, 0)  38.3 us
    all_to_all x1, blocking collectives, all_to_all(): return lax.all_to_all(x, axis, 0, 0)  24.2 us
    ppermute x6, waiting for transfers between devices, body(): loss = loss + lax.ppermute(loss, axis, moves)  19.2 us
    ppermute x1, waiting for transfers between devices, body(): mine = pair.astype(f32) + lax.ppermute(pair, 'seq', other_y).astype(f32)  12.1 us
    pallas_call x1, Pallas kernels, body(): call(input_grad, (jax.ShapeDtypeStruct((dp_count, chunk, LANES), f32), ja...  4.81 us
    ppermute x1, starting transfers between devices, body(): mine = pair.astype(f32) + lax.ppermute(pair, 'seq', other_y).astype(f32)  4.52 us
  transfers between devices with their start and end apart: 13, of which 10 were waited for; matrix products, arithmetic and copies ran while one was open for 2% of the time, Pallas kernels for 3%

profile of v1, /device:TPU:1, one launch (start us, length us, event | category | flops | bytes accessed | tf_op | source)
XLA Modules:
  0.0 217.3 jit_solution(6361464338422772148)
XLA Ops:
  0.6 5.9 %all-to-all-start.1 = ((bf16[8,8,2048]{2,1,0:T(8,128)(2,1)}), bf16[8,8,2048]{2,1,0:T(8,128)(2,1)S(1)}, u32[]{:S(2)}, u32[]{:S(2)}) async-start(bf16[8,8,2048]{2,1,0:T(8,128)(2,1)} %bitcast.21), calls=%async_computation.1 | async-start | bytes 524288 | tf_op jit(solution)/shard_map/teacher/all_to_all | solution.py:27
  6.5 1.2 copy-done
  7.7 1.2 copy-done.2
  9.0 3.6 %prediction.1 = f32[8,1040,128]{2,1,0:T(8,128)S(1)} custom-call(bf16[1024,512]{1,0:T(8,128)(2,1)S(1)} %bitcast.17, bf16[512,1024]{1,0:T(8,128)(2,1)S(1)} %copy-done), custom_call_target="tpu_custom_call" | custom-call | flops 1073741824 | bytes 6000000 | tf_op jit(solution)/shard_map/prediction/pallas_call | solution.py:139
  12.5 1.6 convert_element_type.30
  14.1 0.0 all-to-all-done.1
  14.1 5.1 %all-to-all-start = ((f16[8,1040,128]{2,1,0:T(8,128)(2,1)}), f16[8,1040,128]{2,1,0:T(8,128)(2,1)S(1)}, u32[]{:S(2)}, u32[]{:S(2)}) async-start(f16[8,1040,128]{2,1,0:T(8,128)(2,1)} %convert_element_type.30), calls=%async_computation | async-start | bytes 4259840 | tf_op jit(solution)/shard_map/prediction/all_to_all | solution.py:27
  19.3 0.9 teacher.1
  20.2 26.5 %all-to-all-done = f16[8,1040,128]{2,1,0:T(8,128)(2,1)S(1)} async-done(((f16[8,1040,128]{2,1,0:T(8,128)(2,1)}), f16[8,1040,128]{2,1,0:T(8,128)(2,1)S(1)}, u32[]{:S(2)}, u32[]{:S(2)}) %all-to-all-start) | async-done | bytes 2129952 | tf_op jit(solution)/shard_map/prediction/all_to_all | solution.py:27
  46.7 14.9 %all-to-all-start.2 = ((bf16[16,8,1152]{2,1,0:T(8,128)(2,1)}), bf16[16,8,1152]{2,1,0:T(8,128)(2,1)S(1)}, u32[]{:S(2)}, u32[]{:S(2)}) async-start(bf16[16,8,1152]{2,1,0:T(8,128)(2,1)} %bitcast.6), calls=%async_computation.2 | async-start | bytes 589824 | tf_op jit(solution)/shard_map/teacher/all_to_all | solution.py:27
  61.6 0.3 convert_element_type.31
  61.9 1.4 fusion
  63.3 11.8 %all-to-all-done.2 = bf16[16,8,1152]{2,1,0:T(8,128)(2,1)S(1)} async-done(((bf16[16,8,1152]{2,1,0:T(8,128)(2,1)}), bf16[16,8,1152]{2,1,0:T(8,128)(2,1)S(1)}, u32[]{:S(2)}, u32[]{:S(2)}) %all-to-all-start.2) | async-done | bytes 294944 | tf_op jit(solution)/shard_map/teacher/all_to_all | solution.py:27
  75.1 0.8 gradient.1
  76.0 0.0 copy-start.1
  76.0 24.2 %all_to_all.25.g_ref = bf16[8,1040,128]{2,1,0:T(8,128)(2,1)S(1)} all-to-all(bf16[8,1040,128]{2,1,0:T(8,128)(2,1)S(1)} %gradient.1), channel_id=1, replica_groups=mesh['dp'=16,'seq'=4,'tensor'=8] {'tensor'}, dimensions={0} | all-to-all | bytes 4259840 | tf_op jit(solution)/shard_map/gradient/all_to_all | solution.py:27
  100.2 4.8 %input_grad.1 = (f32[16,272,128]{2,1,0:T(8,128)S(1)}, f32[1,128]{1,0:T(1,128)S(1)}) custom-call(bf16[8,1040,128]{2,1,0:T(8,128)(2,1)S(1)} %all_to_all.25.g_ref, bf16[512,1024]{1,0:T(8,128)(2,1)S(1)} %copy-done.1), custom_call_target="tpu_custom_call" | custom-call | flops 1073741824 | bytes 5000000 | tf_op jit(solution)/shard_map/input_grad/pallas_call | solution.py:174
  105.0 0.0 copy-start.3
  105.0 1.1 convert_element_type.35
  106.2 16.7 %all-to-all-start.4 = ((f16[16,272,128]{2,1,0:T(8,128)(2,1)}), f16[16,272,128]{2,1,0:T(8,128)(2,1)}, u32[]{:S(2)}, u32[]{:S(2)}) async-start(f16[16,272,128]{2,1,0:T(8,128)(2,1)} %convert_element_type.35), calls=%async_computation.4 | async-start | bytes 2228224 | tf_op jit(solution)/shard_map/input_grad/all_to_all | solution.py:27
  122.9 2.6 %weight_grad.1 = (f32[256,1024]{1,0:T(8,128)S(1)}, f32[256,1024]{1,0:T(8,128)S(1)}) custom-call(s32[1]{0:T(128)} %bitcast.9.core_ref, bf16[1024,512]{1,0:T(8,128)(2,1)S(1)} %bitcast.18, bf16[8,1040,128]{2,1,0:T(8,128)(2,1)S(1)} %all_to_all.25.g_ref, f32[1,128]{1,0:T(1,128)S(1)} %get-tuple-element.7.after_ref), custom_call_target="tpu_custom_call" | custom-call | flops 1073741824 | bytes 5000000 | tf_op jit(solution)/shard_map/weight_grad/pallas_call | solution.py:201
  125.6 4.5 %collective-permute-start.6 = (f32[256,1024]{1,0:T(8,128)S(1)}, f32[256,1024]{1,0:T(8,128)S(1)}, u32[]{:S(2)}, u32[]{:S(2)}) collective-permute-start(f32[256,1024]{1,0:T(8,128)S(1)} %get-tuple-element.9), channel_id=1, source_target_pairs={{0,8},{8,0},{16,24},{24,16},{1,9},{9,1},{17,25},{25,17},{2,10},{10... | collective-permute-start | bytes 3145736 | tf_op jit(solution)/shard_map/weight_grad/ppermute | solution.py:218
  130.1 2.3 %collective-permute-done.6 = f32[256,1024]{1,0:T(8,128)S(1)} collective-permute-done((f32[256,1024]{1,0:T(8,128)S(1)}, f32[256,1024]{1,0:T(8,128)S(1)}, u32[]{:S(2)}, u32[]{:S(2)}) %collective-permute-start.6) | collective-permute-done | bytes 1048608 | tf_op jit(solution)/shard_map/weight_grad/ppermute | solution.py:218
  132.3 0.2 add_convert_fusion
  132.5 4.5 %collective-permute-start.7 = (bf16[256,1024]{1,0:T(8,128)(2,1)S(1)}, bf16[256,1024]{1,0:T(8,128)(2,1)S(1)}, u32[]{:S(2)}, u32[]{:S(2)}) collective-permute-start(bf16[256,1024]{1,0:T(8,128)(2,1)S(1)} %add_convert_fusion), channel_id=1, source_target_pairs={{0,16},{8,24},{16,0},{24,8},{1,17},{9,25},{17,1},{25,9},{2,18},{10... | collective-permute-start | bytes 1572872 | tf_op jit(solution)/shard_map/weight_grad/ppermute | solution.py:219
  137.0 12.1 %collective-permute-done.7 = bf16[256,1024]{1,0:T(8,128)(2,1)S(1)} collective-permute-done((bf16[256,1024]{1,0:T(8,128)(2,1)S(1)}, bf16[256,1024]{1,0:T(8,128)(2,1)S(1)}, u32[]{:S(2)}, u32[]{:S(2)}) %collective-permute-start.7) | collective-permute-done | bytes 524320 | tf_op jit(solution)/shard_map/weight_grad/ppermute | solution.py:219
  149.1 0.2 convert_add_fusion
  149.3 3.0 %collective-permute-start.8 = (f32[256,1024]{1,0:T(8,128)S(1)}, f32[256,1024]{1,0:T(8,128)S(1)}, u32[]{:S(2)}, u32[]{:S(2)}) collective-permute-start(f32[256,1024]{1,0:T(8,128)S(1)} %convert_add_fusion), channel_id=1, source_target_pairs={{0,8},{8,0},{16,24},{24,16},{1,9},{9,1},{17,25},{25,17},{2,10},{10... | collective-permute-start | bytes 3145736 | tf_op jit(solution)/shard_map/weight_grad/ppermute | solution.py:220
  152.3 3.5 %collective-permute-start = (f32[1,128]{1,0:T(1,128)S(1)}, f32[1,128]{1,0:T(1,128)S(1)}, u32[]{:S(2)}, u32[]{:S(2)}) collective-permute-start(f32[1,128]{1,0:T(1,128)S(1)} %get-tuple-element.7.after_ref), channel_id=1, source_target_pairs={{0,32},{32,0},{64,96},{96,64},{128,160},{160,128},{192,224},{224,1... | collective-permute-start | bytes 1544 | tf_op jit(solution)/shard_map/loss/ppermute | solution.py:230
  155.8 14.2 %collective-permute-done = f32[1,128]{1,0:T(1,128)S(1)} collective-permute-done((f32[1,128]{1,0:T(1,128)S(1)}, f32[1,128]{1,0:T(1,128)S(1)}, u32[]{:S(2)}, u32[]{:S(2)}) %collective-permute-start) | collective-permute-done | bytes 544 | tf_op jit(solution)/shard_map/loss/ppermute | solution.py:230
  170.0 4.6 %collective-permute-start.1 = (f32[1,128]{1,0:T(1,128)S(1)}, f32[1,128]{1,0:T(1,128)S(1)}, u32[]{:S(2)}, u32[]{:S(2)}) collective-permute-start(f32[1,128]{1,0:T(1,128)S(1)} %add.35), channel_id=1, source_target_pairs={{0,64},{32,96},{64,0},{96,32},{128,192},{160,224},{192,128},{224,1... | collective-permute-start | bytes 1544 | tf_op jit(solution)/shard_map/loss/ppermute | solution.py:230
  174.6 0.9 collective-permute-done.1
  175.5 8.6 %collective-permute-start.2 = (f32[1,128]{1,0:T(1,128)S(1)}, f32[1,128]{1,0:T(1,128)S(1)}, u32[]{:S(2)}, u32[]{:S(2)}) collective-permute-start(f32[1,128]{1,0:T(1,128)S(1)} %add.36), channel_id=1, source_target_pairs={{0,128},{32,160},{64,192},{96,224},{128,0},{160,32},{192,64},{224,... | collective-permute-start | bytes 1544 | tf_op jit(solution)/shard_map/loss/ppermute | solution.py:230
  184.1 0.9 collective-permute-done.2
  185.1 11.8 %collective-permute-start.3 = (f32[1,128]{1,0:T(1,128)S(1)}, f32[1,128]{1,0:T(1,128)S(1)}, u32[]{:S(2)}, u32[]{:S(2)}) collective-permute-start(f32[1,128]{1,0:T(1,128)S(1)} %add.37), channel_id=1, source_target_pairs={{0,256},{32,288},{64,320},{96,352},{128,384},{160,416},{192,448},{... | collective-permute-start | bytes 1544 | tf_op jit(solution)/shard_map/loss/ppermute | solution.py:230
  196.8 1.2 collective-permute-done.3
  198.1 7.4 %collective-permute-start.4 = (f32[1,128]{1,0:T(1,128)S(1)}, f32[1,128]{1,0:T(1,128)S(1)}, u32[]{:S(2)}, u32[]{:S(2)}) collective-permute-start(f32[1,128]{1,0:T(1,128)S(1)} %add.38), channel_id=1, source_target_pairs={{0,8},{8,0},{16,24},{24,16},{1,9},{9,1},{17,25},{25,17},{2,10},{10... | collective-permute-start | bytes 1544 | tf_op jit(solution)/shard_map/loss/ppermute | solution.py:230
  205.5 0.8 collective-permute-done.4
  206.3 4.5 %collective-permute-start.5 = (f32[1,128]{1,0:T(1,128)S(1)}, f32[1,128]{1,0:T(1,128)S(1)}, u32[]{:S(2)}, u32[]{:S(2)}) collective-permute-start(f32[1,128]{1,0:T(1,128)S(1)} %add.39), channel_id=1, source_target_pairs={{0,16},{8,24},{16,0},{24,8},{1,17},{9,25},{17,1},{25,9},{2,18},{10... | collective-permute-start | bytes 1544 | tf_op jit(solution)/shard_map/loss/ppermute | solution.py:230
  210.9 1.2 collective-permute-done.5
  212.1 0.0 collective-permute-done.8
  212.1 1.5 maximum_select_fusion
  213.6 0.0 all-to-all-done.4
  213.6 1.4 convert_element_type.36
  215.0 0.2 fusion.4
  215.2 0.2 fusion.1
  215.5 0.1 copy.6
  215.5 0.7 reshape.52
  (12 shorter events, 0.0 us)
Async XLA Ops:
  0.6 13.5 %all-to-all-start.1 = ((bf16[8,8,2048]{2,1,0:T(8,128)(2,1)}), bf16[8,8,2048]{2,1,0:T(8,128)(2,1)S(1)}, u32[]{:S(2)}, u32[]{:S(2)}) async-start(bf16[8,8,2048]{2,1,0:T(8,128)(2,1)} %bitcast.21), calls=%async_computation.1 | async-start | bytes 524288 | tf_op jit(solution)/shard_map/teacher/all_to_all | solution.py:27
  6.5 1.2 copy-start
  7.7 1.2 copy-start.2
  14.1 32.5 %all-to-all-start = ((f16[8,1040,128]{2,1,0:T(8,128)(2,1)}), f16[8,1040,128]{2,1,0:T(8,128)(2,1)S(1)}, u32[]{:S(2)}, u32[]{:S(2)}) async-start(f16[8,1040,128]{2,1,0:T(8,128)(2,1)} %convert_element_type.30), calls=%async_computation | async-start | bytes 4259840 | tf_op jit(solution)/shard_map/prediction/all_to_all | solution.py:27
  46.7 28.5 %all-to-all-start.2 = ((bf16[16,8,1152]{2,1,0:T(8,128)(2,1)}), bf16[16,8,1152]{2,1,0:T(8,128)(2,1)S(1)}, u32[]{:S(2)}, u32[]{:S(2)}) async-start(bf16[16,8,1152]{2,1,0:T(8,128)(2,1)} %bitcast.6), calls=%async_computation.2 | async-start | bytes 589824 | tf_op jit(solution)/shard_map/teacher/all_to_all | solution.py:27
  76.0 24.3 %copy-start.1 = (bf16[512,1024]{1,0:T(8,128)(2,1)S(1)}, bf16[512,1024]{1,0:T(8,128)(2,1)}, u32[]{:S(2)}) copy-start(bf16[512,1024]{1,0:T(8,128)(2,1)} %w_ref.3) | copy-start | bytes 3145732
  105.0 17.9 %copy-start.3 = (bf16[1,64,16,512]{3,2,1,0:T(8,128)(2,1)S(1)}, bf16[1,64,16,512]{3,2,1,0:T(8,128)(2,1)}, u32[]{:S(2)}) copy-start(bf16[1,64,16,512]{3,2,1,0:T(8,128)(2,1)} %param.3) | copy-start | bytes 3145732
  106.2 107.5 %all-to-all-start.4 = ((f16[16,272,128]{2,1,0:T(8,128)(2,1)}), f16[16,272,128]{2,1,0:T(8,128)(2,1)}, u32[]{:S(2)}, u32[]{:S(2)}) async-start(f16[16,272,128]{2,1,0:T(8,128)(2,1)} %convert_element_type.35), calls=%async_computation.4 | async-start | bytes 2228224 | tf_op jit(solution)/shard_map/input_grad/all_to_all | solution.py:27
  125.6 6.8 %collective-permute-start.6 = (f32[256,1024]{1,0:T(8,128)S(1)}, f32[256,1024]{1,0:T(8,128)S(1)}, u32[]{:S(2)}, u32[]{:S(2)}) collective-permute-start(f32[256,1024]{1,0:T(8,128)S(1)} %get-tuple-element.9), channel_id=1, source_target_pairs={{0,8},{8,0},{16,24},{24,16},{1,9},{9,1},{17,25},{25,17},{2,10},{10... | collective-permute-start | bytes 3145736 | tf_op jit(solution)/shard_map/weight_grad/ppermute | solution.py:218
  132.5 16.6 %collective-permute-start.7 = (bf16[256,1024]{1,0:T(8,128)(2,1)S(1)}, bf16[256,1024]{1,0:T(8,128)(2,1)S(1)}, u32[]{:S(2)}, u32[]{:S(2)}) collective-permute-start(bf16[256,1024]{1,0:T(8,128)(2,1)S(1)} %add_convert_fusion), channel_id=1, source_target_pairs={{0,16},{8,24},{16,0},{24,8},{1,17},{9,25},{17,1},{25,9},{2,18},{10... | collective-permute-start | bytes 1572872 | tf_op jit(solution)/shard_map/weight_grad/ppermute | solution.py:219
  149.3 62.8 %collective-permute-start.8 = (f32[256,1024]{1,0:T(8,128)S(1)}, f32[256,1024]{1,0:T(8,128)S(1)}, u32[]{:S(2)}, u32[]{:S(2)}) collective-permute-start(f32[256,1024]{1,0:T(8,128)S(1)} %convert_add_fusion), channel_id=1, source_target_pairs={{0,8},{8,0},{16,24},{24,16},{1,9},{9,1},{17,25},{25,17},{2,10},{10... | collective-permute-start | bytes 3145736 | tf_op jit(solution)/shard_map/weight_grad/ppermute | solution.py:220
  152.3 17.7 %collective-permute-start = (f32[1,128]{1,0:T(1,128)S(1)}, f32[1,128]{1,0:T(1,128)S(1)}, u32[]{:S(2)}, u32[]{:S(2)}) collective-permute-start(f32[1,128]{1,0:T(1,128)S(1)} %get-tuple-element.7.after_ref), channel_id=1, source_target_pairs={{0,32},{32,0},{64,96},{96,64},{128,160},{160,128},{192,224},{224,1... | collective-permute-start | bytes 1544 | tf_op jit(solution)/shard_map/loss/ppermute | solution.py:230
  170.0 5.5 %collective-permute-start.1 = (f32[1,128]{1,0:T(1,128)S(1)}, f32[1,128]{1,0:T(1,128)S(1)}, u32[]{:S(2)}, u32[]{:S(2)}) collective-permute-start(f32[1,128]{1,0:T(1,128)S(1)} %add.35), channel_id=1, source_target_pairs={{0,64},{32,96},{64,0},{96,32},{128,192},{160,224},{192,128},{224,1... | collective-permute-start | bytes 1544 | tf_op jit(solution)/shard_map/loss/ppermute | solution.py:230
  175.5 9.5 %collective-permute-start.2 = (f32[1,128]{1,0:T(1,128)S(1)}, f32[1,128]{1,0:T(1,128)S(1)}, u32[]{:S(2)}, u32[]{:S(2)}) collective-permute-start(f32[1,128]{1,0:T(1,128)S(1)} %add.36), channel_id=1, source_target_pairs={{0,128},{32,160},{64,192},{96,224},{128,0},{160,32},{192,64},{224,... | collective-permute-start | bytes 1544 | tf_op jit(solution)/shard_map/loss/ppermute | solution.py:230
  185.1 13.0 %collective-permute-start.3 = (f32[1,128]{1,0:T(1,128)S(1)}, f32[1,128]{1,0:T(1,128)S(1)}, u32[]{:S(2)}, u32[]{:S(2)}) collective-permute-start(f32[1,128]{1,0:T(1,128)S(1)} %add.37), channel_id=1, source_target_pairs={{0,256},{32,288},{64,320},{96,352},{128,384},{160,416},{192,448},{... | collective-permute-start | bytes 1544 | tf_op jit(solution)/shard_map/loss/ppermute | solution.py:230
  198.1 8.2 %collective-permute-start.4 = (f32[1,128]{1,0:T(1,128)S(1)}, f32[1,128]{1,0:T(1,128)S(1)}, u32[]{:S(2)}, u32[]{:S(2)}) collective-permute-start(f32[1,128]{1,0:T(1,128)S(1)} %add.38), channel_id=1, source_target_pairs={{0,8},{8,0},{16,24},{24,16},{1,9},{9,1},{17,25},{25,17},{2,10},{10... | collective-permute-start | bytes 1544 | tf_op jit(solution)/shard_map/loss/ppermute | solution.py:230
  206.3 5.8 %collective-permute-start.5 = (f32[1,128]{1,0:T(1,128)S(1)}, f32[1,128]{1,0:T(1,128)S(1)}, u32[]{:S(2)}, u32[]{:S(2)}) collective-permute-start(f32[1,128]{1,0:T(1,128)S(1)} %add.39), channel_id=1, source_target_pairs={{0,16},{8,24},{16,0},{24,8},{1,17},{9,25},{17,1},{25,9},{2,18},{10... | collective-permute-start | bytes 1544 | tf_op jit(solution)/shard_map/loss/ppermute | solution.py:230

commit v2 on v1

--- a/solution.py
+++ b/solution.py
@@ -18,7 +18,7 @@
         kernel,
         out_shape=out_shape,
         cost_estimate=pl.CostEstimate(flops=flops, bytes_accessed=nbytes, transcendentals=0),
-        compiler_params=pltpu.CompilerParams(vmem_limit_bytes=40 * 1024 * 1024),
+        compiler_params=pltpu.CompilerParams(vmem_limit_bytes=16 * 1024 * 1024),
         **kw,
     )
 
@@ -31,39 +31,59 @@
     return jnp.clip(jnp.ceil(jnp.log2(jnp.maximum(largest, 1e-30))), -100.0, 100.0)
 
 
-def pack_teacher(x_ref, o_ref):
+def pack_teacher(place_ref, x_ref, *refs):
+    held = refs[4]
     rows = x_ref[...].astype(f32)
     largest = jnp.max(jnp.max(jnp.abs(rows).reshape(8, 8, -1), axis=0), axis=1, keepdims=True)
-    half = rows.shape[1] // 2
     wide = jnp.broadcast_to(jnp.concatenate([largest, largest], axis=0), (16, LANES)).astype(bf16)
+    half = rows.shape[1] // 4
     for t in range(8):
-        block = rows[8 * t : 8 * t + 8]
-        both = jnp.concatenate([block[:, :half], block[:, half:]], axis=0)
-        o_ref[16 * t : 16 * t + 16, :half] = both.astype(bf16)
-        o_ref[16 * t : 16 * t + 16, half:] = wide
+        for j in range(2):
+            block = rows[8 * t : 8 * t + 8, 2 * half * j : 2 * half * (j + 1)]
+            both = jnp.concatenate([block[:, :half], block[:, half:]], axis=0)
+            low, high = 2 * (t % 2) + j, t // 2
+            held[low, 16 * high : 16 * high + 16, :half] = both.astype(bf16)
+            held[low, 16 * high : 16 * high + 16, half:] = wide
+    for k in range(4):
+        refs[k][...] = held[(place_ref[1] + k) & 3]
+
+
+def regroup_teacher(place_ref, *refs):
+    for m in range(4):
+        high = (place_ref[0] + m) & 3
+        for k in range(4):
+            refs[4 + m][16 * k : 16 * k + 16, :] = refs[k][pl.ds(pl.multiple_of(16 * high, 16), 16), :]
 
 
 def forward(s_ref, w_ref, o_ref):
     partial = jnp.dot(s_ref[...], w_ref[...], preferred_element_type=f32)
     power = exponent_of(jnp.max(jnp.abs(partial), axis=1, keepdims=True))
     scaled = partial * jnp.exp2(TOP - power)
-    rows, width = scaled.shape
-    for c in range(width // LANES):
-        o_ref[0, c * rows : (c + 1) * rows, :] = scaled[:, c * LANES : (c + 1) * LANES]
-    meta = jnp.transpose(jnp.broadcast_to(power, (rows, LANES)))
-    o_ref[0, width // LANES * rows :, :] = meta[:META]
-
-
-def token_grad(pred_ref, tgt_ref, o_ref, held):
+    rows, width = scaled.shape[0] // 2, scaled.shape[1]
+    for n in range(2):
+        for c in range(width // LANES):
+            o_ref[n, c * rows : (c + 1) * rows, :] = scaled[n * rows : (n + 1) * rows, c * LANES : (c + 1) * LANES]
+        meta = jnp.transpose(jnp.broadcast_to(power[n * rows : (n + 1) * rows], (rows, LANES)))
+        o_ref[n, width // LANES * rows :, :] = meta[:META]
+
+
+def token_grad(place_ref, pred_ref, t0_ref, t1_ref, t2_ref, t3_ref, o_ref, held):
     blocks, rows, _ = pred_ref.shape
 
     @pl.when(pl.program_id(0) == 0)
     def _():
-        r = lax.broadcasted_iota(jnp.int32, (rows, rows), 0)
-        q = lax.broadcasted_iota(jnp.int32, (rows, rows), 1)
-        order = jnp.where(q == (r % 16) * 8 + r // 16, 1.0, 0.0).astype(bf16)
-        target = jnp.dot(order, tgt_ref[...], preferred_element_type=f32)
-        token_scale = target[:, blocks * LANES : blocks * LANES + 1] + scale_epsilon
+        arrived = jnp.concatenate([t0_ref[...], t1_ref[...], t2_ref[...], t3_ref[...]], axis=0)
+        count, half = arrived.shape[0], blocks // 2 * LANES
+        r = lax.broadcasted_iota(jnp.int32, (rows, count), 0)
+        q = lax.broadcasted_iota(jnp.int32, (rows, count), 1)
+        second = ((place_ref[0] - q // 64) & 3) * 4 + ((place_ref[1] - q // 16 % 4) & 3)
+        match = r == (q % 8) * 16 + second
+        first = jnp.where(match & (q // 8 % 2 == 0), 1.0, 0.0).astype(bf16)
+        other = jnp.where(match & (q // 8 % 2 == 1), 1.0, 0.0).astype(bf16)
+        left = jnp.dot(first, arrived, preferred_element_type=f32)
+        right = jnp.dot(other, arrived[:, :half], preferred_element_type=f32)
+        target = jnp.concatenate([left[:, :half], right], axis=1)
+        token_scale = left[:, half : half + 1] + scale_epsilon
         total = jnp.zeros((rows, LANES), f32)
         for c in range(blocks):
             quantized = (target[:, c * LANES : (c + 1) * LANES] / token_scale).astype(bf16)
@@ -81,25 +101,35 @@
     o_ref[0] = held[...]
 
 
-def input_grad(g_ref, w_ref, o_ref, loss_ref):
+def input_grad(g_ref, w_ref, loss_ref, o_ref, total_ref):
     rows = 128
-
-    @pl.when(pl.program_id(0) == 0)
-    def _():
-        loss_ref[...] = jnp.zeros_like(loss_ref)
-
-    pieces = g_ref[0, 8 * rows :, :].astype(f32)
-    loss_ref[...] += jnp.sum(pieces, axis=0, keepdims=True)
-    grad = jnp.concatenate([g_ref[0, c * rows : (c + 1) * rows, :] for c in range(8)], axis=1)
+    pieces = jnp.sum(loss_ref[...].astype(f32), axis=0)
+    loss = jnp.sum(pieces, axis=0, keepdims=True)
+    total_ref[...] = loss
+    row = lax.broadcasted_iota(jnp.int32, (META, LANES), 0)
+    loss_power = exponent_of(loss)
+    scaled_loss = loss * jnp.exp2(10.0 - loss_power)
+    high = jnp.floor(scaled_loss)
+    rest = (scaled_loss - high) * 2048.0
+    middle = jnp.floor(rest)
+    low = jnp.floor((rest - middle) * 2048.0)
+    meta = jnp.where(row == 1, loss_power, jnp.where(row == 2, high, jnp.where(row == 3, middle, low)))
+    grad = jnp.concatenate(
+        [
+            jnp.concatenate([g_ref[n, c * rows : (c + 1) * rows, :] for c in range(8)], axis=1)
+            for n in range(2)
+        ],
+        axis=0,
+    )
     partial = lax.dot_general(grad, w_ref[...], (((1,), (1,)), ((), ())), preferred_element_type=f32)
-    for n in range(2):
+    for n in range(4):
         chunk = partial[64 * n : 64 * n + 64]
         largest = jnp.max(jnp.max(jnp.abs(chunk), axis=0, keepdims=True), axis=1, keepdims=True)
         power = exponent_of(largest)
         scaled = chunk * jnp.exp2(TOP - power)
         for c in range(4):
             o_ref[n, 64 * c : 64 * c + 64, :] = scaled[:, c * LANES : (c + 1) * LANES]
-        o_ref[n, 256:, :] = jnp.broadcast_to(power, (META, LANES))
+        o_ref[n, 256:, :] = jnp.where(row == 0, power, meta)
 
 
 def weight_grad(core_ref, s_ref, g_ref, after_ref, send_ref, keep_ref):
@@ -124,15 +154,39 @@
     own = tokens // tensor_count
     blocks = columns // LANES
 
+    dp_index = lax.axis_index("dp").astype(jnp.int32)
+    place = jnp.stack([dp_index // 4, dp_index % 4])
+    scalars = pl.BlockSpec(memory_space=pltpu.SMEM)
+    whole = pl.BlockSpec(memory_space=pltpu.VMEM)
+
     with jax.named_scope("teacher"):
         spread = all_to_all(teacher_hidden.reshape(8, 8, -1), "tensor")
+        group = (jax.ShapeDtypeStruct((64, columns // 2 + LANES), bf16),) * 4
         packed = call(
             pack_teacher,
-            jax.ShapeDtypeStruct((128, columns + LANES), bf16),
+            group,
             0,
             600_000,
-        )(spread.reshape(64, -1))
-        target = all_to_all(packed.reshape(16, 8, -1), "dp").reshape(own, -1)
+            in_specs=[scalars, whole],
+            out_specs=(whole,) * 4,
+            scratch_shapes=[pltpu.VMEM((4, 64, columns // 2 + LANES), bf16)],
+        )(place, spread.reshape(64, -1))
+        near = [packed[0]]
+        for k in range(1, 4):
+            moves = [(z, z // 4 * 4 + (z + k) % 4) for z in range(dp_count)]
+            near.append(lax.ppermute(packed[k], "dp", moves))
+        packed = call(
+            regroup_teacher,
+            group,
+            0,
+            600_000,
+            in_specs=[scalars] + [whole] * 4,
+            out_specs=(whole,) * 4,
+        )(place, *near)
+        target = [packed[0]]
+        for m in range(1, 4):
+            moves = [(z, (z + 4 * m) % dp_count) for z in range(dp_count)]
+            target.append(lax.ppermute(packed[m], "dp", moves))
 
     with jax.named_scope("prediction"):
         size = blocks * own + META
@@ -141,12 +195,12 @@
             jax.ShapeDtypeStruct((tensor_count, size, LANES), f32),
             2 * tokens * width_local * columns,
             6_000_000,
-            grid=(tensor_count,),
+            grid=(tensor_count // 2,),
             in_specs=[
-                pl.BlockSpec((own, width_local), lambda i: (i, 0)),
+                pl.BlockSpec((2 * own, width_local), lambda i: (i, 0)),
                 pl.BlockSpec((width_local, columns), lambda i: (0, 0)),
             ],
-            out_specs=pl.BlockSpec((1, size, LANES), lambda i: (i, 0, 0)),
+            out_specs=pl.BlockSpec((2, size, LANES), lambda i: (i, 0, 0)),
         )(student, proj_weight)
         parts = all_to_all(partial.astype(f16), "tensor").astype(f32)
         unscale = jnp.exp2(parts[:, blocks * own, :] - TOP)
@@ -160,32 +214,31 @@
             2 * own * own * columns,
             3_000_000,
             grid=(tensor_count,),
-            in_specs=[
-                pl.BlockSpec((blocks, own, LANES), lambda i: (0, 0, 0)),
-                pl.BlockSpec((own, columns + LANES), lambda i: (0, 0)),
-            ],
+            in_specs=[scalars, pl.BlockSpec((blocks, own, LANES), lambda i: (0, 0, 0))]
+            + [pl.BlockSpec(group[0].shape, lambda i: (0, 0))] * 4,
             out_specs=pl.BlockSpec((1, size, LANES), lambda i: (i, 0, 0)),
             scratch_shapes=[pltpu.VMEM((size, LANES), bf16)],
-        )(prediction, target)
+        )(place, prediction, *target)
         grad = all_to_all(grad_own, "tensor")
 
     with jax.named_scope("input_grad"):
         chunk = 64 * 4 + META
-        term, loss = call(
+        term, total = call(
             input_grad,
             (jax.ShapeDtypeStruct((dp_count, chunk, LANES), f32), jax.ShapeDtypeStruct((1, LANES), f32)),
             2 * tokens * width_local * columns,
             5_000_000,
-            grid=(tensor_count,),
+            grid=(tensor_count // 2,),
             in_specs=[
-                pl.BlockSpec((1, size, LANES), lambda i: (i, 0, 0)),
+                pl.BlockSpec((2, size, LANES), lambda i: (i, 0, 0)),
                 pl.BlockSpec((width_local, columns), lambda i: (0, 0)),
+                pl.BlockSpec((tensor_count, META, LANES), lambda i: (0, blocks * own // META, 0)),
             ],
             out_specs=(
-                pl.BlockSpec((2, chunk, LANES), lambda i: (i, 0, 0)),
+                pl.BlockSpec((4, chunk, LANES), lambda i: (i, 0, 0)),
                 pl.BlockSpec((1, LANES), lambda i: (0, 0)),
             ),
-        )(grad, proj_weight)
+        )(grad, proj_weight, grad)
         terms = all_to_all(term.astype(f16), "dp").astype(f32)
         unscale = jnp.exp2(terms[:, 256:257, 0:1] - TOP)
         summed = jnp.sum(terms[:, :256, :] * unscale, axis=0)
@@ -205,7 +258,7 @@
             5_000_000,
             grid=(4,),
             in_specs=[
-                pl.BlockSpec(memory_space=pltpu.SMEM),
+                scalars,
                 pl.BlockSpec((tokens, width_local), lambda i: (0, 0)),
                 pl.BlockSpec((tensor_count, 2 * own, LANES), lambda i: (0, i, 0)),
                 pl.BlockSpec((1, LANES), lambda i: (0, 0)),
@@ -214,7 +267,7 @@
                 pl.BlockSpec((width_local // 2, 2 * LANES), lambda i: (0, i)),
                 pl.BlockSpec((width_local // 2, 2 * LANES), lambda i: (0, i)),
             ),
-        )(core.reshape(1).astype(jnp.int32), student, grad, loss)
+        )(core.reshape(1).astype(jnp.int32), student, grad, total)
         pair = (keep + lax.ppermute(send, "seq", other_core)).astype(bf16)
         mine = pair.astype(f32) + lax.ppermute(pair, "seq", other_y).astype(f32)
         theirs = lax.ppermute(mine, "seq", other_core)
@@ -225,10 +278,9 @@
         )
 
     with jax.named_scope("loss"):
-        for axis, step in (("dp", 1), ("dp", 2), ("dp", 4), ("dp", 8), ("seq", 1), ("seq", 2)):
-            moves = [(i, i ^ step) for i in range(lax.axis_size(axis))]
-            loss = loss + lax.ppermute(loss, axis, moves)
-        loss_value = loss[0, 0] / (tokens * seq_count * columns * dp_count)
+        pieces = terms[:, 257:261, 0]
+        losses = (pieces[:, 1] + (pieces[:, 2] + pieces[:, 3] / 2048.0) / 2048.0) * jnp.exp2(pieces[:, 0] - 10.0)
+        loss_value = lax.psum(jnp.sum(losses), "seq") / (tokens * seq_count * columns * dp_count)
     return (loss_value, grad_weight, grad_input)
 
 

time: 218 us -> 179 us (0.82)
  waiting for transfers between devices: 71.9 us -> 42.3 us
  starting transfers between devices: 95.1 us -> 65.6 us
  blocking collectives: 24.2 us -> 45.2 us
  Pallas kernels: 12.7 us -> 10 us
    all_to_all x4 -> x3, waiting for transfers between devices: 38.3 us -> 14.9 us  [all_to_all(): return lax.all_to_all(x, axis, 0, 0)]
    all_to_all x4 -> x3, starting transfers between devices: 42.7 us -> 20.3 us  [all_to_all(): return lax.all_to_all(x, axis, 0, 0)]
    psum x0 -> x1, blocking collectives: none -> 12.7 us  [body(): lax.psum(jnp.sum(losses), 'seq') / (tokens * seq_count * columns * dp_count)]
    ppermute x6, waiting for transfers between devices: 19.2 us -> 10.7 us  [the longest x3 7.54 us: body(): target.append(lax.ppermute(packed[m], 'dp', moves))]
    all_to_all x1, blocking collectives: 24.2 us -> 32.5 us  [all_to_all(): return lax.all_to_all(x, axis, 0, 0)]
    ppermute x6, starting transfers between devices: 40.4 us -> 33.5 us  [the longest x3 22.5 us: body(): target.append(lax.ppermute(packed[m], 'dp', moves))]
    pallas_call x1, Pallas kernels: 4.81 us -> 2.38 us  [body(): call(input_grad, (jax.ShapeDtypeStruct((dp_count, chunk, LANES), f32), ja...]
    ppermute x1, waiting for transfers between devices: 0.01 us -> 2.26 us  [body(): theirs = lax.ppermute(mine, 'seq', other_core)]
  transfers between devices with their start and end apart: 13 -> 12, of which waited for: 10 -> 8; matrix products, arithmetic and copies ran while one was open for 2% -> 3% of each run, Pallas kernels for 3% -> 4%
where the time goes in v2:
time: 179 us; the launch traced here: 178 us
  starting transfers between devices  65.6 us (37%)
  blocking collectives  45.2 us (25%)
  waiting for transfers between devices  42.3 us (24%)
  Pallas kernels  10 us (6%)
  other arithmetic  8.79 us (5%)
  local copies, waits for them, and re-layouts  3.29 us (2%)
  between operations  2.67 us (1%)
    all_to_all x1, blocking collectives, all_to_all(): return lax.all_to_all(x, axis, 0, 0)  32.5 us
    ppermute x3, starting transfers between devices, body(): target.append(lax.ppermute(packed[m], 'dp', moves))  22.5 us
    all_to_all x3, starting transfers between devices, all_to_all(): return lax.all_to_all(x, axis, 0, 0)  20.3 us
    all_to_all x3, waiting for transfers between devices, all_to_all(): return lax.all_to_all(x, axis, 0, 0)  14.9 us
    psum x1, blocking collectives, body(): lax.psum(jnp.sum(losses), 'seq') / (tokens * seq_count * columns * dp_count)  12.7 us
    ppermute x1, waiting for transfers between devices, body(): mine = pair.astype(f32) + lax.ppermute(pair, 'seq', other_y).astype(f32)  12.1 us
    ppermute x3, starting transfers between devices, body(): near.append(lax.ppermute(packed[k], 'dp', moves))  11.1 us
    ppermute x3, waiting for transfers between devices, body(): target.append(lax.ppermute(packed[m], 'dp', moves))  7.54 us
  transfers between devices with their start and end apart: 12, of which 8 were waited for; matrix products, arithmetic and copies ran while one was open for 3% of the time, Pallas kernels for 4%

profile of v2, /device:TPU:1, one launch (start us, length us, event | category | flops | bytes accessed | tf_op | source)
XLA Modules:
  0.0 177.8 jit_solution(1914599455995547929)
XLA Ops:
  0.6 5.9 %all-to-all-start.1 = ((bf16[8,8,2048]{2,1,0:T(8,128)(2,1)}), bf16[8,8,2048]{2,1,0:T(8,128)(2,1)S(1)}, u32[]{:S(2)}, u32[]{:S(2)}) async-start(bf16[8,8,2048]{2,1,0:T(8,128)(2,1)} %bitcast.19), calls=%async_computation.1 | async-start | bytes 524288 | tf_op jit(solution)/shard_map/teacher/all_to_all | solution.py:27
  6.5 1.2 copy-done
  7.7 1.2 copy-done.2
  9.0 2.3 %prediction.1 = f32[8,1040,128]{2,1,0:T(8,128)S(1)} custom-call(bf16[1024,512]{1,0:T(8,128)(2,1)S(1)} %bitcast.15, bf16[512,1024]{1,0:T(8,128)(2,1)S(1)} %copy-done), custom_call_target="tpu_custom_call" | custom-call | flops 1073741824 | bytes 6000000 | tf_op jit(solution)/shard_map/prediction/pallas_call | solution.py:193
  11.3 1.6 convert_element_type.30
  12.9 0.0 all-to-all-done.1
  12.9 5.1 %all-to-all-start = ((f16[8,1040,128]{2,1,0:T(8,128)(2,1)}), f16[8,1040,128]{2,1,0:T(8,128)(2,1)S(1)}, u32[]{:S(2)}, u32[]{:S(2)}) async-start(f16[8,1040,128]{2,1,0:T(8,128)(2,1)} %convert_element_type.30), calls=%async_computation | async-start | bytes 4259840 | tf_op jit(solution)/shard_map/prediction/all_to_all | solution.py:27
  18.0 0.1 pad_add_fusion.place_ref
  18.1 0.7 teacher.2
  18.9 3.5 %collective-permute-start = (bf16[64,640]{1,0:T(8,128)(2,1)S(1)}, bf16[64,640]{1,0:T(8,128)(2,1)S(1)}, u32[]{:S(2)}, u32[]{:S(2)}) collective-permute-start(bf16[64,640]{1,0:T(8,128)(2,1)S(1)} %get-tuple-element.16), channel_id=1, source_target_pairs={{0,32},{32,64},{64,96},{96,0},{128,160},{160,192},{192,224},{224,1... | collective-permute-start | bytes 245768 | tf_op jit(solution)/shard_map/teacher/ppermute | solution.py:177
  22.4 4.9 %collective-permute-start.1 = (bf16[64,640]{1,0:T(8,128)(2,1)S(1)}, bf16[64,640]{1,0:T(8,128)(2,1)S(1)}, u32[]{:S(2)}, u32[]{:S(2)}) collective-permute-start(bf16[64,640]{1,0:T(8,128)(2,1)S(1)} %get-tuple-element.17), channel_id=1, source_target_pairs={{0,64},{32,96},{64,0},{96,32},{128,192},{160,224},{192,128},{224,1... | collective-permute-start | bytes 245768 | tf_op jit(solution)/shard_map/teacher/ppermute | solution.py:177
  27.3 2.6 %collective-permute-start.2 = (bf16[64,640]{1,0:T(8,128)(2,1)S(1)}, bf16[64,640]{1,0:T(8,128)(2,1)S(1)}, u32[]{:S(2)}, u32[]{:S(2)}) collective-permute-start(bf16[64,640]{1,0:T(8,128)(2,1)S(1)} %get-tuple-element.18), channel_id=1, source_target_pairs={{0,96},{32,0},{64,32},{96,64},{128,224},{160,128},{192,160},{224,1... | collective-permute-start | bytes 245768 | tf_op jit(solution)/shard_map/teacher/ppermute | solution.py:177
  30.0 0.3 collective-permute-done.1.refs_2_
  30.3 2.9 %collective-permute-done.2.refs_3_ = bf16[64,640]{1,0:T(8,128)(2,1)S(1)} collective-permute-done((bf16[64,640]{1,0:T(8,128)(2,1)S(1)}, bf16[64,640]{1,0:T(8,128)(2,1)S(1)}, u32[]{:S(2)}, u32[]{:S(2)}) %collective-permute-start.2) | collective-permute-done | bytes 81952 | tf_op jit(solution)/shard_map/teacher/ppermute | solution.py:177
  33.2 0.6 teacher.3
  33.8 8.4 %collective-permute-start.3 = (bf16[64,640]{1,0:T(8,128)(2,1)S(1)}, bf16[64,640]{1,0:T(8,128)(2,1)S(1)}, u32[]{:S(2)}, u32[]{:S(2)}) collective-permute-start(bf16[64,640]{1,0:T(8,128)(2,1)S(1)} %get-tuple-element.20), channel_id=1, source_target_pairs={{0,128},{32,160},{64,192},{96,224},{128,256},{160,288},{192,320},{... | collective-permute-start | bytes 245768 | tf_op jit(solution)/shard_map/teacher/ppermute | solution.py:189
  42.2 8.8 %collective-permute-start.4 = (bf16[64,640]{1,0:T(8,128)(2,1)S(1)}, bf16[64,640]{1,0:T(8,128)(2,1)S(1)}, u32[]{:S(2)}, u32[]{:S(2)}) collective-permute-start(bf16[64,640]{1,0:T(8,128)(2,1)S(1)} %get-tuple-element.21), channel_id=1, source_target_pairs={{0,256},{32,288},{64,320},{96,352},{128,384},{160,416},{192,448},{... | collective-permute-start | bytes 245768 | tf_op jit(solution)/shard_map/teacher/ppermute | solution.py:189
  51.0 5.2 %collective-permute-start.5 = (bf16[64,640]{1,0:T(8,128)(2,1)S(1)}, bf16[64,640]{1,0:T(8,128)(2,1)S(1)}, u32[]{:S(2)}, u32[]{:S(2)}) collective-permute-start(bf16[64,640]{1,0:T(8,128)(2,1)S(1)} %get-tuple-element.22), channel_id=1, source_target_pairs={{0,384},{32,416},{64,448},{96,480},{128,0},{160,32},{192,64},{224,... | collective-permute-start | bytes 245768 | tf_op jit(solution)/shard_map/teacher/ppermute | solution.py:189
  56.3 0.3 convert_element_type.31
  56.6 1.4 fusion
  58.0 1.8 collective-permute-done.4.t2_ref
  59.7 5.8 %collective-permute-done.5.t3_ref = bf16[64,640]{1,0:T(8,128)(2,1)S(1)} collective-permute-done((bf16[64,640]{1,0:T(8,128)(2,1)S(1)}, bf16[64,640]{1,0:T(8,128)(2,1)S(1)}, u32[]{:S(2)}, u32[]{:S(2)}) %collective-permute-start.5) | collective-permute-done | bytes 81952 | tf_op jit(solution)/shard_map/teacher/ppermute | solution.py:189
  65.5 1.4 gradient.1
  66.9 0.0 copy-start.1
  66.9 32.5 %all_to_all.20.g_ref.loss_ref = bf16[8,1040,128]{2,1,0:T(8,128)(2,1)S(1)} all-to-all(bf16[8,1040,128]{2,1,0:T(8,128)(2,1)S(1)} %gradient.1), channel_id=1, replica_groups=mesh['dp'=16,'seq'=4,'tensor'=8] {'tensor'}, dimensions={0} | all-to-all | bytes 4259840 | tf_op jit(solution)/shard_map/gradient/all_to_all | solution.py:27
  99.5 2.4 %input_grad.1 = (f32[16,272,128]{2,1,0:T(8,128)S(1)}, f32[1,128]{1,0:T(1,128)S(1)}) custom-call(bf16[8,1040,128]{2,1,0:T(8,128)(2,1)S(1)} %all_to_all.20.g_ref.loss_ref, bf16[512,1024]{1,0:T(8,128)(2,1)S(1)} %copy-done.1, bf16[8,1040,128]{2,1,0:T(8,128)(2,1)S(1)} %all_to_all.20.g_ref.loss_ref), custom_call_target="tpu_custom_call" | custom-call | flops 1073741824 | bytes 5000000 | tf_op jit(solution)/shard_map/input_grad/pallas_call | solution.py:226
  101.8 0.0 copy-start.3
  101.9 1.2 convert_element_type.32
  103.0 9.3 %all-to-all-start.3 = ((f16[16,272,128]{2,1,0:T(8,128)(2,1)}), f16[16,272,128]{2,1,0:T(8,128)(2,1)}, u32[]{:S(2)}, u32[]{:S(2)}) async-start(f16[16,272,128]{2,1,0:T(8,128)(2,1)} %convert_element_type.32), calls=%async_computation.3 | async-start | bytes 2228224 | tf_op jit(solution)/shard_map/input_grad/all_to_all | solution.py:27
  112.3 2.6 %weight_grad.1 = (f32[256,1024]{1,0:T(8,128)S(1)}, f32[256,1024]{1,0:T(8,128)S(1)}) custom-call(s32[1]{0:T(128)} %bitcast.9.core_ref, bf16[1024,512]{1,0:T(8,128)(2,1)S(1)} %bitcast.16, bf16[8,1040,128]{2,1,0:T(8,128)(2,1)S(1)} %all_to_all.20.g_ref.loss_ref, f32[1,128]{1,0:T(1,128)S(1)} %get-tuple-element.24.after_ref), custom_call_target="tpu_custom_call" | custom-call | flops 1073741824 | bytes 5000000 | tf_op jit(solution)/shard_map/weight_grad/pallas_call | solution.py:254
  115.0 4.2 %collective-permute-start.6 = (f32[256,1024]{1,0:T(8,128)S(1)}, f32[256,1024]{1,0:T(8,128)S(1)}, u32[]{:S(2)}, u32[]{:S(2)}) collective-permute-start(f32[256,1024]{1,0:T(8,128)S(1)} %get-tuple-element.26), channel_id=1, source_target_pairs={{0,8},{8,0},{16,24},{24,16},{1,9},{9,1},{17,25},{25,17},{2,10},{10... | collective-permute-start | bytes 3145736 | tf_op jit(solution)/shard_map/weight_grad/ppermute | solution.py:271
  119.1 2.3 %collective-permute-done.6 = f32[256,1024]{1,0:T(8,128)S(1)} collective-permute-done((f32[256,1024]{1,0:T(8,128)S(1)}, f32[256,1024]{1,0:T(8,128)S(1)}, u32[]{:S(2)}, u32[]{:S(2)}) %collective-permute-start.6) | collective-permute-done | bytes 1048608 | tf_op jit(solution)/shard_map/weight_grad/ppermute | solution.py:271
  121.4 0.2 add_convert_fusion
  121.6 4.5 %collective-permute-start.7 = (bf16[256,1024]{1,0:T(8,128)(2,1)S(1)}, bf16[256,1024]{1,0:T(8,128)(2,1)S(1)}, u32[]{:S(2)}, u32[]{:S(2)}) collective-permute-start(bf16[256,1024]{1,0:T(8,128)(2,1)S(1)} %add_convert_fusion), channel_id=1, source_target_pairs={{0,16},{8,24},{16,0},{24,8},{1,17},{9,25},{17,1},{25,9},{2,18},{10... | collective-permute-start | bytes 1572872 | tf_op jit(solution)/shard_map/weight_grad/ppermute | solution.py:272
  126.1 12.1 %collective-permute-done.7 = bf16[256,1024]{1,0:T(8,128)(2,1)S(1)} collective-permute-done((bf16[256,1024]{1,0:T(8,128)(2,1)S(1)}, bf16[256,1024]{1,0:T(8,128)(2,1)S(1)}, u32[]{:S(2)}, u32[]{:S(2)}) %collective-permute-start.7) | collective-permute-done | bytes 524320 | tf_op jit(solution)/shard_map/weight_grad/ppermute | solution.py:272
  138.2 0.2 convert_add_fusion
  138.4 3.0 %collective-permute-start.8 = (f32[256,1024]{1,0:T(8,128)S(1)}, f32[256,1024]{1,0:T(8,128)S(1)}, u32[]{:S(2)}, u32[]{:S(2)}) collective-permute-start(f32[256,1024]{1,0:T(8,128)S(1)} %convert_add_fusion), channel_id=1, source_target_pairs={{0,8},{8,0},{16,24},{24,16},{1,9},{9,1},{17,25},{25,17},{2,10},{10... | collective-permute-start | bytes 3145736 | tf_op jit(solution)/shard_map/weight_grad/ppermute | solution.py:273
  141.4 2.3 %collective-permute-done.8 = f32[256,1024]{1,0:T(8,128)S(1)} collective-permute-done((f32[256,1024]{1,0:T(8,128)S(1)}, f32[256,1024]{1,0:T(8,128)S(1)}, u32[]{:S(2)}, u32[]{:S(2)}) %collective-permute-start.8) | collective-permute-done | bytes 1048608 | tf_op jit(solution)/shard_map/weight_grad/ppermute | solution.py:273
  143.7 1.5 maximum_select_fusion
  145.2 14.9 %all-to-all-done.3 = f16[16,272,128]{2,1,0:T(8,128)(2,1)} async-done(((f16[16,272,128]{2,1,0:T(8,128)(2,1)}), f16[16,272,128]{2,1,0:T(8,128)(2,1)}, u32[]{:S(2)}, u32[]{:S(2)}) %all-to-all-start.3) | async-done | bytes 1114144 | tf_op jit(solution)/shard_map/input_grad/all_to_all | solution.py:27
  160.1 1.4 convert_element_type.33
  161.5 0.1 copy.8
  161.6 0.6 multiply_reduce_fusion
  162.2 0.2 fusion.4
  162.4 12.7 %psum.7 = f32[]{:T(128)} all-reduce(f32[]{:T(128)} %multiply_reduce_fusion), channel_id=1, replica_groups=mesh['dp'=16,'seq'=4,'tensor'=8] {'seq'}, use_global_device_ids=true, to_apply=%region_2.3 | all-reduce | flops 1 | bytes 8 | tf_op jit(solution)/shard_map/loss/psum | solution.py:283
  175.1 0.2 fusion.1
  175.3 0.1 copy.9
  175.4 0.7 reshape.53
  (10 shorter events, 0.0 us)
Async XLA Ops:
  0.6 12.3 %all-to-all-start.1 = ((bf16[8,8,2048]{2,1,0:T(8,128)(2,1)}), bf16[8,8,2048]{2,1,0:T(8,128)(2,1)S(1)}, u32[]{:S(2)}, u32[]{:S(2)}) async-start(bf16[8,8,2048]{2,1,0:T(8,128)(2,1)} %bitcast.19), calls=%async_computation.1 | async-start | bytes 524288 | tf_op jit(solution)/shard_map/teacher/all_to_all | solution.py:27
  6.5 1.2 copy-start
  7.7 1.2 copy-start.2
  12.9 43.4 %all-to-all-start = ((f16[8,1040,128]{2,1,0:T(8,128)(2,1)}), f16[8,1040,128]{2,1,0:T(8,128)(2,1)S(1)}, u32[]{:S(2)}, u32[]{:S(2)}) async-start(f16[8,1040,128]{2,1,0:T(8,128)(2,1)} %convert_element_type.30), calls=%async_computation | async-start | bytes 4259840 | tf_op jit(solution)/shard_map/prediction/all_to_all | solution.py:27
  18.9 11.1 %collective-permute-start = (bf16[64,640]{1,0:T(8,128)(2,1)S(1)}, bf16[64,640]{1,0:T(8,128)(2,1)S(1)}, u32[]{:S(2)}, u32[]{:S(2)}) collective-permute-start(bf16[64,640]{1,0:T(8,128)(2,1)S(1)} %get-tuple-element.16), channel_id=1, source_target_pairs={{0,32},{32,64},{64,96},{96,0},{128,160},{160,192},{192,224},{224,1... | collective-permute-start | bytes 245768 | tf_op jit(solution)/shard_map/teacher/ppermute | solution.py:177
  22.4 7.9 %collective-permute-start.1 = (bf16[64,640]{1,0:T(8,128)(2,1)S(1)}, bf16[64,640]{1,0:T(8,128)(2,1)S(1)}, u32[]{:S(2)}, u32[]{:S(2)}) collective-permute-start(bf16[64,640]{1,0:T(8,128)(2,1)S(1)} %get-tuple-element.17), channel_id=1, source_target_pairs={{0,64},{32,96},{64,0},{96,32},{128,192},{160,224},{192,128},{224,1... | collective-permute-start | bytes 245768 | tf_op jit(solution)/shard_map/teacher/ppermute | solution.py:177
  27.3 5.9 %collective-permute-start.2 = (bf16[64,640]{1,0:T(8,128)(2,1)S(1)}, bf16[64,640]{1,0:T(8,128)(2,1)S(1)}, u32[]{:S(2)}, u32[]{:S(2)}) collective-permute-start(bf16[64,640]{1,0:T(8,128)(2,1)S(1)} %get-tuple-element.18), channel_id=1, source_target_pairs={{0,96},{32,0},{64,32},{96,64},{128,224},{160,128},{192,160},{224,1... | collective-permute-start | bytes 245768 | tf_op jit(solution)/shard_map/teacher/ppermute | solution.py:177
  33.8 24.2 %collective-permute-start.3 = (bf16[64,640]{1,0:T(8,128)(2,1)S(1)}, bf16[64,640]{1,0:T(8,128)(2,1)S(1)}, u32[]{:S(2)}, u32[]{:S(2)}) collective-permute-start(bf16[64,640]{1,0:T(8,128)(2,1)S(1)} %get-tuple-element.20), channel_id=1, source_target_pairs={{0,128},{32,160},{64,192},{96,224},{128,256},{160,288},{192,320},{... | collective-permute-start | bytes 245768 | tf_op jit(solution)/shard_map/teacher/ppermute | solution.py:189
  42.2 17.5 %collective-permute-start.4 = (bf16[64,640]{1,0:T(8,128)(2,1)S(1)}, bf16[64,640]{1,0:T(8,128)(2,1)S(1)}, u32[]{:S(2)}, u32[]{:S(2)}) collective-permute-start(bf16[64,640]{1,0:T(8,128)(2,1)S(1)} %get-tuple-element.21), channel_id=1, source_target_pairs={{0,256},{32,288},{64,320},{96,352},{128,384},{160,416},{192,448},{... | collective-permute-start | bytes 245768 | tf_op jit(solution)/shard_map/teacher/ppermute | solution.py:189
  51.0 14.5 %collective-permute-start.5 = (bf16[64,640]{1,0:T(8,128)(2,1)S(1)}, bf16[64,640]{1,0:T(8,128)(2,1)S(1)}, u32[]{:S(2)}, u32[]{:S(2)}) collective-permute-start(bf16[64,640]{1,0:T(8,128)(2,1)S(1)} %get-tuple-element.22), channel_id=1, source_target_pairs={{0,384},{32,416},{64,448},{96,480},{128,0},{160,32},{192,64},{224,... | collective-permute-start | bytes 245768 | tf_op jit(solution)/shard_map/teacher/ppermute | solution.py:189
  66.9 32.5 %copy-start.1 = (bf16[512,1024]{1,0:T(8,128)(2,1)S(1)}, bf16[512,1024]{1,0:T(8,128)(2,1)}, u32[]{:S(2)}) copy-start(bf16[512,1024]{1,0:T(8,128)(2,1)} %w_ref.3) | copy-start | bytes 3145732
  101.8 10.5 %copy-start.3 = (bf16[1,64,16,512]{3,2,1,0:T(8,128)(2,1)S(1)}, bf16[1,64,16,512]{3,2,1,0:T(8,128)(2,1)}, u32[]{:S(2)}) copy-start(bf16[1,64,16,512]{3,2,1,0:T(8,128)(2,1)} %param.3) | copy-start | bytes 3145732
  103.0 57.1 %all-to-all-start.3 = ((f16[16,272,128]{2,1,0:T(8,128)(2,1)}), f16[16,272,128]{2,1,0:T(8,128)(2,1)}, u32[]{:S(2)}, u32[]{:S(2)}) async-start(f16[16,272,128]{2,1,0:T(8,128)(2,1)} %convert_element_type.32), calls=%async_computation.3 | async-start | bytes 2228224 | tf_op jit(solution)/shard_map/input_grad/all_to_all | solution.py:27
  115.0 6.4 %collective-permute-start.6 = (f32[256,1024]{1,0:T(8,128)S(1)}, f32[256,1024]{1,0:T(8,128)S(1)}, u32[]{:S(2)}, u32[]{:S(2)}) collective-permute-start(f32[256,1024]{1,0:T(8,128)S(1)} %get-tuple-element.26), channel_id=1, source_target_pairs={{0,8},{8,0},{16,24},{24,16},{1,9},{9,1},{17,25},{25,17},{2,10},{10... | collective-permute-start | bytes 3145736 | tf_op jit(solution)/shard_map/weight_grad/ppermute | solution.py:271
  121.6 16.6 %collective-permute-start.7 = (bf16[256,1024]{1,0:T(8,128)(2,1)S(1)}, bf16[256,1024]{1,0:T(8,128)(2,1)S(1)}, u32[]{:S(2)}, u32[]{:S(2)}) collective-permute-start(bf16[256,1024]{1,0:T(8,128)(2,1)S(1)} %add_convert_fusion), channel_id=1, source_target_pairs={{0,16},{8,24},{16,0},{24,8},{1,17},{9,25},{17,1},{25,9},{2,18},{10... | collective-permute-start | bytes 1572872 | tf_op jit(solution)/shard_map/weight_grad/ppermute | solution.py:272
  138.4 5.3 %collective-permute-start.8 = (f32[256,1024]{1,0:T(8,128)S(1)}, f32[256,1024]{1,0:T(8,128)S(1)}, u32[]{:S(2)}, u32[]{:S(2)}) collective-permute-start(f32[256,1024]{1,0:T(8,128)S(1)} %convert_add_fusion), channel_id=1, source_target_pairs={{0,8},{8,0},{16,24},{24,16},{1,9},{9,1},{17,25},{25,17},{2,10},{10... | collective-permute-start | bytes 3145736 | tf_op jit(solution)/shard_map/weight_grad/ppermute | solution.py:273

commit v3 on v2

--- a/solution.py
+++ b/solution.py
@@ -8,7 +8,8 @@
 scale_epsilon = 1e-06
 grad_factor = 0.25
 LANES = 128
-META = 16
+META = 8
+PIECES = 16
 TOP = 14.0
 bf16, f16, f32 = jnp.bfloat16, jnp.float16, jnp.float32
 
@@ -25,6 +26,12 @@
 
 def all_to_all(x, axis):
     return lax.all_to_all(x, axis, 0, 0)
+
+
+def butterfly(x, steps):
+    for axis, step in steps:
+        x = x + lax.ppermute(x, axis, [(i, i ^ step) for i in range(lax.axis_size(axis))])
+    return x
 
 
 def exponent_of(largest):
@@ -67,7 +74,7 @@
         o_ref[n, width // LANES * rows :, :] = meta[:META]
 
 
-def token_grad(place_ref, pred_ref, t0_ref, t1_ref, t2_ref, t3_ref, o_ref, held):
+def token_grad(place_ref, pred_ref, t0_ref, t1_ref, t2_ref, t3_ref, a_ref, b_ref, held):
     blocks, rows, _ = pred_ref.shape
 
     @pl.when(pl.program_id(0) == 0)
@@ -76,7 +83,9 @@
         count, half = arrived.shape[0], blocks // 2 * LANES
         r = lax.broadcasted_iota(jnp.int32, (rows, count), 0)
         q = lax.broadcasted_iota(jnp.int32, (rows, count), 1)
-        second = ((place_ref[0] - q // 64) & 3) * 4 + ((place_ref[1] - q // 16 % 4) & 3)
+        shift = q // 16 % 4
+        shift = jnp.where(shift == 3, -1, shift)
+        second = (place_ref[0] * 4 + place_ref[1] - 4 * (q // 64) - shift) & 15
         match = r == (q % 8) * 16 + second
         first = jnp.where(match & (q // 8 % 2 == 0), 1.0, 0.0).astype(bf16)
         other = jnp.where(match & (q // 8 % 2 == 1), 1.0, 0.0).astype(bf16)
@@ -94,56 +103,102 @@
         high = loss.astype(bf16).astype(f32)
         middle = (loss - high).astype(bf16).astype(f32)
         low = loss - high - middle
-        row = lax.broadcasted_iota(jnp.int32, (META, LANES), 0)
+        row = lax.broadcasted_iota(jnp.int32, (PIECES, LANES), 0)
         pieces = jnp.where(row == 0, high, jnp.where(row == 1, middle, jnp.where(row == 2, low, 0.0)))
         held[blocks * rows :, :] = pieces.astype(bf16)
 
-    o_ref[0] = held[...]
-
-
-def input_grad(g_ref, w_ref, loss_ref, o_ref, total_ref):
-    rows = 128
-    pieces = jnp.sum(loss_ref[...].astype(f32), axis=0)
-    loss = jnp.sum(pieces, axis=0, keepdims=True)
-    total_ref[...] = loss
+    part = rows // 2
+    for ref, chunk in ((a_ref, 1 - place_ref[2]), (b_ref, place_ref[2])):
+        for c in range(blocks):
+            start = pl.multiple_of(c * rows + chunk * part, part)
+            ref[0, c * part : (c + 1) * part, :] = held[pl.ds(start, part), :]
+    a_ref[0, blocks * part :, :] = held[blocks * rows :, :]
+
+
+def scaled_by_power(chunk):
+    largest = jnp.max(jnp.max(jnp.abs(chunk), axis=0, keepdims=True), axis=1, keepdims=True)
+    power = exponent_of(largest)
+    return chunk * jnp.exp2(TOP - power), power
+
+
+def loss_rows(loss):
     row = lax.broadcasted_iota(jnp.int32, (META, LANES), 0)
-    loss_power = exponent_of(loss)
-    scaled_loss = loss * jnp.exp2(10.0 - loss_power)
-    high = jnp.floor(scaled_loss)
-    rest = (scaled_loss - high) * 2048.0
+    power = exponent_of(loss)
+    scaled = loss * jnp.exp2(10.0 - power)
+    high = jnp.floor(scaled)
+    rest = (scaled - high) * 2048.0
     middle = jnp.floor(rest)
     low = jnp.floor((rest - middle) * 2048.0)
-    meta = jnp.where(row == 1, loss_power, jnp.where(row == 2, high, jnp.where(row == 3, middle, low)))
+    return row, jnp.where(row == 1, power, jnp.where(row == 2, high, jnp.where(row == 3, middle, low)))
+
+
+def chunk_terms(g_ref, w_ref):
+    part = 64
     grad = jnp.concatenate(
         [
-            jnp.concatenate([g_ref[n, c * rows : (c + 1) * rows, :] for c in range(8)], axis=1)
-            for n in range(2)
+            jnp.concatenate([g_ref[n, c * part : (c + 1) * part, :] for c in range(8)], axis=1)
+            for n in range(g_ref.shape[0])
         ],
         axis=0,
     )
-    partial = lax.dot_general(grad, w_ref[...], (((1,), (1,)), ((), ())), preferred_element_type=f32)
-    for n in range(4):
-        chunk = partial[64 * n : 64 * n + 64]
-        largest = jnp.max(jnp.max(jnp.abs(chunk), axis=0, keepdims=True), axis=1, keepdims=True)
-        power = exponent_of(largest)
-        scaled = chunk * jnp.exp2(TOP - power)
+    terms = lax.dot_general(grad, w_ref[...], (((1,), (1,)), ((), ())), preferred_element_type=f32)
+    return [terms[n * part : (n + 1) * part] for n in range(g_ref.shape[0])]
+
+
+def send_terms(g_ref, w_ref, loss_ref, send_ref, total_ref):
+    pieces = jnp.sum(loss_ref[...].astype(f32), axis=0)
+    total_ref[...] = jnp.sum(pieces, axis=0, keepdims=True)
+    for n, chunk in enumerate(chunk_terms(g_ref, w_ref)):
+        scaled, power = scaled_by_power(chunk)
+        for c in range(4):
+            send_ref[n, 64 * c : 64 * c + 64, :] = scaled[:, c * LANES : (c + 1) * LANES]
+        send_ref[n, 256:, :] = jnp.broadcast_to(power, (META, LANES))
+
+
+def keep_terms(g_ref, w_ref, got_ref, loss_ref, o_ref):
+    row, meta = loss_rows(loss_ref[...])
+    for n, chunk in enumerate(chunk_terms(g_ref, w_ref)):
+        got = jnp.concatenate([got_ref[n, 64 * c : 64 * c + 64, :] for c in range(4)], axis=1)
+        chunk = chunk + got * jnp.exp2(got_ref[n, 256:257, 0:1] - TOP)
+        scaled, power = scaled_by_power(chunk)
         for c in range(4):
             o_ref[n, 64 * c : 64 * c + 64, :] = scaled[:, c * LANES : (c + 1) * LANES]
         o_ref[n, 256:, :] = jnp.where(row == 0, power, meta)
 
 
-def weight_grad(core_ref, s_ref, g_ref, after_ref, send_ref, keep_ref):
+def weight_grad(place_ref, s_ref, t_ref, g_ref, h_ref, after_ref, send_ref, keep_ref, held):
     del after_ref
-    tokens, width = s_ref.shape
-    half = width // 2
-    rows = 128
-    grad = jnp.concatenate(
-        [g_ref[:, c * rows : (c + 1) * rows, :].reshape(tokens, LANES) for c in range(2)], axis=1
-    )
-    core = core_ref[0]
-    for ref, which in ((send_ref, 1 - core), (keep_ref, core)):
-        part = s_ref[:, pl.ds(pl.multiple_of(which * half, half), half)]
-        ref[...] = lax.dot_general(part, grad, (((0,), (0,)), ((), ())), preferred_element_type=f32)
+    width = s_ref.shape[-1]
+    half, part = width // 2, 64
+    core = place_ref[3]
+
+    @pl.when(pl.program_id(0) == 0)
+    def _():
+        for n, which in enumerate((1 - core, core)):
+            lanes = pl.ds(pl.multiple_of(which * half, half), half)
+            student = jnp.concatenate([x[:, 0, :, lanes].reshape(-1, half) for x in (s_ref, t_ref)], axis=0)
+            held[n * half : (n + 1) * half, :] = student.T
+
+    def columns(ref):
+        parts = [ref[:, c * part : (c + 1) * part, :].reshape(-1, LANES) for c in range(2)]
+        return jnp.concatenate(parts, axis=1)
+
+    grad = jnp.concatenate([columns(g_ref), columns(h_ref)], axis=0)
+    send_ref[...] = jnp.dot(held[:half, :], grad, preferred_element_type=f32)
+    keep_ref[...] = jnp.dot(held[half:, :], grad, preferred_element_type=f32)
+
+
+def finish(terms_ref, after_ref, o_ref, loss_ref):
+    del after_ref
+    total = jnp.zeros(terms_ref.shape[1:], f32)[:256]
+    loss = jnp.zeros((1, LANES), f32)
+    for n in range(terms_ref.shape[0]):
+        meta = terms_ref[n, 256:, :]
+        total = total + terms_ref[n, :256, :] * jnp.exp2(meta[:1] - TOP)
+        loss = loss + (meta[2:3] + (meta[3:4] + meta[4:5] / 2048.0) / 2048.0) * jnp.exp2(meta[1:2] - 10.0)
+    loss_ref[...] = loss
+    for c in range(4):
+        o_ref[:, c * LANES : (c + 1) * LANES] = total[64 * c : 64 * c + 64].astype(bf16)
 
 
 def body(student_hidden, teacher_hidden, proj_weight):
@@ -155,7 +210,8 @@
     blocks = columns // LANES
 
     dp_index = lax.axis_index("dp").astype(jnp.int32)
-    place = jnp.stack([dp_index // 4, dp_index % 4])
+    core = (lax.axis_index("seq") % 2).astype(jnp.int32)
+    place = jnp.stack([dp_index // 4, dp_index % 4, dp_index % 2, core])
     scalars = pl.BlockSpec(memory_space=pltpu.SMEM)
     whole = pl.BlockSpec(memory_space=pltpu.VMEM)
 
@@ -173,7 +229,7 @@
         )(place, spread.reshape(64, -1))
         near = [packed[0]]
         for k in range(1, 4):
-            moves = [(z, z // 4 * 4 + (z + k) % 4) for z in range(dp_count)]
+            moves = [(z, (z + (k if k < 3 else -1)) % dp_count) for z in range(dp_count)]
             near.append(lax.ppermute(packed[k], "dp", moves))
         packed = call(
             regroup_teacher,
@@ -208,66 +264,88 @@
         prediction = jnp.sum(data * unscale[:, None, :, None], axis=0)
 
     with jax.named_scope("gradient"):
-        grad_own = call(
+        part = blocks * own // 2
+        block_a = pl.BlockSpec((1, part + PIECES, LANES), lambda i: (i, 0, 0))
+        block_b = pl.BlockSpec((1, part, LANES), lambda i: (i, 0, 0))
+        own_a, own_b = call(
             token_grad,
-            jax.ShapeDtypeStruct((tensor_count, size, LANES), bf16),
+            (
+                jax.ShapeDtypeStruct((tensor_count, part + PIECES, LANES), bf16),
+                jax.ShapeDtypeStruct((tensor_count, part, LANES), bf16),
+            ),
             2 * own * own * columns,
             3_000_000,
             grid=(tensor_count,),
             in_specs=[scalars, pl.BlockSpec((blocks, own, LANES), lambda i: (0, 0, 0))]
             + [pl.BlockSpec(group[0].shape, lambda i: (0, 0))] * 4,
-            out_specs=pl.BlockSpec((1, size, LANES), lambda i: (i, 0, 0)),
-            scratch_shapes=[pltpu.VMEM((size, LANES), bf16)],
+            out_specs=(block_a, block_b),
+            scratch_shapes=[pltpu.VMEM((blocks * own + PIECES, LANES), bf16)],
         )(place, prediction, *target)
-        grad = all_to_all(grad_own, "tensor")
+        grad_a = all_to_all(own_a, "tensor")
+        grad_b = all_to_all(own_b, "tensor")
 
     with jax.named_scope("input_grad"):
         chunk = 64 * 4 + META
-        term, total = call(
-            input_grad,
-            (jax.ShapeDtypeStruct((dp_count, chunk, LANES), f32), jax.ShapeDtypeStruct((1, LANES), f32)),
-            2 * tokens * width_local * columns,
+        dp_half = dp_count // 2
+        half_terms = jax.ShapeDtypeStruct((dp_half, chunk, LANES), f32)
+        weights = pl.BlockSpec((width_local, columns), lambda i: (0, 0))
+        losses = pl.BlockSpec((1, LANES), lambda i: (0, 0))
+        block = pl.BlockSpec((4, chunk, LANES), lambda i: (i, 0, 0))
+        send, total = call(
+            send_terms,
+            (half_terms, jax.ShapeDtypeStruct((1, LANES), f32)),
+            tokens * width_local * columns,
+            4_000_000,
+            grid=(2,),
+            in_specs=[
+                pl.BlockSpec((4, part + PIECES, LANES), lambda i: (i, 0, 0)),
+                weights,
+                pl.BlockSpec((tensor_count, PIECES, LANES), lambda i: (0, part // PIECES, 0)),
+            ],
+            out_specs=(block, losses),
+        )(grad_a, proj_weight, grad_a)
+        neighbour = [(z, z ^ 1) for z in range(dp_count)]
+        loss = butterfly(total, (("seq", 1), ("seq", 2), ("dp", 1)))
+        got = lax.ppermute(send.astype(f16), "dp", neighbour).astype(f32)
+        term = call(
+            keep_terms,
+            half_terms,
+            tokens * width_local * columns,
             5_000_000,
-            grid=(tensor_count // 2,),
-            in_specs=[
-                pl.BlockSpec((2, size, LANES), lambda i: (i, 0, 0)),
-                pl.BlockSpec((width_local, columns), lambda i: (0, 0)),
-                pl.BlockSpec((tensor_count, META, LANES), lambda i: (0, blocks * own // META, 0)),
-            ],
-            out_specs=(
-                pl.BlockSpec((4, chunk, LANES), lambda i: (i, 0, 0)),
-                pl.BlockSpec((1, LANES), lambda i: (0, 0)),
-            ),
-        )(grad, proj_weight, grad)
-        terms = all_to_all(term.astype(f16), "dp").astype(f32)
-        unscale = jnp.exp2(terms[:, 256:257, 0:1] - TOP)
-        summed = jnp.sum(terms[:, :256, :] * unscale, axis=0)
-        grad_input = jnp.transpose(summed.reshape(4, 64, LANES), (1, 0, 2)).astype(bf16)
-        grad_input = grad_input.reshape(1, 4, 16, width_local)
+            grid=(2,),
+            in_specs=[pl.BlockSpec((4, part, LANES), lambda i: (i, 0, 0)), weights, block, losses],
+            out_specs=block,
+        )(grad_b, proj_weight, got, loss)
+        same_parity = [list(range(p, dp_count, 2)) for p in range(2)]
+        terms = lax.all_to_all(term.astype(f16), "dp", 0, 0, axis_index_groups=same_parity).astype(f32)
 
     with jax.named_scope("weight_grad"):
-        seq_index = lax.axis_index("seq")
-        core = seq_index % 2
         other_core = [(i, i ^ 1) for i in range(seq_count)]
         other_y = [(i, i ^ 2) for i in range(seq_count)]
         half = jax.ShapeDtypeStruct((width_local // 2, columns), f32)
+        by_chunk = student.reshape(8, 2, 64, width_local)
         send, keep = call(
             weight_grad,
             (half, half),
             2 * tokens * width_local * columns,
             5_000_000,
-            grid=(4,),
-            in_specs=[
-                scalars,
-                pl.BlockSpec((tokens, width_local), lambda i: (0, 0)),
-                pl.BlockSpec((tensor_count, 2 * own, LANES), lambda i: (0, i, 0)),
-                pl.BlockSpec((1, LANES), lambda i: (0, 0)),
-            ],
-            out_specs=(
-                pl.BlockSpec((width_local // 2, 2 * LANES), lambda i: (0, i)),
-                pl.BlockSpec((width_local // 2, 2 * LANES), lambda i: (0, i)),
+            grid_spec=pltpu.PrefetchScalarGridSpec(
+                num_scalar_prefetch=1,
+                grid=(4,),
+                in_specs=[
+                    pl.BlockSpec((8, 1, 64, width_local), lambda i, p: (0, 1 - p[2], 0, 0)),
+                    pl.BlockSpec((8, 1, 64, width_local), lambda i, p: (0, p[2], 0, 0)),
+                    pl.BlockSpec((tensor_count, own, LANES), lambda i, p: (0, i, 0)),
+                    pl.BlockSpec((tensor_count, own, LANES), lambda i, p: (0, i, 0)),
+                    pl.BlockSpec((1, META, LANES), lambda i, p: (0, 256 // META, 0)),
+                ],
+                out_specs=(
+                    pl.BlockSpec((width_local // 2, 2 * LANES), lambda i, p: (0, i)),
+                    pl.BlockSpec((width_local // 2, 2 * LANES), lambda i, p: (0, i)),
+                ),
+                scratch_shapes=[pltpu.VMEM((width_local, tokens), bf16)],
             ),
-        )(core.reshape(1).astype(jnp.int32), student, grad, total)
+        )(place, by_chunk, by_chunk, grad_a, grad_b, term)
         pair = (keep + lax.ppermute(send, "seq", other_core)).astype(bf16)
         mine = pair.astype(f32) + lax.ppermute(pair, "seq", other_y).astype(f32)
         theirs = lax.ppermute(mine, "seq", other_core)
@@ -277,10 +355,24 @@
             jnp.concatenate([theirs, mine], axis=0),
         )
 
-    with jax.named_scope("loss"):
-        pieces = terms[:, 257:261, 0]
-        losses = (pieces[:, 1] + (pieces[:, 2] + pieces[:, 3] / 2048.0) / 2048.0) * jnp.exp2(pieces[:, 0] - 10.0)
-        loss_value = lax.psum(jnp.sum(losses), "seq") / (tokens * seq_count * columns * dp_count)
+    with jax.named_scope("results"):
+        grad_input, loss = call(
+            finish,
+            (jax.ShapeDtypeStruct((own // 2, width_local), bf16), jax.ShapeDtypeStruct((1, LANES), f32)),
+            0,
+            1_200_000,
+            grid=(1,),
+            in_specs=[
+                pl.BlockSpec((dp_half, chunk, LANES), lambda i: (0, 0, 0)),
+                pl.BlockSpec((8, LANES), lambda i: (0, 0)),
+            ],
+            out_specs=(
+                pl.BlockSpec((own // 2, width_local), lambda i: (0, 0)),
+                pl.BlockSpec((1, LANES), lambda i: (0, 0)),
+            ),
+        )(terms, grad_weight)
+        grad_input = grad_input.reshape(1, 4, 16, width_local)
+        loss_value = loss[0, 0] / (tokens * seq_count * columns * dp_count)
     return (loss_value, grad_weight, grad_input)
 
 

time: 179 us -> 169 us (0.944)
  the two profiles are of different devices: /device:TPU:1 before, /device:TPU:34 now
where the time goes in v3:
time: 169 us; the launch traced here: 168 us
  starting transfers between devices  84 us (50%)
  waiting for transfers between devices  41.3 us (24%)
  blocking collectives  16.1 us (10%)
  Pallas kernels  11.6 us (7%)
  other arithmetic  7.28 us (4%)
  local copies, waits for them, and re-layouts  5.14 us (3%)
  between operations  2.11 us (1%)
    ppermute x3, starting transfers between devices, body(): target.append(lax.ppermute(packed[m], 'dp', moves))  20.7 us
    all_to_all x3, starting transfers between devices, all_to_all(): return lax.all_to_all(x, axis, 0, 0)  16.4 us
    all_to_all x1, blocking collectives, all_to_all(): return lax.all_to_all(x, axis, 0, 0)  16.1 us
    ppermute x1, waiting for transfers between devices, body(): mine = pair.astype(f32) + lax.ppermute(pair, 'seq', other_y).astype(f32)  12.6 us
    ppermute x3, starting transfers between devices, body(): near.append(lax.ppermute(packed[k], 'dp', moves))  12.1 us
    all_to_all x1, waiting for transfers between devices, body(): lax.all_to_all(term.astype(f16), 'dp', 0, 0, axis_index_groups=same_parity)  11.5 us
    all_to_all x1, starting transfers between devices, body(): lax.all_to_all(term.astype(f16), 'dp', 0, 0, axis_index_groups=same_parity)  10.6 us
    ppermute x3, starting transfers between devices, butterfly(): lax.ppermute(x, axis, [(i, i ^ step) for i in range(lax.axis_size(axis))])  8.36 us
  transfers between devices with their start and end apart: 17, of which 8 were waited for; matrix products, arithmetic and copies ran while one was open for 4% of the time, Pallas kernels for 3%

profile of v3, /device:TPU:34, one launch (start us, length us, event | category | flops | bytes accessed | tf_op | source)
XLA Modules:
  0.0 167.6 jit_solution(17199086353505258541)
XLA Ops:
  0.6 5.9 %all-to-all-start.1 = ((bf16[8,8,2048]{2,1,0:T(8,128)(2,1)}), bf16[8,8,2048]{2,1,0:T(8,128)(2,1)S(1)}, u32[]{:S(2)}, u32[]{:S(2)}) async-start(bf16[8,8,2048]{2,1,0:T(8,128)(2,1)} %bitcast.21), calls=%async_computation.1 | async-start | bytes 524288 | tf_op jit(solution)/shard_map/teacher/all_to_all | solution.py:28
  6.5 1.2 copy-done
  7.7 1.2 copy-done.2
  8.9 2.3 %prediction.1 = f32[8,1032,128]{2,1,0:T(8,128)S(1)} custom-call(bf16[1024,512]{1,0:T(8,128)(2,1)S(1)} %bitcast.15, bf16[512,1024]{1,0:T(8,128)(2,1)S(1)} %copy-done), custom_call_target="tpu_custom_call" | custom-call | flops 1073741824 | bytes 6000000 | tf_op jit(solution)/shard_map/prediction/pallas_call | solution.py:249
  11.2 1.6 convert_element_type.27
  12.9 5.7 %all-to-all-start = ((f16[8,1032,128]{2,1,0:T(8,128)(2,1)}), f16[8,1032,128]{2,1,0:T(8,128)(2,1)S(1)}, u32[]{:S(2)}, u32[]{:S(2)}) async-start(f16[8,1032,128]{2,1,0:T(8,128)(2,1)} %convert_element_type.27), calls=%async_computation | async-start | bytes 4227072 | tf_op jit(solution)/shard_map/prediction/all_to_all | solution.py:28
  18.6 0.1 pad_add_fusion.place_ref
  18.7 0.8 teacher.2
  19.4 3.8 %collective-permute-start = (bf16[64,640]{1,0:T(8,128)(2,1)S(1)}, bf16[64,640]{1,0:T(8,128)(2,1)S(1)}, u32[]{:S(2)}, u32[]{:S(2)}) collective-permute-start(bf16[64,640]{1,0:T(8,128)(2,1)S(1)} %get-tuple-element.20), channel_id=1, source_target_pairs={{0,32},{32,64},{64,96},{96,128},{128,160},{160,192},{192,224},{224... | collective-permute-start | bytes 245768 | tf_op jit(solution)/shard_map/teacher/ppermute | solution.py:233
  23.2 6.4 %collective-permute-start.1 = (bf16[64,640]{1,0:T(8,128)(2,1)S(1)}, bf16[64,640]{1,0:T(8,128)(2,1)S(1)}, u32[]{:S(2)}, u32[]{:S(2)}) collective-permute-start(bf16[64,640]{1,0:T(8,128)(2,1)S(1)} %get-tuple-element.21), channel_id=1, source_target_pairs={{0,64},{32,96},{64,128},{96,160},{128,192},{160,224},{192,256},{22... | collective-permute-start | bytes 245768 | tf_op jit(solution)/shard_map/teacher/ppermute | solution.py:233
  29.6 1.9 %collective-permute-start.2 = (bf16[64,640]{1,0:T(8,128)(2,1)S(1)}, bf16[64,640]{1,0:T(8,128)(2,1)S(1)}, u32[]{:S(2)}, u32[]{:S(2)}) collective-permute-start(bf16[64,640]{1,0:T(8,128)(2,1)S(1)} %get-tuple-element.22), channel_id=1, source_target_pairs={{0,480},{32,0},{64,32},{96,64},{128,96},{160,128},{192,160},{224,1... | collective-permute-start | bytes 245768 | tf_op jit(solution)/shard_map/teacher/ppermute | solution.py:233
  31.6 3.8 %collective-permute-done.1.refs_2_ = bf16[64,640]{1,0:T(8,128)(2,1)S(1)} collective-permute-done((bf16[64,640]{1,0:T(8,128)(2,1)S(1)}, bf16[64,640]{1,0:T(8,128)(2,1)S(1)}, u32[]{:S(2)}, u32[]{:S(2)}) %collective-permute-start.1) | collective-permute-done | bytes 81952 | tf_op jit(solution)/shard_map/teacher/ppermute | solution.py:233
  35.4 0.6 collective-permute-done.2.refs_3_
  36.0 0.6 teacher.3
  36.6 9.1 %collective-permute-start.3 = (bf16[64,640]{1,0:T(8,128)(2,1)S(1)}, bf16[64,640]{1,0:T(8,128)(2,1)S(1)}, u32[]{:S(2)}, u32[]{:S(2)}) collective-permute-start(bf16[64,640]{1,0:T(8,128)(2,1)S(1)} %get-tuple-element.24), channel_id=1, source_target_pairs={{0,128},{32,160},{64,192},{96,224},{128,256},{160,288},{192,320},{... | collective-permute-start | bytes 245768 | tf_op jit(solution)/shard_map/teacher/ppermute | solution.py:245
  45.7 5.4 %collective-permute-start.4 = (bf16[64,640]{1,0:T(8,128)(2,1)S(1)}, bf16[64,640]{1,0:T(8,128)(2,1)S(1)}, u32[]{:S(2)}, u32[]{:S(2)}) collective-permute-start(bf16[64,640]{1,0:T(8,128)(2,1)S(1)} %get-tuple-element.25), channel_id=1, source_target_pairs={{0,256},{32,288},{64,320},{96,352},{128,384},{160,416},{192,448},{... | collective-permute-start | bytes 245768 | tf_op jit(solution)/shard_map/teacher/ppermute | solution.py:245
  51.0 6.2 %collective-permute-start.5 = (bf16[64,640]{1,0:T(8,128)(2,1)S(1)}, bf16[64,640]{1,0:T(8,128)(2,1)S(1)}, u32[]{:S(2)}, u32[]{:S(2)}) collective-permute-start(bf16[64,640]{1,0:T(8,128)(2,1)S(1)} %get-tuple-element.26), channel_id=1, source_target_pairs={{0,384},{32,416},{64,448},{96,480},{128,0},{160,32},{192,64},{224,... | collective-permute-start | bytes 245768 | tf_op jit(solution)/shard_map/teacher/ppermute | solution.py:245
  57.3 0.3 convert_element_type.28
  57.6 1.4 fusion
  59.0 5.8 %collective-permute-done.4.t2_ref = bf16[64,640]{1,0:T(8,128)(2,1)S(1)} collective-permute-done((bf16[64,640]{1,0:T(8,128)(2,1)S(1)}, bf16[64,640]{1,0:T(8,128)(2,1)S(1)}, u32[]{:S(2)}, u32[]{:S(2)}) %collective-permute-start.4) | collective-permute-done | bytes 81952 | tf_op jit(solution)/shard_map/teacher/ppermute | solution.py:245
  64.7 1.4 gradient.1
  66.2 16.1 %all_to_all.25.g_ref.loss_ref = bf16[8,528,128]{2,1,0:T(8,128)(2,1)S(1)} all-to-all(bf16[8,528,128]{2,1,0:T(8,128)(2,1)S(1)} %get-tuple-element.28), channel_id=1, replica_groups=mesh['dp'=16,'seq'=4,'tensor'=8] {'tensor'}, dimensions={0} | all-to-all | bytes 2162688 | tf_op jit(solution)/shard_map/gradient/all_to_all | solution.py:28
  82.3 4.8 %all-to-all-start.2 = ((bf16[8,512,128]{2,1,0:T(8,128)(2,1)}), bf16[8,512,128]{2,1,0:T(8,128)(2,1)S(1)}, u32[]{:S(2)}, u32[]{:S(2)}) async-start(bf16[8,512,128]{2,1,0:T(8,128)(2,1)} %copy-done.6), calls=%async_computation.2 | async-start | bytes 2097152 | tf_op jit(solution)/shard_map/gradient/all_to_all | solution.py:28
  87.2 1.2 input_grad.2
  88.4 7.1 %collective-permute-start.6 = (f16[8,264,128]{2,1,0:T(8,128)(2,1)S(1)}, f16[8,264,128]{2,1,0:T(8,128)(2,1)S(1)}, u32[]{:S(2)}, u32[]{:S(2)}) collective-permute-start(f16[8,264,128]{2,1,0:T(8,128)(2,1)S(1)} %convert_element_type.29), channel_id=1, source_target_pairs={{0,32},{32,0},{64,96},{96,64},{128,160},{160,128},{192,224},{224,1... | collective-permute-start | bytes 1622024 | tf_op jit(solution)/shard_map/input_grad/ppermute | solution.py:309
  95.5 1.9 %collective-permute-start.7 = (f32[1,128]{1,0:T(1,128)S(1)}, f32[1,128]{1,0:T(1,128)S(1)}, u32[]{:S(2)}, u32[]{:S(2)}) collective-permute-start(f32[1,128]{1,0:T(1,128)S(1)} %get-tuple-element.30), channel_id=1, source_target_pairs={{0,8},{8,0},{16,24},{24,16},{1,9},{9,1},{17,25},{25,17},{2,10},{10... | collective-permute-start | bytes 1544 | tf_op jit(solution)/shard_map/input_grad/ppermute | solution.py:33
  97.5 1.1 collective-permute-done.7
  98.5 4.5 %collective-permute-start.8 = (f32[1,128]{1,0:T(1,128)S(1)}, f32[1,128]{1,0:T(1,128)S(1)}, u32[]{:S(2)}, u32[]{:S(2)}) collective-permute-start(f32[1,128]{1,0:T(1,128)S(1)} %add.35), channel_id=1, source_target_pairs={{0,16},{8,24},{16,0},{24,8},{1,17},{9,25},{17,1},{25,9},{2,18},{10... | collective-permute-start | bytes 1544 | tf_op jit(solution)/shard_map/input_grad/ppermute | solution.py:33
  103.1 2.4 %collective-permute-done.8 = f32[1,128]{1,0:T(1,128)S(1)} collective-permute-done((f32[1,128]{1,0:T(1,128)S(1)}, f32[1,128]{1,0:T(1,128)S(1)}, u32[]{:S(2)}, u32[]{:S(2)}) %collective-permute-start.8) | collective-permute-done | bytes 544 | tf_op jit(solution)/shard_map/input_grad/ppermute | solution.py:33
  105.5 1.9 %collective-permute-start.9 = (f32[1,128]{1,0:T(1,128)S(1)}, f32[1,128]{1,0:T(1,128)S(1)}, u32[]{:S(2)}, u32[]{:S(2)}) collective-permute-start(f32[1,128]{1,0:T(1,128)S(1)} %add.36), channel_id=1, source_target_pairs={{0,32},{32,0},{64,96},{96,64},{128,160},{160,128},{192,224},{224,1... | collective-permute-start | bytes 1544 | tf_op jit(solution)/shard_map/input_grad/ppermute | solution.py:33
  107.4 3.5 %collective-permute-done.9 = f32[1,128]{1,0:T(1,128)S(1)} collective-permute-done((f32[1,128]{1,0:T(1,128)S(1)}, f32[1,128]{1,0:T(1,128)S(1)}, u32[]{:S(2)}, u32[]{:S(2)}) %collective-permute-start.9) | collective-permute-done | bytes 544 | tf_op jit(solution)/shard_map/input_grad/ppermute | solution.py:33
  110.9 1.1 convert_element_type.30.got_ref
  112.0 1.2 copy-done.5
  113.2 1.2 input_grad.3.after_ref
  114.4 3.3 %weight_grad.1 = (f32[256,1024]{1,0:T(8,128)S(1)}, f32[256,1024]{1,0:T(8,128)S(1)}) custom-call(s32[4]{0:T(128)S(1)} %pad_add_fusion.place_ref, bf16[8,2,64,512]{3,2,1,0:T(8,128)(2,1)S(1)} %bitcast.16, bf16[8,2,64,512]{3,2,1,0:T(8,128)(2,1)S(1)} %bitcast.17, bf16[8,528,128]{2,1,0:T(8,128)(2,1)S(1)} %all_to_all.25.g_ref.loss_ref, ...), custom_call_target="tpu_custom_call" | custom-call | flops 1073741824 | bytes 5000000 | tf_op jit(solution)/shard_map/weight_grad/pallas_call | solution.py:327
  117.8 1.0 copy-done.7
  118.7 2.0 %collective-permute-start.10 = (f32[256,1024]{1,0:T(8,128)S(1)}, f32[256,1024]{1,0:T(8,128)}, u32[]{:S(2)}, u32[]{:S(2)}) collective-permute-start(f32[256,1024]{1,0:T(8,128)S(1)} %get-tuple-element.32), channel_id=1, source_target_pairs={{0,8},{8,0},{16,24},{24,16},{1,9},{9,1},{17,25},{25,17},{2,10},{10... | collective-permute-start | bytes 3145736 | tf_op jit(solution)/shard_map/weight_grad/ppermute | solution.py:349
  120.8 0.9 convert_element_type.31
  121.6 10.6 %all-to-all-start.4 = ((f16[8,264,128]{2,1,0:T(8,128)(2,1)}), f16[8,264,128]{2,1,0:T(8,128)(2,1)S(1)}, u32[]{:S(2)}, u32[]{:S(2)}) async-start(f16[8,264,128]{2,1,0:T(8,128)(2,1)} %convert_element_type.31), calls=%async_computation.4 | async-start | bytes 1081344 | tf_op jit(solution)/shard_map/input_grad/all_to_all | solution.py:320
  132.3 1.4 add_convert_fusion
  133.7 4.8 %collective-permute-start.11 = (bf16[256,1024]{1,0:T(8,128)(2,1)S(1)}, bf16[256,1024]{1,0:T(8,128)(2,1)S(1)}, u32[]{:S(2)}, u32[]{:S(2)}) collective-permute-start(bf16[256,1024]{1,0:T(8,128)(2,1)S(1)} %add_convert_fusion), channel_id=1, source_target_pairs={{0,16},{8,24},{16,0},{24,8},{1,17},{9,25},{17,1},{25,9},{2,18},{10... | collective-permute-start | bytes 1572872 | tf_op jit(solution)/shard_map/weight_grad/ppermute | solution.py:350
  138.5 12.6 %collective-permute-done.11 = bf16[256,1024]{1,0:T(8,128)(2,1)S(1)} collective-permute-done((bf16[256,1024]{1,0:T(8,128)(2,1)S(1)}, bf16[256,1024]{1,0:T(8,128)(2,1)S(1)}, u32[]{:S(2)}, u32[]{:S(2)}) %collective-permute-start.11) | collective-permute-done | bytes 524320 | tf_op jit(solution)/shard_map/weight_grad/ppermute | solution.py:350
  151.1 0.2 convert_add_fusion
  151.3 1.9 %collective-permute-start.12 = (f32[256,1024]{1,0:T(8,128)S(1)}, f32[256,1024]{1,0:T(8,128)S(1)}, u32[]{:S(2)}, u32[]{:S(2)}) collective-permute-start(f32[256,1024]{1,0:T(8,128)S(1)} %convert_add_fusion), channel_id=1, source_target_pairs={{0,8},{8,0},{16,24},{24,16},{1,9},{9,1},{17,25},{25,17},{2,10},{10... | collective-permute-start | bytes 3145736 | tf_op jit(solution)/shard_map/weight_grad/ppermute | solution.py:351
  153.2 11.5 %all-to-all-done.4 = f16[8,264,128]{2,1,0:T(8,128)(2,1)S(1)} async-done(((f16[8,264,128]{2,1,0:T(8,128)(2,1)}), f16[8,264,128]{2,1,0:T(8,128)(2,1)S(1)}, u32[]{:S(2)}, u32[]{:S(2)}) %all-to-all-start.4) | async-done | bytes 540704 | tf_op jit(solution)/shard_map/input_grad/all_to_all | solution.py:320
  164.8 0.3 maximum_select_fusion.after_ref
  165.2 0.8 results.1
  166.0 0.5 copy-done.4
  (29 shorter events, 0.2 us)
Async XLA Ops:
  0.6 12.2 %all-to-all-start.1 = ((bf16[8,8,2048]{2,1,0:T(8,128)(2,1)}), bf16[8,8,2048]{2,1,0:T(8,128)(2,1)S(1)}, u32[]{:S(2)}, u32[]{:S(2)}) async-start(bf16[8,8,2048]{2,1,0:T(8,128)(2,1)} %bitcast.21), calls=%async_computation.1 | async-start | bytes 524288 | tf_op jit(solution)/shard_map/teacher/all_to_all | solution.py:28
  6.5 1.2 copy-start
  7.7 1.2 copy-start.2
  12.9 44.4 %all-to-all-start = ((f16[8,1032,128]{2,1,0:T(8,128)(2,1)}), f16[8,1032,128]{2,1,0:T(8,128)(2,1)S(1)}, u32[]{:S(2)}, u32[]{:S(2)}) async-start(f16[8,1032,128]{2,1,0:T(8,128)(2,1)} %convert_element_type.27), calls=%async_computation | async-start | bytes 4227072 | tf_op jit(solution)/shard_map/prediction/all_to_all | solution.py:28
  19.4 12.2 %collective-permute-start = (bf16[64,640]{1,0:T(8,128)(2,1)S(1)}, bf16[64,640]{1,0:T(8,128)(2,1)S(1)}, u32[]{:S(2)}, u32[]{:S(2)}) collective-permute-start(bf16[64,640]{1,0:T(8,128)(2,1)S(1)} %get-tuple-element.20), channel_id=1, source_target_pairs={{0,32},{32,64},{64,96},{96,128},{128,160},{160,192},{192,224},{224... | collective-permute-start | bytes 245768 | tf_op jit(solution)/shard_map/teacher/ppermute | solution.py:233
  23.2 12.1 %collective-permute-start.1 = (bf16[64,640]{1,0:T(8,128)(2,1)S(1)}, bf16[64,640]{1,0:T(8,128)(2,1)S(1)}, u32[]{:S(2)}, u32[]{:S(2)}) collective-permute-start(bf16[64,640]{1,0:T(8,128)(2,1)S(1)} %get-tuple-element.21), channel_id=1, source_target_pairs={{0,64},{32,96},{64,128},{96,160},{128,192},{160,224},{192,256},{22... | collective-permute-start | bytes 245768 | tf_op jit(solution)/shard_map/teacher/ppermute | solution.py:233
  29.6 6.3 %collective-permute-start.2 = (bf16[64,640]{1,0:T(8,128)(2,1)S(1)}, bf16[64,640]{1,0:T(8,128)(2,1)S(1)}, u32[]{:S(2)}, u32[]{:S(2)}) collective-permute-start(bf16[64,640]{1,0:T(8,128)(2,1)S(1)} %get-tuple-element.22), channel_id=1, source_target_pairs={{0,480},{32,0},{64,32},{96,64},{128,96},{160,128},{192,160},{224,1... | collective-permute-start | bytes 245768 | tf_op jit(solution)/shard_map/teacher/ppermute | solution.py:233
  36.6 22.4 %collective-permute-start.3 = (bf16[64,640]{1,0:T(8,128)(2,1)S(1)}, bf16[64,640]{1,0:T(8,128)(2,1)S(1)}, u32[]{:S(2)}, u32[]{:S(2)}) collective-permute-start(bf16[64,640]{1,0:T(8,128)(2,1)S(1)} %get-tuple-element.24), channel_id=1, source_target_pairs={{0,128},{32,160},{64,192},{96,224},{128,256},{160,288},{192,320},{... | collective-permute-start | bytes 245768 | tf_op jit(solution)/shard_map/teacher/ppermute | solution.py:245
  45.7 19.1 %collective-permute-start.4 = (bf16[64,640]{1,0:T(8,128)(2,1)S(1)}, bf16[64,640]{1,0:T(8,128)(2,1)S(1)}, u32[]{:S(2)}, u32[]{:S(2)}) collective-permute-start(bf16[64,640]{1,0:T(8,128)(2,1)S(1)} %get-tuple-element.25), channel_id=1, source_target_pairs={{0,256},{32,288},{64,320},{96,352},{128,384},{160,416},{192,448},{... | collective-permute-start | bytes 245768 | tf_op jit(solution)/shard_map/teacher/ppermute | solution.py:245
  51.0 13.7 %collective-permute-start.5 = (bf16[64,640]{1,0:T(8,128)(2,1)S(1)}, bf16[64,640]{1,0:T(8,128)(2,1)S(1)}, u32[]{:S(2)}, u32[]{:S(2)}) collective-permute-start(bf16[64,640]{1,0:T(8,128)(2,1)S(1)} %get-tuple-element.26), channel_id=1, source_target_pairs={{0,384},{32,416},{64,448},{96,480},{128,0},{160,32},{192,64},{224,... | collective-permute-start | bytes 245768 | tf_op jit(solution)/shard_map/teacher/ppermute | solution.py:245
  66.2 16.2 %copy-start.6 = (bf16[8,512,128]{2,1,0:T(8,128)(2,1)}, bf16[8,512,128]{2,1,0:T(8,128)(2,1)S(1)}, u32[]{:S(2)}) copy-start(bf16[8,512,128]{2,1,0:T(8,128)(2,1)S(1)} %get-tuple-element.27) | copy-start | bytes 3145732
  66.2 21.0 %copy-start.1 = (bf16[512,1024]{1,0:T(8,128)(2,1)S(1)}, bf16[512,1024]{1,0:T(8,128)(2,1)}, u32[]{:S(2)}) copy-start(bf16[512,1024]{1,0:T(8,128)(2,1)} %w_ref.5) | copy-start | bytes 3145732
  82.3 29.6 %all-to-all-start.2 = ((bf16[8,512,128]{2,1,0:T(8,128)(2,1)}), bf16[8,512,128]{2,1,0:T(8,128)(2,1)S(1)}, u32[]{:S(2)}, u32[]{:S(2)}) async-start(bf16[8,512,128]{2,1,0:T(8,128)(2,1)} %copy-done.6), calls=%async_computation.2 | async-start | bytes 2097152 | tf_op jit(solution)/shard_map/gradient/all_to_all | solution.py:28
  88.4 22.5 %collective-permute-start.6 = (f16[8,264,128]{2,1,0:T(8,128)(2,1)S(1)}, f16[8,264,128]{2,1,0:T(8,128)(2,1)S(1)}, u32[]{:S(2)}, u32[]{:S(2)}) collective-permute-start(f16[8,264,128]{2,1,0:T(8,128)(2,1)S(1)} %convert_element_type.29), channel_id=1, source_target_pairs={{0,32},{32,0},{64,96},{96,64},{128,160},{160,128},{192,224},{224,1... | collective-permute-start | bytes 1622024 | tf_op jit(solution)/shard_map/input_grad/ppermute | solution.py:309
  95.5 3.0 %collective-permute-start.7 = (f32[1,128]{1,0:T(1,128)S(1)}, f32[1,128]{1,0:T(1,128)S(1)}, u32[]{:S(2)}, u32[]{:S(2)}) collective-permute-start(f32[1,128]{1,0:T(1,128)S(1)} %get-tuple-element.30), channel_id=1, source_target_pairs={{0,8},{8,0},{16,24},{24,16},{1,9},{9,1},{17,25},{25,17},{2,10},{10... | collective-permute-start | bytes 1544 | tf_op jit(solution)/shard_map/input_grad/ppermute | solution.py:33
  98.5 6.9 %collective-permute-start.8 = (f32[1,128]{1,0:T(1,128)S(1)}, f32[1,128]{1,0:T(1,128)S(1)}, u32[]{:S(2)}, u32[]{:S(2)}) collective-permute-start(f32[1,128]{1,0:T(1,128)S(1)} %add.35), channel_id=1, source_target_pairs={{0,16},{8,24},{16,0},{24,8},{1,17},{9,25},{17,1},{25,9},{2,18},{10... | collective-permute-start | bytes 1544 | tf_op jit(solution)/shard_map/input_grad/ppermute | solution.py:33
  105.5 5.4 %collective-permute-start.9 = (f32[1,128]{1,0:T(1,128)S(1)}, f32[1,128]{1,0:T(1,128)S(1)}, u32[]{:S(2)}, u32[]{:S(2)}) collective-permute-start(f32[1,128]{1,0:T(1,128)S(1)} %add.36), channel_id=1, source_target_pairs={{0,32},{32,0},{64,96},{96,64},{128,160},{160,128},{192,224},{224,1... | collective-permute-start | bytes 1544 | tf_op jit(solution)/shard_map/input_grad/ppermute | solution.py:33
  112.0 1.2 copy-start.5
  113.2 1.2 copy-start.3
  117.7 1.0 copy-start.7
  118.7 13.6 %copy-start.8 = (f32[256,1024]{1,0:T(8,128)S(1)}, f32[256,1024]{1,0:T(8,128)}, u32[]{:S(2)}) copy-start(f32[256,1024]{1,0:T(8,128)} %copy-done.7) | copy-start | bytes 3145732
  118.7 13.6 %collective-permute-start.10 = (f32[256,1024]{1,0:T(8,128)S(1)}, f32[256,1024]{1,0:T(8,128)}, u32[]{:S(2)}, u32[]{:S(2)}) collective-permute-start(f32[256,1024]{1,0:T(8,128)S(1)} %get-tuple-element.32), channel_id=1, source_target_pairs={{0,8},{8,0},{16,24},{24,16},{1,9},{9,1},{17,25},{25,17},{2,10},{10... | collective-permute-start | bytes 3145736 | tf_op jit(solution)/shard_map/weight_grad/ppermute | solution.py:349
  121.6 43.1 %all-to-all-start.4 = ((f16[8,264,128]{2,1,0:T(8,128)(2,1)}), f16[8,264,128]{2,1,0:T(8,128)(2,1)S(1)}, u32[]{:S(2)}, u32[]{:S(2)}) async-start(f16[8,264,128]{2,1,0:T(8,128)(2,1)} %convert_element_type.31), calls=%async_computation.4 | async-start | bytes 1081344 | tf_op jit(solution)/shard_map/input_grad/all_to_all | solution.py:320
  133.7 17.4 %collective-permute-start.11 = (bf16[256,1024]{1,0:T(8,128)(2,1)S(1)}, bf16[256,1024]{1,0:T(8,128)(2,1)S(1)}, u32[]{:S(2)}, u32[]{:S(2)}) collective-permute-start(bf16[256,1024]{1,0:T(8,128)(2,1)S(1)} %add_convert_fusion), channel_id=1, source_target_pairs={{0,16},{8,24},{16,0},{24,8},{1,17},{9,25},{17,1},{25,9},{2,18},{10... | collective-permute-start | bytes 1572872 | tf_op jit(solution)/shard_map/weight_grad/ppermute | solution.py:350
  151.3 13.6 %collective-permute-start.12 = (f32[256,1024]{1,0:T(8,128)S(1)}, f32[256,1024]{1,0:T(8,128)S(1)}, u32[]{:S(2)}, u32[]{:S(2)}) collective-permute-start(f32[256,1024]{1,0:T(8,128)S(1)} %convert_add_fusion), channel_id=1, source_target_pairs={{0,8},{8,0},{16,24},{24,16},{1,9},{9,1},{17,25},{25,17},{2,10},{10... | collective-permute-start | bytes 3145736 | tf_op jit(solution)/shard_map/weight_grad/ppermute | solution.py:351
  165.2 1.3 copy-start.4

commit v4 on v3

--- a/solution.py
+++ b/solution.py
@@ -11,6 +11,7 @@
 META = 8
 PIECES = 16
 TOP = 14.0
+WAITS = 30_000_000_000
 bf16, f16, f32 = jnp.bfloat16, jnp.float16, jnp.float32
 
 
@@ -38,7 +39,8 @@
     return jnp.clip(jnp.ceil(jnp.log2(jnp.maximum(largest, 1e-30))), -100.0, 100.0)
 
 
-def pack_teacher(place_ref, x_ref, *refs):
+def pack_teacher(place_ref, x_ref, after_ref, *refs):
+    del after_ref
     held = refs[4]
     rows = x_ref[...].astype(f32)
     largest = jnp.max(jnp.max(jnp.abs(rows).reshape(8, 8, -1), axis=0), axis=1, keepdims=True)
@@ -217,34 +219,6 @@
 
     with jax.named_scope("teacher"):
         spread = all_to_all(teacher_hidden.reshape(8, 8, -1), "tensor")
-        group = (jax.ShapeDtypeStruct((64, columns // 2 + LANES), bf16),) * 4
-        packed = call(
-            pack_teacher,
-            group,
-            0,
-            600_000,
-            in_specs=[scalars, whole],
-            out_specs=(whole,) * 4,
-            scratch_shapes=[pltpu.VMEM((4, 64, columns // 2 + LANES), bf16)],
-        )(place, spread.reshape(64, -1))
-        near = [packed[0]]
-        for k in range(1, 4):
-            moves = [(z, (z + (k if k < 3 else -1)) % dp_count) for z in range(dp_count)]
-            near.append(lax.ppermute(packed[k], "dp", moves))
-        packed = call(
-            regroup_teacher,
-            group,
-            0,
-            600_000,
-            in_specs=[scalars] + [whole] * 4,
-            out_specs=(whole,) * 4,
-        )(place, *near)
-        target = [packed[0]]
-        for m in range(1, 4):
-            moves = [(z, (z + 4 * m) % dp_count) for z in range(dp_count)]
-            target.append(lax.ppermute(packed[m], "dp", moves))
-
-    with jax.named_scope("prediction"):
         size = blocks * own + META
         partial = call(
             forward,
@@ -258,7 +232,41 @@
             ],
             out_specs=pl.BlockSpec((2, size, LANES), lambda i: (i, 0, 0)),
         )(student, proj_weight)
-        parts = all_to_all(partial.astype(f16), "tensor").astype(f32)
+        partial = partial.astype(f16)
+        group = (jax.ShapeDtypeStruct((64, columns // 2 + LANES), bf16),) * 4
+        packed = call(
+            pack_teacher,
+            group,
+            0,
+            600_000,
+            grid=(1,),
+            in_specs=[
+                scalars,
+                pl.BlockSpec((64, 2 * columns), lambda i: (0, 0)),
+                pl.BlockSpec((META, LANES), lambda i: (0, 0)),
+            ],
+            out_specs=(pl.BlockSpec(group[0].shape, lambda i: (0, 0)),) * 4,
+            scratch_shapes=[pltpu.VMEM((4, 64, columns // 2 + LANES), bf16)],
+        )(place, spread.reshape(64, -1), partial[0, :META, :].astype(f32))
+        near = [packed[0]]
+        for k in range(1, 4):
+            moves = [(z, (z + (k if k < 3 else -1)) % dp_count) for z in range(dp_count)]
+            near.append(lax.ppermute(packed[k], "dp", moves))
+        packed = call(
+            regroup_teacher,
+            group,
+            WAITS,
+            600_000,
+            in_specs=[scalars] + [whole] * 4,
+            out_specs=(whole,) * 4,
+        )(place, *near)
+        target = [packed[0]]
+        for m in range(1, 4):
+            moves = [(z, (z + 4 * m) % dp_count) for z in range(dp_count)]
+            target.append(lax.ppermute(packed[m], "dp", moves))
+
+    with jax.named_scope("prediction"):
+        parts = all_to_all(partial, "tensor").astype(f32)
         unscale = jnp.exp2(parts[:, blocks * own, :] - TOP)
         data = parts[:, : blocks * own, :].reshape(tensor_count, blocks, own, LANES)
         prediction = jnp.sum(data * unscale[:, None, :, None], axis=0)

time: 169 us -> 167 us (0.988)
  waiting for transfers between devices: 41.3 us -> 38.2 us
    ppermute x3, waiting for transfers between devices: 4.4 us -> 0.01 us  [body(): near.append(lax.ppermute(packed[k], 'dp', moves))]
    all_to_all x3, waiting for transfers between devices: 0.01 us -> 2.54 us  [all_to_all(): return lax.all_to_all(x, axis, 0, 0)]
    all_to_all x1, starting transfers between devices: 10.6 us -> 8.29 us  [body(): lax.all_to_all(term.astype(f16), 'dp', 0, 0, axis_index_groups=same_parity)]
  transfers between devices with their start and end apart: 17 -> 17, of which waited for: 8 -> 7; matrix products, arithmetic and copies ran while one was open for 4% -> 5% of each run, Pallas kernels for 3% -> 2%
where the time goes in v4:
time: 167 us; the launch traced here: 165 us
  starting transfers between devices  84.3 us (50%)
  waiting for transfers between devices  38.2 us (23%)
  blocking collectives  16.1 us (10%)
  Pallas kernels  11.6 us (7%)
  other arithmetic  7.95 us (5%)
  local copies, waits for them, and re-layouts  5.15 us (3%)
  between operations  2.1 us (1%)
    ppermute x3, starting transfers between devices, body(): target.append(lax.ppermute(packed[m], 'dp', moves))  21.7 us
    all_to_all x3, starting transfers between devices, all_to_all(): return lax.all_to_all(x, axis, 0, 0)  16.4 us
    all_to_all x1, blocking collectives, all_to_all(): return lax.all_to_all(x, axis, 0, 0)  16.1 us
    ppermute x1, waiting for transfers between devices, body(): mine = pair.astype(f32) + lax.ppermute(pair, 'seq', other_y).astype(f32)  12.6 us
    ppermute x3, starting transfers between devices, body(): near.append(lax.ppermute(packed[k], 'dp', moves))  12.1 us
    all_to_all x1, waiting for transfers between devices, body(): lax.all_to_all(term.astype(f16), 'dp', 0, 0, axis_index_groups=same_parity)  11.5 us
    ppermute x3, starting transfers between devices, butterfly(): lax.ppermute(x, axis, [(i, i ^ step) for i in range(lax.axis_size(axis))])  8.63 us
    ppermute x1, starting transfers between devices, body(): got = lax.ppermute(send.astype(f16), 'dp', neighbour).astype(f32)  8.44 us
  transfers between devices with their start and end apart: 17, of which 7 were waited for; matrix products, arithmetic and copies ran while one was open for 5% of the time, Pallas kernels for 2%

profile of v4, /device:TPU:34, one launch (start us, length us, event | category | flops | bytes accessed | tf_op | source)
XLA Modules:
  0.0 165.5 jit_solution(644849561672056351)
XLA Ops:
  0.6 5.9 %all-to-all-start.1 = ((bf16[8,8,2048]{2,1,0:T(8,128)(2,1)}), bf16[8,8,2048]{2,1,0:T(8,128)(2,1)S(1)}, u32[]{:S(2)}, u32[]{:S(2)}) async-start(bf16[8,8,2048]{2,1,0:T(8,128)(2,1)} %bitcast.26), calls=%async_computation.1 | async-start | bytes 524288 | tf_op jit(solution)/shard_map/teacher/all_to_all | solution.py:29
  6.5 0.1 pad_add_fusion.place_ref
  6.6 1.2 copy-done
  7.8 1.2 copy-done.2
  9.0 2.3 %teacher.3 = f32[8,1032,128]{2,1,0:T(8,128)S(1)} custom-call(bf16[1024,512]{1,0:T(8,128)(2,1)S(1)} %bitcast.20, bf16[512,1024]{1,0:T(8,128)(2,1)S(1)} %copy-done), custom_call_target="tpu_custom_call" | custom-call | flops 1073741824 | bytes 6000000 | tf_op jit(solution)/shard_map/teacher/pallas_call | solution.py:223
  11.3 1.6 convert_element_type.32
  12.9 0.7 fusion.3.after_ref
  13.6 0.8 teacher.4
  14.4 3.8 %collective-permute-start = (bf16[64,640]{1,0:T(8,128)(2,1)S(1)}, bf16[64,640]{1,0:T(8,128)(2,1)S(1)}, u32[]{:S(2)}, u32[]{:S(2)}) collective-permute-start(bf16[64,640]{1,0:T(8,128)(2,1)S(1)} %get-tuple-element.20), channel_id=1, source_target_pairs={{0,32},{32,64},{64,96},{96,128},{128,160},{160,192},{192,224},{224... | collective-permute-start | bytes 245768 | tf_op jit(solution)/shard_map/teacher/ppermute | solution.py:254
  18.2 6.4 %collective-permute-start.1 = (bf16[64,640]{1,0:T(8,128)(2,1)S(1)}, bf16[64,640]{1,0:T(8,128)(2,1)S(1)}, u32[]{:S(2)}, u32[]{:S(2)}) collective-permute-start(bf16[64,640]{1,0:T(8,128)(2,1)S(1)} %get-tuple-element.21), channel_id=1, source_target_pairs={{0,64},{32,96},{64,128},{96,160},{128,192},{160,224},{192,256},{22... | collective-permute-start | bytes 245768 | tf_op jit(solution)/shard_map/teacher/ppermute | solution.py:254
  24.6 1.9 %collective-permute-start.2 = (bf16[64,640]{1,0:T(8,128)(2,1)S(1)}, bf16[64,640]{1,0:T(8,128)(2,1)S(1)}, u32[]{:S(2)}, u32[]{:S(2)}) collective-permute-start(bf16[64,640]{1,0:T(8,128)(2,1)S(1)} %get-tuple-element.22), channel_id=1, source_target_pairs={{0,480},{32,0},{64,32},{96,64},{128,96},{160,128},{192,160},{224,1... | collective-permute-start | bytes 245768 | tf_op jit(solution)/shard_map/teacher/ppermute | solution.py:254
  26.5 5.7 %all-to-all-start = ((f16[8,1032,128]{2,1,0:T(8,128)(2,1)}), f16[8,1032,128]{2,1,0:T(8,128)(2,1)S(1)}, u32[]{:S(2)}, u32[]{:S(2)}) async-start(f16[8,1032,128]{2,1,0:T(8,128)(2,1)} %convert_element_type.32), calls=%async_computation | async-start | bytes 4227072 | tf_op jit(solution)/shard_map/prediction/all_to_all | solution.py:29
  32.3 0.6 teacher.5
  32.9 9.1 %collective-permute-start.3 = (bf16[64,640]{1,0:T(8,128)(2,1)S(1)}, bf16[64,640]{1,0:T(8,128)(2,1)S(1)}, u32[]{:S(2)}, u32[]{:S(2)}) collective-permute-start(bf16[64,640]{1,0:T(8,128)(2,1)S(1)} %get-tuple-element.24), channel_id=1, source_target_pairs={{0,128},{32,160},{64,192},{96,224},{128,256},{160,288},{192,320},{... | collective-permute-start | bytes 245768 | tf_op jit(solution)/shard_map/teacher/ppermute | solution.py:266
  42.0 7.1 %collective-permute-start.4 = (bf16[64,640]{1,0:T(8,128)(2,1)S(1)}, bf16[64,640]{1,0:T(8,128)(2,1)S(1)}, u32[]{:S(2)}, u32[]{:S(2)}) collective-permute-start(bf16[64,640]{1,0:T(8,128)(2,1)S(1)} %get-tuple-element.25), channel_id=1, source_target_pairs={{0,256},{32,288},{64,320},{96,352},{128,384},{160,416},{192,448},{... | collective-permute-start | bytes 245768 | tf_op jit(solution)/shard_map/teacher/ppermute | solution.py:266
  49.1 5.5 %collective-permute-start.5 = (bf16[64,640]{1,0:T(8,128)(2,1)S(1)}, bf16[64,640]{1,0:T(8,128)(2,1)S(1)}, u32[]{:S(2)}, u32[]{:S(2)}) collective-permute-start(bf16[64,640]{1,0:T(8,128)(2,1)S(1)} %get-tuple-element.26), channel_id=1, source_target_pairs={{0,384},{32,416},{64,448},{96,480},{128,0},{160,32},{192,64},{224,... | collective-permute-start | bytes 245768 | tf_op jit(solution)/shard_map/teacher/ppermute | solution.py:266
  54.5 2.5 %all-to-all-done = f16[8,1032,128]{2,1,0:T(8,128)(2,1)S(1)} async-done(((f16[8,1032,128]{2,1,0:T(8,128)(2,1)}), f16[8,1032,128]{2,1,0:T(8,128)(2,1)S(1)}, u32[]{:S(2)}, u32[]{:S(2)}) %all-to-all-start) | async-done | bytes 2113568 | tf_op jit(solution)/shard_map/prediction/all_to_all | solution.py:29
  57.1 0.3 convert_element_type.33
  57.4 1.4 fusion
  58.8 4.8 %collective-permute-done.4.t2_ref = bf16[64,640]{1,0:T(8,128)(2,1)S(1)} collective-permute-done((bf16[64,640]{1,0:T(8,128)(2,1)S(1)}, bf16[64,640]{1,0:T(8,128)(2,1)S(1)}, u32[]{:S(2)}, u32[]{:S(2)}) %collective-permute-start.4) | collective-permute-done | bytes 81952 | tf_op jit(solution)/shard_map/teacher/ppermute | solution.py:266
  63.6 1.4 gradient.1
  65.1 16.1 %all_to_all.25.g_ref.loss_ref = bf16[8,528,128]{2,1,0:T(8,128)(2,1)S(1)} all-to-all(bf16[8,528,128]{2,1,0:T(8,128)(2,1)S(1)} %get-tuple-element.28), channel_id=1, replica_groups=mesh['dp'=16,'seq'=4,'tensor'=8] {'tensor'}, dimensions={0} | all-to-all | bytes 2162688 | tf_op jit(solution)/shard_map/gradient/all_to_all | solution.py:29
  81.2 4.8 %all-to-all-start.2 = ((bf16[8,512,128]{2,1,0:T(8,128)(2,1)}), bf16[8,512,128]{2,1,0:T(8,128)(2,1)S(1)}, u32[]{:S(2)}, u32[]{:S(2)}) async-start(bf16[8,512,128]{2,1,0:T(8,128)(2,1)} %copy-done.6), calls=%async_computation.2 | async-start | bytes 2097152 | tf_op jit(solution)/shard_map/gradient/all_to_all | solution.py:29
  86.0 1.2 input_grad.2
  87.3 8.4 %collective-permute-start.6 = (f16[8,264,128]{2,1,0:T(8,128)(2,1)S(1)}, f16[8,264,128]{2,1,0:T(8,128)(2,1)S(1)}, u32[]{:S(2)}, u32[]{:S(2)}) collective-permute-start(f16[8,264,128]{2,1,0:T(8,128)(2,1)S(1)} %convert_element_type.36), channel_id=1, source_target_pairs={{0,32},{32,0},{64,96},{96,64},{128,160},{160,128},{192,224},{224,1... | collective-permute-start | bytes 1622024 | tf_op jit(solution)/shard_map/input_grad/ppermute | solution.py:317
  95.8 1.9 %collective-permute-start.7 = (f32[1,128]{1,0:T(1,128)S(1)}, f32[1,128]{1,0:T(1,128)S(1)}, u32[]{:S(2)}, u32[]{:S(2)}) collective-permute-start(f32[1,128]{1,0:T(1,128)S(1)} %get-tuple-element.30), channel_id=1, source_target_pairs={{0,8},{8,0},{16,24},{24,16},{1,9},{9,1},{17,25},{25,17},{2,10},{10... | collective-permute-start | bytes 1544 | tf_op jit(solution)/shard_map/input_grad/ppermute | solution.py:34
  97.7 1.1 collective-permute-done.7
  98.8 4.8 %collective-permute-start.8 = (f32[1,128]{1,0:T(1,128)S(1)}, f32[1,128]{1,0:T(1,128)S(1)}, u32[]{:S(2)}, u32[]{:S(2)}) collective-permute-start(f32[1,128]{1,0:T(1,128)S(1)} %add.35), channel_id=1, source_target_pairs={{0,16},{8,24},{16,0},{24,8},{1,17},{9,25},{17,1},{25,9},{2,18},{10... | collective-permute-start | bytes 1544 | tf_op jit(solution)/shard_map/input_grad/ppermute | solution.py:34
  103.6 2.1 %collective-permute-done.8 = f32[1,128]{1,0:T(1,128)S(1)} collective-permute-done((f32[1,128]{1,0:T(1,128)S(1)}, f32[1,128]{1,0:T(1,128)S(1)}, u32[]{:S(2)}, u32[]{:S(2)}) %collective-permute-start.8) | collective-permute-done | bytes 544 | tf_op jit(solution)/shard_map/input_grad/ppermute | solution.py:34
  105.7 1.9 %collective-permute-start.9 = (f32[1,128]{1,0:T(1,128)S(1)}, f32[1,128]{1,0:T(1,128)S(1)}, u32[]{:S(2)}, u32[]{:S(2)}) collective-permute-start(f32[1,128]{1,0:T(1,128)S(1)} %add.36), channel_id=1, source_target_pairs={{0,32},{32,0},{64,96},{96,64},{128,160},{160,128},{192,224},{224,1... | collective-permute-start | bytes 1544 | tf_op jit(solution)/shard_map/input_grad/ppermute | solution.py:34
  107.7 3.5 %collective-permute-done.9 = f32[1,128]{1,0:T(1,128)S(1)} collective-permute-done((f32[1,128]{1,0:T(1,128)S(1)}, f32[1,128]{1,0:T(1,128)S(1)}, u32[]{:S(2)}, u32[]{:S(2)}) %collective-permute-start.9) | collective-permute-done | bytes 544 | tf_op jit(solution)/shard_map/input_grad/ppermute | solution.py:34
  111.2 1.1 convert_element_type.37.got_ref
  112.2 1.2 copy-done.5
  113.5 1.2 input_grad.3.after_ref
  114.7 3.3 %weight_grad.1 = (f32[256,1024]{1,0:T(8,128)S(1)}, f32[256,1024]{1,0:T(8,128)S(1)}) custom-call(s32[4]{0:T(128)S(1)} %pad_add_fusion.place_ref, bf16[8,2,64,512]{3,2,1,0:T(8,128)(2,1)S(1)} %bitcast.21, bf16[8,2,64,512]{3,2,1,0:T(8,128)(2,1)S(1)} %bitcast.22, bf16[8,528,128]{2,1,0:T(8,128)(2,1)S(1)} %all_to_all.25.g_ref.loss_ref, ...), custom_call_target="tpu_custom_call" | custom-call | flops 1073741824 | bytes 5000000 | tf_op jit(solution)/shard_map/weight_grad/pallas_call | solution.py:335
  118.0 1.0 copy-done.7
  119.0 2.0 %collective-permute-start.10 = (f32[256,1024]{1,0:T(8,128)S(1)}, f32[256,1024]{1,0:T(8,128)}, u32[]{:S(2)}, u32[]{:S(2)}) collective-permute-start(f32[256,1024]{1,0:T(8,128)S(1)} %get-tuple-element.32), channel_id=1, source_target_pairs={{0,8},{8,0},{16,24},{24,16},{1,9},{9,1},{17,25},{25,17},{2,10},{10... | collective-permute-start | bytes 3145736 | tf_op jit(solution)/shard_map/weight_grad/ppermute | solution.py:357
  121.0 0.9 convert_element_type.38
  121.9 8.3 %all-to-all-start.4 = ((f16[8,264,128]{2,1,0:T(8,128)(2,1)}), f16[8,264,128]{2,1,0:T(8,128)(2,1)S(1)}, u32[]{:S(2)}, u32[]{:S(2)}) async-start(f16[8,264,128]{2,1,0:T(8,128)(2,1)} %convert_element_type.38), calls=%async_computation.4 | async-start | bytes 1081344 | tf_op jit(solution)/shard_map/input_grad/all_to_all | solution.py:328
  130.2 1.4 add_convert_fusion
  131.6 4.8 %collective-permute-start.11 = (bf16[256,1024]{1,0:T(8,128)(2,1)S(1)}, bf16[256,1024]{1,0:T(8,128)(2,1)S(1)}, u32[]{:S(2)}, u32[]{:S(2)}) collective-permute-start(bf16[256,1024]{1,0:T(8,128)(2,1)S(1)} %add_convert_fusion), channel_id=1, source_target_pairs={{0,16},{8,24},{16,0},{24,8},{1,17},{9,25},{17,1},{25,9},{2,18},{10... | collective-permute-start | bytes 1572872 | tf_op jit(solution)/shard_map/weight_grad/ppermute | solution.py:358
  136.4 12.6 %collective-permute-done.11 = bf16[256,1024]{1,0:T(8,128)(2,1)S(1)} collective-permute-done((bf16[256,1024]{1,0:T(8,128)(2,1)S(1)}, bf16[256,1024]{1,0:T(8,128)(2,1)S(1)}, u32[]{:S(2)}, u32[]{:S(2)}) %collective-permute-start.11) | collective-permute-done | bytes 524320 | tf_op jit(solution)/shard_map/weight_grad/ppermute | solution.py:358
  149.0 0.2 convert_add_fusion
  149.2 1.9 %collective-permute-start.12 = (f32[256,1024]{1,0:T(8,128)S(1)}, f32[256,1024]{1,0:T(8,128)S(1)}, u32[]{:S(2)}, u32[]{:S(2)}) collective-permute-start(f32[256,1024]{1,0:T(8,128)S(1)} %convert_add_fusion), channel_id=1, source_target_pairs={{0,8},{8,0},{16,24},{24,16},{1,9},{9,1},{17,25},{25,17},{2,10},{10... | collective-permute-start | bytes 3145736 | tf_op jit(solution)/shard_map/weight_grad/ppermute | solution.py:359
  151.1 11.5 %all-to-all-done.4 = f16[8,264,128]{2,1,0:T(8,128)(2,1)S(1)} async-done(((f16[8,264,128]{2,1,0:T(8,128)(2,1)}), f16[8,264,128]{2,1,0:T(8,128)(2,1)S(1)}, u32[]{:S(2)}, u32[]{:S(2)}) %all-to-all-start.4) | async-done | bytes 540704 | tf_op jit(solution)/shard_map/input_grad/all_to_all | solution.py:328
  162.7 0.3 maximum_select_fusion.after_ref
  163.0 0.8 results.1
  163.9 0.5 copy-done.4
  (30 shorter events, 0.2 us)
Async XLA Ops:
  0.6 13.0 %all-to-all-start.1 = ((bf16[8,8,2048]{2,1,0:T(8,128)(2,1)}), bf16[8,8,2048]{2,1,0:T(8,128)(2,1)S(1)}, u32[]{:S(2)}, u32[]{:S(2)}) async-start(bf16[8,8,2048]{2,1,0:T(8,128)(2,1)} %bitcast.26), calls=%async_computation.1 | async-start | bytes 524288 | tf_op jit(solution)/shard_map/teacher/all_to_all | solution.py:29
  6.6 1.2 copy-start
  7.8 1.2 copy-start.2
  14.4 17.9 %collective-permute-start = (bf16[64,640]{1,0:T(8,128)(2,1)S(1)}, bf16[64,640]{1,0:T(8,128)(2,1)S(1)}, u32[]{:S(2)}, u32[]{:S(2)}) collective-permute-start(bf16[64,640]{1,0:T(8,128)(2,1)S(1)} %get-tuple-element.20), channel_id=1, source_target_pairs={{0,32},{32,64},{64,96},{96,128},{128,160},{160,192},{192,224},{224... | collective-permute-start | bytes 245768 | tf_op jit(solution)/shard_map/teacher/ppermute | solution.py:254
  18.2 14.0 %collective-permute-start.1 = (bf16[64,640]{1,0:T(8,128)(2,1)S(1)}, bf16[64,640]{1,0:T(8,128)(2,1)S(1)}, u32[]{:S(2)}, u32[]{:S(2)}) collective-permute-start(bf16[64,640]{1,0:T(8,128)(2,1)S(1)} %get-tuple-element.21), channel_id=1, source_target_pairs={{0,64},{32,96},{64,128},{96,160},{128,192},{160,224},{192,256},{22... | collective-permute-start | bytes 245768 | tf_op jit(solution)/shard_map/teacher/ppermute | solution.py:254
  24.6 7.7 %collective-permute-start.2 = (bf16[64,640]{1,0:T(8,128)(2,1)S(1)}, bf16[64,640]{1,0:T(8,128)(2,1)S(1)}, u32[]{:S(2)}, u32[]{:S(2)}) collective-permute-start(bf16[64,640]{1,0:T(8,128)(2,1)S(1)} %get-tuple-element.22), channel_id=1, source_target_pairs={{0,480},{32,0},{64,32},{96,64},{128,96},{160,128},{192,160},{224,1... | collective-permute-start | bytes 245768 | tf_op jit(solution)/shard_map/teacher/ppermute | solution.py:254
  26.5 30.5 %all-to-all-start = ((f16[8,1032,128]{2,1,0:T(8,128)(2,1)}), f16[8,1032,128]{2,1,0:T(8,128)(2,1)S(1)}, u32[]{:S(2)}, u32[]{:S(2)}) async-start(f16[8,1032,128]{2,1,0:T(8,128)(2,1)} %convert_element_type.32), calls=%async_computation | async-start | bytes 4227072 | tf_op jit(solution)/shard_map/prediction/all_to_all | solution.py:29
  32.9 25.9 %collective-permute-start.3 = (bf16[64,640]{1,0:T(8,128)(2,1)S(1)}, bf16[64,640]{1,0:T(8,128)(2,1)S(1)}, u32[]{:S(2)}, u32[]{:S(2)}) collective-permute-start(bf16[64,640]{1,0:T(8,128)(2,1)S(1)} %get-tuple-element.24), channel_id=1, source_target_pairs={{0,128},{32,160},{64,192},{96,224},{128,256},{160,288},{192,320},{... | collective-permute-start | bytes 245768 | tf_op jit(solution)/shard_map/teacher/ppermute | solution.py:266
  42.0 21.7 %collective-permute-start.4 = (bf16[64,640]{1,0:T(8,128)(2,1)S(1)}, bf16[64,640]{1,0:T(8,128)(2,1)S(1)}, u32[]{:S(2)}, u32[]{:S(2)}) collective-permute-start(bf16[64,640]{1,0:T(8,128)(2,1)S(1)} %get-tuple-element.25), channel_id=1, source_target_pairs={{0,256},{32,288},{64,320},{96,352},{128,384},{160,416},{192,448},{... | collective-permute-start | bytes 245768 | tf_op jit(solution)/shard_map/teacher/ppermute | solution.py:266
  49.1 14.5 %collective-permute-start.5 = (bf16[64,640]{1,0:T(8,128)(2,1)S(1)}, bf16[64,640]{1,0:T(8,128)(2,1)S(1)}, u32[]{:S(2)}, u32[]{:S(2)}) collective-permute-start(bf16[64,640]{1,0:T(8,128)(2,1)S(1)} %get-tuple-element.26), channel_id=1, source_target_pairs={{0,384},{32,416},{64,448},{96,480},{128,0},{160,32},{192,64},{224,... | collective-permute-start | bytes 245768 | tf_op jit(solution)/shard_map/teacher/ppermute | solution.py:266
  65.0 16.2 %copy-start.6 = (bf16[8,512,128]{2,1,0:T(8,128)(2,1)}, bf16[8,512,128]{2,1,0:T(8,128)(2,1)S(1)}, u32[]{:S(2)}) copy-start(bf16[8,512,128]{2,1,0:T(8,128)(2,1)S(1)} %get-tuple-element.27) | copy-start | bytes 3145732
  65.0 21.0 %copy-start.1 = (bf16[512,1024]{1,0:T(8,128)(2,1)S(1)}, bf16[512,1024]{1,0:T(8,128)(2,1)}, u32[]{:S(2)}) copy-start(bf16[512,1024]{1,0:T(8,128)(2,1)} %w_ref.5) | copy-start | bytes 3145732
  81.2 31.0 %all-to-all-start.2 = ((bf16[8,512,128]{2,1,0:T(8,128)(2,1)}), bf16[8,512,128]{2,1,0:T(8,128)(2,1)S(1)}, u32[]{:S(2)}, u32[]{:S(2)}) async-start(bf16[8,512,128]{2,1,0:T(8,128)(2,1)} %copy-done.6), calls=%async_computation.2 | async-start | bytes 2097152 | tf_op jit(solution)/shard_map/gradient/all_to_all | solution.py:29
  87.3 23.8 %collective-permute-start.6 = (f16[8,264,128]{2,1,0:T(8,128)(2,1)S(1)}, f16[8,264,128]{2,1,0:T(8,128)(2,1)S(1)}, u32[]{:S(2)}, u32[]{:S(2)}) collective-permute-start(f16[8,264,128]{2,1,0:T(8,128)(2,1)S(1)} %convert_element_type.36), channel_id=1, source_target_pairs={{0,32},{32,0},{64,96},{96,64},{128,160},{160,128},{192,224},{224,1... | collective-permute-start | bytes 1622024 | tf_op jit(solution)/shard_map/input_grad/ppermute | solution.py:317
  95.8 3.0 %collective-permute-start.7 = (f32[1,128]{1,0:T(1,128)S(1)}, f32[1,128]{1,0:T(1,128)S(1)}, u32[]{:S(2)}, u32[]{:S(2)}) collective-permute-start(f32[1,128]{1,0:T(1,128)S(1)} %get-tuple-element.30), channel_id=1, source_target_pairs={{0,8},{8,0},{16,24},{24,16},{1,9},{9,1},{17,25},{25,17},{2,10},{10... | collective-permute-start | bytes 1544 | tf_op jit(solution)/shard_map/input_grad/ppermute | solution.py:34
  98.8 6.9 %collective-permute-start.8 = (f32[1,128]{1,0:T(1,128)S(1)}, f32[1,128]{1,0:T(1,128)S(1)}, u32[]{:S(2)}, u32[]{:S(2)}) collective-permute-start(f32[1,128]{1,0:T(1,128)S(1)} %add.35), channel_id=1, source_target_pairs={{0,16},{8,24},{16,0},{24,8},{1,17},{9,25},{17,1},{25,9},{2,18},{10... | collective-permute-start | bytes 1544 | tf_op jit(solution)/shard_map/input_grad/ppermute | solution.py:34
  105.7 5.4 %collective-permute-start.9 = (f32[1,128]{1,0:T(1,128)S(1)}, f32[1,128]{1,0:T(1,128)S(1)}, u32[]{:S(2)}, u32[]{:S(2)}) collective-permute-start(f32[1,128]{1,0:T(1,128)S(1)} %add.36), channel_id=1, source_target_pairs={{0,32},{32,0},{64,96},{96,64},{128,160},{160,128},{192,224},{224,1... | collective-permute-start | bytes 1544 | tf_op jit(solution)/shard_map/input_grad/ppermute | solution.py:34
  112.2 1.2 copy-start.5
  113.5 1.2 copy-start.3
  118.0 1.0 copy-start.7
  119.0 11.2 %copy-start.8 = (f32[256,1024]{1,0:T(8,128)S(1)}, f32[256,1024]{1,0:T(8,128)}, u32[]{:S(2)}) copy-start(f32[256,1024]{1,0:T(8,128)} %copy-done.7) | copy-start | bytes 3145732
  119.0 11.2 %collective-permute-start.10 = (f32[256,1024]{1,0:T(8,128)S(1)}, f32[256,1024]{1,0:T(8,128)}, u32[]{:S(2)}, u32[]{:S(2)}) collective-permute-start(f32[256,1024]{1,0:T(8,128)S(1)} %get-tuple-element.32), channel_id=1, source_target_pairs={{0,8},{8,0},{16,24},{24,16},{1,9},{9,1},{17,25},{25,17},{2,10},{10... | collective-permute-start | bytes 3145736 | tf_op jit(solution)/shard_map/weight_grad/ppermute | solution.py:357
  121.9 40.7 %all-to-all-start.4 = ((f16[8,264,128]{2,1,0:T(8,128)(2,1)}), f16[8,264,128]{2,1,0:T(8,128)(2,1)S(1)}, u32[]{:S(2)}, u32[]{:S(2)}) async-start(f16[8,264,128]{2,1,0:T(8,128)(2,1)} %convert_element_type.38), calls=%async_computation.4 | async-start | bytes 1081344 | tf_op jit(solution)/shard_map/input_grad/all_to_all | solution.py:328
  131.6 17.4 %collective-permute-start.11 = (bf16[256,1024]{1,0:T(8,128)(2,1)S(1)}, bf16[256,1024]{1,0:T(8,128)(2,1)S(1)}, u32[]{:S(2)}, u32[]{:S(2)}) collective-permute-start(bf16[256,1024]{1,0:T(8,128)(2,1)S(1)} %add_convert_fusion), channel_id=1, source_target_pairs={{0,16},{8,24},{16,0},{24,8},{1,17},{9,25},{17,1},{25,9},{2,18},{10... | collective-permute-start | bytes 1572872 | tf_op jit(solution)/shard_map/weight_grad/ppermute | solution.py:358
  149.2 13.5 %collective-permute-start.12 = (f32[256,1024]{1,0:T(8,128)S(1)}, f32[256,1024]{1,0:T(8,128)S(1)}, u32[]{:S(2)}, u32[]{:S(2)}) collective-permute-start(f32[256,1024]{1,0:T(8,128)S(1)} %convert_add_fusion), channel_id=1, source_target_pairs={{0,8},{8,0},{16,24},{24,16},{1,9},{9,1},{17,25},{25,17},{2,10},{10... | collective-permute-start | bytes 3145736 | tf_op jit(solution)/shard_map/weight_grad/ppermute | solution.py:359
  163.0 1.3 copy-start.4

commit v5 on v4

--- a/solution.py
+++ b/solution.py
@@ -64,7 +64,8 @@
             refs[4 + m][16 * k : 16 * k + 16, :] = refs[k][pl.ds(pl.multiple_of(16 * high, 16), 16), :]
 
 
-def forward(s_ref, w_ref, o_ref):
+def forward(s_ref, w_ref, o_ref, done_ref):
+    done_ref[...] = jnp.zeros_like(done_ref)
     partial = jnp.dot(s_ref[...], w_ref[...], preferred_element_type=f32)
     power = exponent_of(jnp.max(jnp.abs(partial), axis=1, keepdims=True))
     scaled = partial * jnp.exp2(TOP - power)
@@ -220,9 +221,12 @@
     with jax.named_scope("teacher"):
         spread = all_to_all(teacher_hidden.reshape(8, 8, -1), "tensor")
         size = blocks * own + META
-        partial = call(
+        partial, done = call(
             forward,
-            jax.ShapeDtypeStruct((tensor_count, size, LANES), f32),
+            (
+                jax.ShapeDtypeStruct((tensor_count, size, LANES), f32),
+                jax.ShapeDtypeStruct((META, LANES), f32),
+            ),
             2 * tokens * width_local * columns,
             6_000_000,
             grid=(tensor_count // 2,),
@@ -230,9 +234,12 @@
                 pl.BlockSpec((2 * own, width_local), lambda i: (i, 0)),
                 pl.BlockSpec((width_local, columns), lambda i: (0, 0)),
             ],
-            out_specs=pl.BlockSpec((2, size, LANES), lambda i: (i, 0, 0)),
+            out_specs=(
+                pl.BlockSpec((2, size, LANES), lambda i: (i, 0, 0)),
+                pl.BlockSpec((META, LANES), lambda i: (0, 0)),
+            ),
         )(student, proj_weight)
-        partial = partial.astype(f16)
+        partial, done = lax.optimization_barrier((partial.astype(f16), done))
         group = (jax.ShapeDtypeStruct((64, columns // 2 + LANES), bf16),) * 4
         packed = call(
             pack_teacher,
@@ -247,7 +254,7 @@
             ],
             out_specs=(pl.BlockSpec(group[0].shape, lambda i: (0, 0)),) * 4,
             scratch_shapes=[pltpu.VMEM((4, 64, columns // 2 + LANES), bf16)],
-        )(place, spread.reshape(64, -1), partial[0, :META, :].astype(f32))
+        )(place, spread.reshape(64, -1), done)
         near = [packed[0]]
         for k in range(1, 4):
             moves = [(z, (z + (k if k < 3 else -1)) % dp_count) for z in range(dp_count)]
@@ -314,7 +321,8 @@
         )(grad_a, proj_weight, grad_a)
         neighbour = [(z, z ^ 1) for z in range(dp_count)]
         loss = butterfly(total, (("seq", 1), ("seq", 2), ("dp", 1)))
-        got = lax.ppermute(send.astype(f16), "dp", neighbour).astype(f32)
+        got = lax.ppermute(send.astype(f16), "dp", neighbour)
+        got = lax.optimization_barrier((got, grad_b))[0].astype(f32)
         term = call(
             keep_terms,
             half_terms,

time: 167 us -> 165 us (0.988)
    unnamed x18 -> x16, local copies, waits for them, and re-layouts: 5.14 us -> 3.9 us
    convert_element_type x4 -> x3, other arithmetic: 3.43 us -> 3.62 us  [the longest x1 1.63 us: body(): partial, done = lax.optimization_barrier((partial.astype(f16), done))]
  transfers between devices with their start and end apart: 17 -> 17, of which waited for: 7 -> 7; matrix products, arithmetic and copies ran while one was open for 5% -> 4% of each run, Pallas kernels for 2% -> 2%
where the time goes in v5:
time: 165 us; the launch traced here: 164 us
  starting transfers between devices  84.4 us (51%)
  waiting for transfers between devices  38.1 us (23%)
  blocking collectives  16.1 us (10%)
  Pallas kernels  11.6 us (7%)
  other arithmetic  8.14 us (5%)
  local copies, waits for them, and re-layouts  3.91 us (2%)
  between operations  2.12 us (1%)
    ppermute x3, starting transfers between devices, body(): target.append(lax.ppermute(packed[m], 'dp', moves))  21.7 us
    all_to_all x3, starting transfers between devices, all_to_all(): return lax.all_to_all(x, axis, 0, 0)  16.4 us
    all_to_all x1, blocking collectives, all_to_all(): return lax.all_to_all(x, axis, 0, 0)  16.1 us
    ppermute x1, waiting for transfers between devices, body(): mine = pair.astype(f32) + lax.ppermute(pair, 'seq', other_y).astype(f32)  12.6 us
    ppermute x3, starting transfers between devices, body(): near.append(lax.ppermute(packed[k], 'dp', moves))  12.1 us
    all_to_all x1, waiting for transfers between devices, body(): lax.all_to_all(term.astype(f16), 'dp', 0, 0, axis_index_groups=same_parity)  11.5 us
    ppermute x3, starting transfers between devices, butterfly(): lax.ppermute(x, axis, [(i, i ^ step) for i in range(lax.axis_size(axis))])  8.69 us
    ppermute x1, starting transfers between devices, body(): got = lax.ppermute(send.astype(f16), 'dp', neighbour)  8.43 us
  transfers between devices with their start and end apart: 17, of which 7 were waited for; matrix products, arithmetic and copies ran while one was open for 4% of the time, Pallas kernels for 2%

profile of v5, /device:TPU:34, one launch (start us, length us, event | category | flops | bytes accessed | tf_op | source)
XLA Modules:
  0.0 164.4 jit_solution(17592520581596916336)
XLA Ops:
  0.6 5.9 %all-to-all-start.1 = ((bf16[8,8,2048]{2,1,0:T(8,128)(2,1)}), bf16[8,8,2048]{2,1,0:T(8,128)(2,1)S(1)}, u32[]{:S(2)}, u32[]{:S(2)}) async-start(bf16[8,8,2048]{2,1,0:T(8,128)(2,1)} %bitcast.21), calls=%async_computation.1 | async-start | bytes 524288 | tf_op jit(solution)/shard_map/teacher/all_to_all | solution.py:29
  6.5 1.2 copy-done.1
  7.7 1.2 copy-done.3
  8.9 2.3 %teacher.3 = (f32[8,1032,128]{2,1,0:T(8,128)S(1)}, f32[8,128]{1,0:T(8,128)S(1)}) custom-call(bf16[1024,512]{1,0:T(8,128)(2,1)S(1)} %bitcast.15, bf16[512,1024]{1,0:T(8,128)(2,1)S(1)} %copy-done.1), custom_call_target="tpu_custom_call" | custom-call | flops 1073741824 | bytes 6000000 | tf_op jit(solution)/shard_map/teacher/pallas_call | solution.py:224
  11.2 1.6 convert_element_type.27
  12.9 0.1 pad_add_fusion.place_ref
  13.0 0.8 teacher.4
  13.7 3.8 %collective-permute-start = (bf16[64,640]{1,0:T(8,128)(2,1)S(1)}, bf16[64,640]{1,0:T(8,128)(2,1)S(1)}, u32[]{:S(2)}, u32[]{:S(2)}) collective-permute-start(bf16[64,640]{1,0:T(8,128)(2,1)S(1)} %get-tuple-element.29), channel_id=1, source_target_pairs={{0,32},{32,64},{64,96},{96,128},{128,160},{160,192},{192,224},{224... | collective-permute-start | bytes 245768 | tf_op jit(solution)/shard_map/teacher/ppermute | solution.py:261
  17.5 6.4 %collective-permute-start.1 = (bf16[64,640]{1,0:T(8,128)(2,1)S(1)}, bf16[64,640]{1,0:T(8,128)(2,1)S(1)}, u32[]{:S(2)}, u32[]{:S(2)}) collective-permute-start(bf16[64,640]{1,0:T(8,128)(2,1)S(1)} %get-tuple-element.30), channel_id=1, source_target_pairs={{0,64},{32,96},{64,128},{96,160},{128,192},{160,224},{192,256},{22... | collective-permute-start | bytes 245768 | tf_op jit(solution)/shard_map/teacher/ppermute | solution.py:261
  23.9 1.9 %collective-permute-start.2 = (bf16[64,640]{1,0:T(8,128)(2,1)S(1)}, bf16[64,640]{1,0:T(8,128)(2,1)S(1)}, u32[]{:S(2)}, u32[]{:S(2)}) collective-permute-start(bf16[64,640]{1,0:T(8,128)(2,1)S(1)} %get-tuple-element.31), channel_id=1, source_target_pairs={{0,480},{32,0},{64,32},{96,64},{128,96},{160,128},{192,160},{224,1... | collective-permute-start | bytes 245768 | tf_op jit(solution)/shard_map/teacher/ppermute | solution.py:261
  25.9 5.7 %all-to-all-start = ((f16[8,1032,128]{2,1,0:T(8,128)(2,1)}), f16[8,1032,128]{2,1,0:T(8,128)(2,1)S(1)}, u32[]{:S(2)}, u32[]{:S(2)}) async-start(f16[8,1032,128]{2,1,0:T(8,128)(2,1)} %convert_element_type.27), calls=%async_computation | async-start | bytes 4227072 | tf_op jit(solution)/shard_map/prediction/all_to_all | solution.py:29
  31.6 0.6 teacher.5
  32.2 9.1 %collective-permute-start.3 = (bf16[64,640]{1,0:T(8,128)(2,1)S(1)}, bf16[64,640]{1,0:T(8,128)(2,1)S(1)}, u32[]{:S(2)}, u32[]{:S(2)}) collective-permute-start(bf16[64,640]{1,0:T(8,128)(2,1)S(1)} %get-tuple-element.33), channel_id=1, source_target_pairs={{0,128},{32,160},{64,192},{96,224},{128,256},{160,288},{192,320},{... | collective-permute-start | bytes 245768 | tf_op jit(solution)/shard_map/teacher/ppermute | solution.py:273
  41.3 7.1 %collective-permute-start.4 = (bf16[64,640]{1,0:T(8,128)(2,1)S(1)}, bf16[64,640]{1,0:T(8,128)(2,1)S(1)}, u32[]{:S(2)}, u32[]{:S(2)}) collective-permute-start(bf16[64,640]{1,0:T(8,128)(2,1)S(1)} %get-tuple-element.34), channel_id=1, source_target_pairs={{0,256},{32,288},{64,320},{96,352},{128,384},{160,416},{192,448},{... | collective-permute-start | bytes 245768 | tf_op jit(solution)/shard_map/teacher/ppermute | solution.py:273
  48.4 5.5 %collective-permute-start.5 = (bf16[64,640]{1,0:T(8,128)(2,1)S(1)}, bf16[64,640]{1,0:T(8,128)(2,1)S(1)}, u32[]{:S(2)}, u32[]{:S(2)}) collective-permute-start(bf16[64,640]{1,0:T(8,128)(2,1)S(1)} %get-tuple-element.35), channel_id=1, source_target_pairs={{0,384},{32,416},{64,448},{96,480},{128,0},{160,32},{192,64},{224,... | collective-permute-start | bytes 245768 | tf_op jit(solution)/shard_map/teacher/ppermute | solution.py:273
  53.9 2.5 %all-to-all-done = f16[8,1032,128]{2,1,0:T(8,128)(2,1)S(1)} async-done(((f16[8,1032,128]{2,1,0:T(8,128)(2,1)}), f16[8,1032,128]{2,1,0:T(8,128)(2,1)S(1)}, u32[]{:S(2)}, u32[]{:S(2)}) %all-to-all-start) | async-done | bytes 2113568 | tf_op jit(solution)/shard_map/prediction/all_to_all | solution.py:29
  56.4 0.3 convert_element_type.28
  56.7 1.4 fusion
  58.1 4.8 %collective-permute-done.4.t2_ref = bf16[64,640]{1,0:T(8,128)(2,1)S(1)} collective-permute-done((bf16[64,640]{1,0:T(8,128)(2,1)S(1)}, bf16[64,640]{1,0:T(8,128)(2,1)S(1)}, u32[]{:S(2)}, u32[]{:S(2)}) %collective-permute-start.4) | collective-permute-done | bytes 81952 | tf_op jit(solution)/shard_map/teacher/ppermute | solution.py:273
  62.9 1.4 gradient.1
  64.4 16.1 %all_to_all.25.g_ref.loss_ref = bf16[8,528,128]{2,1,0:T(8,128)(2,1)S(1)} all-to-all(bf16[8,528,128]{2,1,0:T(8,128)(2,1)S(1)} %get-tuple-element.37), channel_id=1, replica_groups=mesh['dp'=16,'seq'=4,'tensor'=8] {'tensor'}, dimensions={0} | all-to-all | bytes 2162688 | tf_op jit(solution)/shard_map/gradient/all_to_all | solution.py:29
  80.5 4.8 %all-to-all-start.2 = ((bf16[8,512,128]{2,1,0:T(8,128)(2,1)}), bf16[8,512,128]{2,1,0:T(8,128)(2,1)S(1)}, u32[]{:S(2)}, u32[]{:S(2)}) async-start(bf16[8,512,128]{2,1,0:T(8,128)(2,1)} %copy-done.5), calls=%async_computation.2 | async-start | bytes 2097152 | tf_op jit(solution)/shard_map/gradient/all_to_all | solution.py:29
  85.4 1.2 input_grad.2
  86.6 0.9 convert_element_type.29
  87.5 8.4 %collective-permute-start.6 = (f16[8,264,128]{2,1,0:T(8,128)(2,1)}, f16[8,264,128]{2,1,0:T(8,128)(2,1)}, u32[]{:S(2)}, u32[]{:S(2)}) collective-permute-start(f16[8,264,128]{2,1,0:T(8,128)(2,1)} %convert_element_type.29), channel_id=1, source_target_pairs={{0,32},{32,0},{64,96},{96,64},{128,160},{160,128},{192,224},{224,1... | collective-permute-start | bytes 1622024 | tf_op jit(solution)/shard_map/input_grad/ppermute | solution.py:324
  95.9 1.9 %collective-permute-start.7 = (f32[1,128]{1,0:T(1,128)S(1)}, f32[1,128]{1,0:T(1,128)S(1)}, u32[]{:S(2)}, u32[]{:S(2)}) collective-permute-start(f32[1,128]{1,0:T(1,128)S(1)} %get-tuple-element.40), channel_id=1, source_target_pairs={{0,8},{8,0},{16,24},{24,16},{1,9},{9,1},{17,25},{25,17},{2,10},{10... | collective-permute-start | bytes 1544 | tf_op jit(solution)/shard_map/input_grad/ppermute | solution.py:34
  97.8 1.1 collective-permute-done.7
  98.9 4.8 %collective-permute-start.8 = (f32[1,128]{1,0:T(1,128)S(1)}, f32[1,128]{1,0:T(1,128)S(1)}, u32[]{:S(2)}, u32[]{:S(2)}) collective-permute-start(f32[1,128]{1,0:T(1,128)S(1)} %add.35), channel_id=1, source_target_pairs={{0,16},{8,24},{16,0},{24,8},{1,17},{9,25},{17,1},{25,9},{2,18},{10... | collective-permute-start | bytes 1544 | tf_op jit(solution)/shard_map/input_grad/ppermute | solution.py:34
  103.7 2.1 %collective-permute-done.8 = f32[1,128]{1,0:T(1,128)S(1)} collective-permute-done((f32[1,128]{1,0:T(1,128)S(1)}, f32[1,128]{1,0:T(1,128)S(1)}, u32[]{:S(2)}, u32[]{:S(2)}) %collective-permute-start.8) | collective-permute-done | bytes 544 | tf_op jit(solution)/shard_map/input_grad/ppermute | solution.py:34
  105.8 2.0 %collective-permute-start.9 = (f32[1,128]{1,0:T(1,128)S(1)}, f32[1,128]{1,0:T(1,128)S(1)}, u32[]{:S(2)}, u32[]{:S(2)}) collective-permute-start(f32[1,128]{1,0:T(1,128)S(1)} %add.36), channel_id=1, source_target_pairs={{0,32},{32,0},{64,96},{96,64},{128,160},{160,128},{192,224},{224,1... | collective-permute-start | bytes 1544 | tf_op jit(solution)/shard_map/input_grad/ppermute | solution.py:34
  107.8 3.4 %collective-permute-done.9 = f32[1,128]{1,0:T(1,128)S(1)} collective-permute-done((f32[1,128]{1,0:T(1,128)S(1)}, f32[1,128]{1,0:T(1,128)S(1)}, u32[]{:S(2)}, u32[]{:S(2)}) %collective-permute-start.9) | collective-permute-done | bytes 544 | tf_op jit(solution)/shard_map/input_grad/ppermute | solution.py:34
  111.3 1.1 convert_element_type.30.got_ref
  112.4 1.2 input_grad.3.after_ref
  113.7 3.3 %weight_grad.1 = (f32[256,1024]{1,0:T(8,128)S(1)}, f32[256,1024]{1,0:T(8,128)S(1)}) custom-call(s32[4]{0:T(128)S(1)} %pad_add_fusion.place_ref, bf16[8,2,64,512]{3,2,1,0:T(8,128)(2,1)S(1)} %bitcast.16, bf16[8,2,64,512]{3,2,1,0:T(8,128)(2,1)S(1)} %bitcast.17, bf16[8,528,128]{2,1,0:T(8,128)(2,1)S(1)} %all_to_all.25.g_ref.loss_ref, ...), custom_call_target="tpu_custom_call" | custom-call | flops 1073741824 | bytes 5000000 | tf_op jit(solution)/shard_map/weight_grad/pallas_call | solution.py:343
  117.0 1.0 copy-done.6
  117.9 2.0 %collective-permute-start.10 = (f32[256,1024]{1,0:T(8,128)S(1)}, f32[256,1024]{1,0:T(8,128)}, u32[]{:S(2)}, u32[]{:S(2)}) collective-permute-start(f32[256,1024]{1,0:T(8,128)S(1)} %get-tuple-element.42), channel_id=1, source_target_pairs={{0,8},{8,0},{16,24},{24,16},{1,9},{9,1},{17,25},{25,17},{2,10},{10... | collective-permute-start | bytes 3145736 | tf_op jit(solution)/shard_map/weight_grad/ppermute | solution.py:365
  120.0 0.9 convert_element_type.31
  120.9 8.3 %all-to-all-start.4 = ((f16[8,264,128]{2,1,0:T(8,128)(2,1)}), f16[8,264,128]{2,1,0:T(8,128)(2,1)S(1)}, u32[]{:S(2)}, u32[]{:S(2)}) async-start(f16[8,264,128]{2,1,0:T(8,128)(2,1)} %convert_element_type.31), calls=%async_computation.4 | async-start | bytes 1081344 | tf_op jit(solution)/shard_map/input_grad/all_to_all | solution.py:336
  129.2 1.4 add_convert_fusion
  130.5 4.8 %collective-permute-start.11 = (bf16[256,1024]{1,0:T(8,128)(2,1)S(1)}, bf16[256,1024]{1,0:T(8,128)(2,1)S(1)}, u32[]{:S(2)}, u32[]{:S(2)}) collective-permute-start(bf16[256,1024]{1,0:T(8,128)(2,1)S(1)} %add_convert_fusion), channel_id=1, source_target_pairs={{0,16},{8,24},{16,0},{24,8},{1,17},{9,25},{17,1},{25,9},{2,18},{10... | collective-permute-start | bytes 1572872 | tf_op jit(solution)/shard_map/weight_grad/ppermute | solution.py:366
  135.4 12.6 %collective-permute-done.11 = bf16[256,1024]{1,0:T(8,128)(2,1)S(1)} collective-permute-done((bf16[256,1024]{1,0:T(8,128)(2,1)S(1)}, bf16[256,1024]{1,0:T(8,128)(2,1)S(1)}, u32[]{:S(2)}, u32[]{:S(2)}) %collective-permute-start.11) | collective-permute-done | bytes 524320 | tf_op jit(solution)/shard_map/weight_grad/ppermute | solution.py:366
  148.0 0.2 convert_add_fusion
  148.2 1.9 %collective-permute-start.12 = (f32[256,1024]{1,0:T(8,128)S(1)}, f32[256,1024]{1,0:T(8,128)S(1)}, u32[]{:S(2)}, u32[]{:S(2)}) collective-permute-start(f32[256,1024]{1,0:T(8,128)S(1)} %convert_add_fusion), channel_id=1, source_target_pairs={{0,8},{8,0},{16,24},{24,16},{1,9},{9,1},{17,25},{25,17},{2,10},{10... | collective-permute-start | bytes 3145736 | tf_op jit(solution)/shard_map/weight_grad/ppermute | solution.py:367
  150.1 11.5 %all-to-all-done.4 = f16[8,264,128]{2,1,0:T(8,128)(2,1)S(1)} async-done(((f16[8,264,128]{2,1,0:T(8,128)(2,1)}), f16[8,264,128]{2,1,0:T(8,128)(2,1)S(1)}, u32[]{:S(2)}, u32[]{:S(2)}) %all-to-all-start.4) | async-done | bytes 540704 | tf_op jit(solution)/shard_map/input_grad/all_to_all | solution.py:336
  161.6 0.1 convert_element_type.32.terms_ref
  161.6 0.3 maximum_select_fusion.after_ref
  162.0 0.8 results.1
  162.8 0.5 copy-done
  (27 shorter events, 0.1 us)
Async XLA Ops:
  0.6 12.3 %all-to-all-start.1 = ((bf16[8,8,2048]{2,1,0:T(8,128)(2,1)}), bf16[8,8,2048]{2,1,0:T(8,128)(2,1)S(1)}, u32[]{:S(2)}, u32[]{:S(2)}) async-start(bf16[8,8,2048]{2,1,0:T(8,128)(2,1)} %bitcast.21), calls=%async_computation.1 | async-start | bytes 524288 | tf_op jit(solution)/shard_map/teacher/all_to_all | solution.py:29
  6.5 1.2 copy-start.1
  7.7 1.2 copy-start.3
  13.7 17.9 %collective-permute-start = (bf16[64,640]{1,0:T(8,128)(2,1)S(1)}, bf16[64,640]{1,0:T(8,128)(2,1)S(1)}, u32[]{:S(2)}, u32[]{:S(2)}) collective-permute-start(bf16[64,640]{1,0:T(8,128)(2,1)S(1)} %get-tuple-element.29), channel_id=1, source_target_pairs={{0,32},{32,64},{64,96},{96,128},{128,160},{160,192},{192,224},{224... | collective-permute-start | bytes 245768 | tf_op jit(solution)/shard_map/teacher/ppermute | solution.py:261
  17.5 14.0 %collective-permute-start.1 = (bf16[64,640]{1,0:T(8,128)(2,1)S(1)}, bf16[64,640]{1,0:T(8,128)(2,1)S(1)}, u32[]{:S(2)}, u32[]{:S(2)}) collective-permute-start(bf16[64,640]{1,0:T(8,128)(2,1)S(1)} %get-tuple-element.30), channel_id=1, source_target_pairs={{0,64},{32,96},{64,128},{96,160},{128,192},{160,224},{192,256},{22... | collective-permute-start | bytes 245768 | tf_op jit(solution)/shard_map/teacher/ppermute | solution.py:261
  23.9 7.7 %collective-permute-start.2 = (bf16[64,640]{1,0:T(8,128)(2,1)S(1)}, bf16[64,640]{1,0:T(8,128)(2,1)S(1)}, u32[]{:S(2)}, u32[]{:S(2)}) collective-permute-start(bf16[64,640]{1,0:T(8,128)(2,1)S(1)} %get-tuple-element.31), channel_id=1, source_target_pairs={{0,480},{32,0},{64,32},{96,64},{128,96},{160,128},{192,160},{224,1... | collective-permute-start | bytes 245768 | tf_op jit(solution)/shard_map/teacher/ppermute | solution.py:261
  25.9 30.5 %all-to-all-start = ((f16[8,1032,128]{2,1,0:T(8,128)(2,1)}), f16[8,1032,128]{2,1,0:T(8,128)(2,1)S(1)}, u32[]{:S(2)}, u32[]{:S(2)}) async-start(f16[8,1032,128]{2,1,0:T(8,128)(2,1)} %convert_element_type.27), calls=%async_computation | async-start | bytes 4227072 | tf_op jit(solution)/shard_map/prediction/all_to_all | solution.py:29
  32.2 25.9 %collective-permute-start.3 = (bf16[64,640]{1,0:T(8,128)(2,1)S(1)}, bf16[64,640]{1,0:T(8,128)(2,1)S(1)}, u32[]{:S(2)}, u32[]{:S(2)}) collective-permute-start(bf16[64,640]{1,0:T(8,128)(2,1)S(1)} %get-tuple-element.33), channel_id=1, source_target_pairs={{0,128},{32,160},{64,192},{96,224},{128,256},{160,288},{192,320},{... | collective-permute-start | bytes 245768 | tf_op jit(solution)/shard_map/teacher/ppermute | solution.py:273
  41.3 21.6 %collective-permute-start.4 = (bf16[64,640]{1,0:T(8,128)(2,1)S(1)}, bf16[64,640]{1,0:T(8,128)(2,1)S(1)}, u32[]{:S(2)}, u32[]{:S(2)}) collective-permute-start(bf16[64,640]{1,0:T(8,128)(2,1)S(1)} %get-tuple-element.34), channel_id=1, source_target_pairs={{0,256},{32,288},{64,320},{96,352},{128,384},{160,416},{192,448},{... | collective-permute-start | bytes 245768 | tf_op jit(solution)/shard_map/teacher/ppermute | solution.py:273
  48.4 14.5 %collective-permute-start.5 = (bf16[64,640]{1,0:T(8,128)(2,1)S(1)}, bf16[64,640]{1,0:T(8,128)(2,1)S(1)}, u32[]{:S(2)}, u32[]{:S(2)}) collective-permute-start(bf16[64,640]{1,0:T(8,128)(2,1)S(1)} %get-tuple-element.35), channel_id=1, source_target_pairs={{0,384},{32,416},{64,448},{96,480},{128,0},{160,32},{192,64},{224,... | collective-permute-start | bytes 245768 | tf_op jit(solution)/shard_map/teacher/ppermute | solution.py:273
  64.4 16.2 %copy-start.5 = (bf16[8,512,128]{2,1,0:T(8,128)(2,1)}, bf16[8,512,128]{2,1,0:T(8,128)(2,1)S(1)}, u32[]{:S(2)}) copy-start(bf16[8,512,128]{2,1,0:T(8,128)(2,1)S(1)} %get-tuple-element.36) | copy-start | bytes 3145732
  64.4 21.0 %copy-start.2 = (bf16[512,1024]{1,0:T(8,128)(2,1)S(1)}, bf16[512,1024]{1,0:T(8,128)(2,1)}, u32[]{:S(2)}) copy-start(bf16[512,1024]{1,0:T(8,128)(2,1)} %w_ref.5) | copy-start | bytes 3145732
  80.5 30.7 %all-to-all-start.2 = ((bf16[8,512,128]{2,1,0:T(8,128)(2,1)}), bf16[8,512,128]{2,1,0:T(8,128)(2,1)S(1)}, u32[]{:S(2)}, u32[]{:S(2)}) async-start(bf16[8,512,128]{2,1,0:T(8,128)(2,1)} %copy-done.5), calls=%async_computation.2 | async-start | bytes 2097152 | tf_op jit(solution)/shard_map/gradient/all_to_all | solution.py:29
  87.5 23.8 %collective-permute-start.6 = (f16[8,264,128]{2,1,0:T(8,128)(2,1)}, f16[8,264,128]{2,1,0:T(8,128)(2,1)}, u32[]{:S(2)}, u32[]{:S(2)}) collective-permute-start(f16[8,264,128]{2,1,0:T(8,128)(2,1)} %convert_element_type.29), channel_id=1, source_target_pairs={{0,32},{32,0},{64,96},{96,64},{128,160},{160,128},{192,224},{224,1... | collective-permute-start | bytes 1622024 | tf_op jit(solution)/shard_map/input_grad/ppermute | solution.py:324
  95.9 3.0 %collective-permute-start.7 = (f32[1,128]{1,0:T(1,128)S(1)}, f32[1,128]{1,0:T(1,128)S(1)}, u32[]{:S(2)}, u32[]{:S(2)}) collective-permute-start(f32[1,128]{1,0:T(1,128)S(1)} %get-tuple-element.40), channel_id=1, source_target_pairs={{0,8},{8,0},{16,24},{24,16},{1,9},{9,1},{17,25},{25,17},{2,10},{10... | collective-permute-start | bytes 1544 | tf_op jit(solution)/shard_map/input_grad/ppermute | solution.py:34
  98.9 6.9 %collective-permute-start.8 = (f32[1,128]{1,0:T(1,128)S(1)}, f32[1,128]{1,0:T(1,128)S(1)}, u32[]{:S(2)}, u32[]{:S(2)}) collective-permute-start(f32[1,128]{1,0:T(1,128)S(1)} %add.35), channel_id=1, source_target_pairs={{0,16},{8,24},{16,0},{24,8},{1,17},{9,25},{17,1},{25,9},{2,18},{10... | collective-permute-start | bytes 1544 | tf_op jit(solution)/shard_map/input_grad/ppermute | solution.py:34
  105.8 5.4 %collective-permute-start.9 = (f32[1,128]{1,0:T(1,128)S(1)}, f32[1,128]{1,0:T(1,128)S(1)}, u32[]{:S(2)}, u32[]{:S(2)}) collective-permute-start(f32[1,128]{1,0:T(1,128)S(1)} %add.36), channel_id=1, source_target_pairs={{0,32},{32,0},{64,96},{96,64},{128,160},{160,128},{192,224},{224,1... | collective-permute-start | bytes 1544 | tf_op jit(solution)/shard_map/input_grad/ppermute | solution.py:34
  112.4 1.2 copy-start.4
  117.0 1.0 copy-start.6
  117.9 11.2 %copy-start.7 = (f32[256,1024]{1,0:T(8,128)S(1)}, f32[256,1024]{1,0:T(8,128)}, u32[]{:S(2)}) copy-start(f32[256,1024]{1,0:T(8,128)} %copy-done.6) | copy-start | bytes 3145732
  117.9 11.2 %collective-permute-start.10 = (f32[256,1024]{1,0:T(8,128)S(1)}, f32[256,1024]{1,0:T(8,128)}, u32[]{:S(2)}, u32[]{:S(2)}) collective-permute-start(f32[256,1024]{1,0:T(8,128)S(1)} %get-tuple-element.42), channel_id=1, source_target_pairs={{0,8},{8,0},{16,24},{24,16},{1,9},{9,1},{17,25},{25,17},{2,10},{10... | collective-permute-start | bytes 3145736 | tf_op jit(solution)/shard_map/weight_grad/ppermute | solution.py:365
  120.9 40.7 %all-to-all-start.4 = ((f16[8,264,128]{2,1,0:T(8,128)(2,1)}), f16[8,264,128]{2,1,0:T(8,128)(2,1)S(1)}, u32[]{:S(2)}, u32[]{:S(2)}) async-start(f16[8,264,128]{2,1,0:T(8,128)(2,1)} %convert_element_type.31), calls=%async_computation.4 | async-start | bytes 1081344 | tf_op jit(solution)/shard_map/input_grad/all_to_all | solution.py:336
  130.5 17.4 %collective-permute-start.11 = (bf16[256,1024]{1,0:T(8,128)(2,1)S(1)}, bf16[256,1024]{1,0:T(8,128)(2,1)S(1)}, u32[]{:S(2)}, u32[]{:S(2)}) collective-permute-start(bf16[256,1024]{1,0:T(8,128)(2,1)S(1)} %add_convert_fusion), channel_id=1, source_target_pairs={{0,16},{8,24},{16,0},{24,8},{1,17},{9,25},{17,1},{25,9},{2,18},{10... | collective-permute-start | bytes 1572872 | tf_op jit(solution)/shard_map/weight_grad/ppermute | solution.py:366
  148.2 13.5 %collective-permute-start.12 = (f32[256,1024]{1,0:T(8,128)S(1)}, f32[256,1024]{1,0:T(8,128)S(1)}, u32[]{:S(2)}, u32[]{:S(2)}) collective-permute-start(f32[256,1024]{1,0:T(8,128)S(1)} %convert_add_fusion), channel_id=1, source_target_pairs={{0,8},{8,0},{16,24},{24,16},{1,9},{9,1},{17,25},{25,17},{2,10},{10... | collective-permute-start | bytes 3145736 | tf_op jit(solution)/shard_map/weight_grad/ppermute | solution.py:367
  162.0 1.3 copy-start

commit v6 on v5

--- a/solution.py
+++ b/solution.py
@@ -183,7 +183,7 @@
             held[n * half : (n + 1) * half, :] = student.T
 
     def columns(ref):
-        parts = [ref[:, c * part : (c + 1) * part, :].reshape(-1, LANES) for c in range(2)]
+        parts = [ref[:, c * part : (c + 1) * part, :].reshape(-1, LANES) for c in range(4)]
         return jnp.concatenate(parts, axis=1)
 
     grad = jnp.concatenate([columns(g_ref), columns(h_ref)], axis=0)
@@ -305,15 +305,15 @@
         half_terms = jax.ShapeDtypeStruct((dp_half, chunk, LANES), f32)
         weights = pl.BlockSpec((width_local, columns), lambda i: (0, 0))
         losses = pl.BlockSpec((1, LANES), lambda i: (0, 0))
-        block = pl.BlockSpec((4, chunk, LANES), lambda i: (i, 0, 0))
+        block = pl.BlockSpec((8, chunk, LANES), lambda i: (i, 0, 0))
         send, total = call(
             send_terms,
             (half_terms, jax.ShapeDtypeStruct((1, LANES), f32)),
             tokens * width_local * columns,
             4_000_000,
-            grid=(2,),
+            grid=(1,),
             in_specs=[
-                pl.BlockSpec((4, part + PIECES, LANES), lambda i: (i, 0, 0)),
+                pl.BlockSpec((8, part + PIECES, LANES), lambda i: (i, 0, 0)),
                 weights,
                 pl.BlockSpec((tensor_count, PIECES, LANES), lambda i: (0, part // PIECES, 0)),
             ],
@@ -328,8 +328,8 @@
             half_terms,
             tokens * width_local * columns,
             5_000_000,
-            grid=(2,),
-            in_specs=[pl.BlockSpec((4, part, LANES), lambda i: (i, 0, 0)), weights, block, losses],
+            grid=(1,),
+            in_specs=[pl.BlockSpec((8, part, LANES), lambda i: (i, 0, 0)), weights, block, losses],
             out_specs=block,
         )(grad_b, proj_weight, got, loss)
         same_parity = [list(range(p, dp_count, 2)) for p in range(2)]
@@ -347,17 +347,17 @@
             5_000_000,
             grid_spec=pltpu.PrefetchScalarGridSpec(
                 num_scalar_prefetch=1,
-                grid=(4,),
+                grid=(2,),
                 in_specs=[
                     pl.BlockSpec((8, 1, 64, width_local), lambda i, p: (0, 1 - p[2], 0, 0)),
                     pl.BlockSpec((8, 1, 64, width_local), lambda i, p: (0, p[2], 0, 0)),
-                    pl.BlockSpec((tensor_count, own, LANES), lambda i, p: (0, i, 0)),
-                    pl.BlockSpec((tensor_count, own, LANES), lambda i, p: (0, i, 0)),
+                    pl.BlockSpec((tensor_count, 2 * own, LANES), lambda i, p: (0, i, 0)),
+                    pl.BlockSpec((tensor_count, 2 * own, LANES), lambda i, p: (0, i, 0)),
                     pl.BlockSpec((1, META, LANES), lambda i, p: (0, 256 // META, 0)),
                 ],
                 out_specs=(
-                    pl.BlockSpec((width_local // 2, 2 * LANES), lambda i, p: (0, i)),
-                    pl.BlockSpec((width_local // 2, 2 * LANES), lambda i, p: (0, i)),
+                    pl.BlockSpec((width_local // 2, 4 * LANES), lambda i, p: (0, i)),
+                    pl.BlockSpec((width_local // 2, 4 * LANES), lambda i, p: (0, i)),
                 ),
                 scratch_shapes=[pltpu.VMEM((width_local, tokens), bf16)],
             ),

time: 165 us -> 165 us (level)
  no operation moved by 1% of the time
where the time goes in v6:
time: 165 us; the launch traced here: 164 us
  starting transfers between devices  84.4 us (51%)
  waiting for transfers between devices  38.2 us (23%)
  blocking collectives  16.1 us (10%)
  Pallas kernels  10.5 us (6%)
  other arithmetic  8.14 us (5%)
  local copies, waits for them, and re-layouts  4.21 us (3%)
  between operations  2.11 us (1%)
    ppermute x3, starting transfers between devices, body(): target.append(lax.ppermute(packed[m], 'dp', moves))  21.7 us
    all_to_all x3, starting transfers between devices, all_to_all(): return lax.all_to_all(x, axis, 0, 0)  16.4 us
    all_to_all x1, blocking collectives, all_to_all(): return lax.all_to_all(x, axis, 0, 0)  16.1 us
    ppermute x1, waiting for transfers between devices, body(): mine = pair.astype(f32) + lax.ppermute(pair, 'seq', other_y).astype(f32)  12.6 us
    ppermute x3, starting transfers between devices, body(): near.append(lax.ppermute(packed[k], 'dp', moves))  12.1 us
    all_to_all x1, waiting for transfers between devices, body(): lax.all_to_all(term.astype(f16), 'dp', 0, 0, axis_index_groups=same_parity)  11.5 us
    ppermute x3, starting transfers between devices, butterfly(): lax.ppermute(x, axis, [(i, i ^ step) for i in range(lax.axis_size(axis))])  8.68 us
    ppermute x1, starting transfers between devices, body(): got = lax.ppermute(send.astype(f16), 'dp', neighbour)  8.43 us
  transfers between devices with their start and end apart: 17, of which 7 were waited for; matrix products, arithmetic and copies ran while one was open for 4% of the time, Pallas kernels for 2%

profile of v6, /device:TPU:34, one launch (start us, length us, event | category | flops | bytes accessed | tf_op | source)
XLA Modules:
  0.0 163.7 jit_solution(8763273469832963311)
XLA Ops:
  0.6 5.9 %all-to-all-start.1 = ((bf16[8,8,2048]{2,1,0:T(8,128)(2,1)}), bf16[8,8,2048]{2,1,0:T(8,128)(2,1)S(1)}, u32[]{:S(2)}, u32[]{:S(2)}) async-start(bf16[8,8,2048]{2,1,0:T(8,128)(2,1)} %bitcast.21), calls=%async_computation.1 | async-start | bytes 524288 | tf_op jit(solution)/shard_map/teacher/all_to_all | solution.py:29
  6.5 1.2 copy-done.1
  7.7 1.2 copy-done.3
  8.9 2.3 %teacher.3 = (f32[8,1032,128]{2,1,0:T(8,128)S(1)}, f32[8,128]{1,0:T(8,128)S(1)}) custom-call(bf16[1024,512]{1,0:T(8,128)(2,1)S(1)} %bitcast.15, bf16[512,1024]{1,0:T(8,128)(2,1)S(1)} %copy-done.1), custom_call_target="tpu_custom_call" | custom-call | flops 1073741824 | bytes 6000000 | tf_op jit(solution)/shard_map/teacher/pallas_call | solution.py:224
  11.2 1.6 convert_element_type.27
  12.9 0.1 pad_add_fusion.place_ref
  13.0 0.8 teacher.4
  13.7 3.8 %collective-permute-start = (bf16[64,640]{1,0:T(8,128)(2,1)S(1)}, bf16[64,640]{1,0:T(8,128)(2,1)S(1)}, u32[]{:S(2)}, u32[]{:S(2)}) collective-permute-start(bf16[64,640]{1,0:T(8,128)(2,1)S(1)} %get-tuple-element.29), channel_id=1, source_target_pairs={{0,32},{32,64},{64,96},{96,128},{128,160},{160,192},{192,224},{224... | collective-permute-start | bytes 245768 | tf_op jit(solution)/shard_map/teacher/ppermute | solution.py:261
  17.5 6.4 %collective-permute-start.1 = (bf16[64,640]{1,0:T(8,128)(2,1)S(1)}, bf16[64,640]{1,0:T(8,128)(2,1)S(1)}, u32[]{:S(2)}, u32[]{:S(2)}) collective-permute-start(bf16[64,640]{1,0:T(8,128)(2,1)S(1)} %get-tuple-element.30), channel_id=1, source_target_pairs={{0,64},{32,96},{64,128},{96,160},{128,192},{160,224},{192,256},{22... | collective-permute-start | bytes 245768 | tf_op jit(solution)/shard_map/teacher/ppermute | solution.py:261
  23.9 1.9 %collective-permute-start.2 = (bf16[64,640]{1,0:T(8,128)(2,1)S(1)}, bf16[64,640]{1,0:T(8,128)(2,1)S(1)}, u32[]{:S(2)}, u32[]{:S(2)}) collective-permute-start(bf16[64,640]{1,0:T(8,128)(2,1)S(1)} %get-tuple-element.31), channel_id=1, source_target_pairs={{0,480},{32,0},{64,32},{96,64},{128,96},{160,128},{192,160},{224,1... | collective-permute-start | bytes 245768 | tf_op jit(solution)/shard_map/teacher/ppermute | solution.py:261
  25.9 5.7 %all-to-all-start = ((f16[8,1032,128]{2,1,0:T(8,128)(2,1)}), f16[8,1032,128]{2,1,0:T(8,128)(2,1)S(1)}, u32[]{:S(2)}, u32[]{:S(2)}) async-start(f16[8,1032,128]{2,1,0:T(8,128)(2,1)} %convert_element_type.27), calls=%async_computation | async-start | bytes 4227072 | tf_op jit(solution)/shard_map/prediction/all_to_all | solution.py:29
  31.6 0.6 teacher.5
  32.2 9.1 %collective-permute-start.3 = (bf16[64,640]{1,0:T(8,128)(2,1)S(1)}, bf16[64,640]{1,0:T(8,128)(2,1)S(1)}, u32[]{:S(2)}, u32[]{:S(2)}) collective-permute-start(bf16[64,640]{1,0:T(8,128)(2,1)S(1)} %get-tuple-element.33), channel_id=1, source_target_pairs={{0,128},{32,160},{64,192},{96,224},{128,256},{160,288},{192,320},{... | collective-permute-start | bytes 245768 | tf_op jit(solution)/shard_map/teacher/ppermute | solution.py:273
  41.3 7.1 %collective-permute-start.4 = (bf16[64,640]{1,0:T(8,128)(2,1)S(1)}, bf16[64,640]{1,0:T(8,128)(2,1)S(1)}, u32[]{:S(2)}, u32[]{:S(2)}) collective-permute-start(bf16[64,640]{1,0:T(8,128)(2,1)S(1)} %get-tuple-element.34), channel_id=1, source_target_pairs={{0,256},{32,288},{64,320},{96,352},{128,384},{160,416},{192,448},{... | collective-permute-start | bytes 245768 | tf_op jit(solution)/shard_map/teacher/ppermute | solution.py:273
  48.4 5.5 %collective-permute-start.5 = (bf16[64,640]{1,0:T(8,128)(2,1)S(1)}, bf16[64,640]{1,0:T(8,128)(2,1)S(1)}, u32[]{:S(2)}, u32[]{:S(2)}) collective-permute-start(bf16[64,640]{1,0:T(8,128)(2,1)S(1)} %get-tuple-element.35), channel_id=1, source_target_pairs={{0,384},{32,416},{64,448},{96,480},{128,0},{160,32},{192,64},{224,... | collective-permute-start | bytes 245768 | tf_op jit(solution)/shard_map/teacher/ppermute | solution.py:273
  53.9 2.5 %all-to-all-done = f16[8,1032,128]{2,1,0:T(8,128)(2,1)S(1)} async-done(((f16[8,1032,128]{2,1,0:T(8,128)(2,1)}), f16[8,1032,128]{2,1,0:T(8,128)(2,1)S(1)}, u32[]{:S(2)}, u32[]{:S(2)}) %all-to-all-start) | async-done | bytes 2113568 | tf_op jit(solution)/shard_map/prediction/all_to_all | solution.py:29
  56.4 0.3 convert_element_type.28
  56.7 1.4 fusion
  58.1 4.8 %collective-permute-done.4.t2_ref = bf16[64,640]{1,0:T(8,128)(2,1)S(1)} collective-permute-done((bf16[64,640]{1,0:T(8,128)(2,1)S(1)}, bf16[64,640]{1,0:T(8,128)(2,1)S(1)}, u32[]{:S(2)}, u32[]{:S(2)}) %collective-permute-start.4) | collective-permute-done | bytes 81952 | tf_op jit(solution)/shard_map/teacher/ppermute | solution.py:273
  62.9 1.4 gradient.1
  64.4 16.1 %all_to_all.25.g_ref.loss_ref = bf16[8,528,128]{2,1,0:T(8,128)(2,1)S(1)} all-to-all(bf16[8,528,128]{2,1,0:T(8,128)(2,1)S(1)} %get-tuple-element.37), channel_id=1, replica_groups=mesh['dp'=16,'seq'=4,'tensor'=8] {'tensor'}, dimensions={0} | all-to-all | bytes 2162688 | tf_op jit(solution)/shard_map/gradient/all_to_all | solution.py:29
  80.5 4.8 %all-to-all-start.2 = ((bf16[8,512,128]{2,1,0:T(8,128)(2,1)}), bf16[8,512,128]{2,1,0:T(8,128)(2,1)S(1)}, u32[]{:S(2)}, u32[]{:S(2)}) async-start(bf16[8,512,128]{2,1,0:T(8,128)(2,1)} %copy-done.5), calls=%async_computation.2 | async-start | bytes 2097152 | tf_op jit(solution)/shard_map/gradient/all_to_all | solution.py:29
  85.4 0.9 input_grad.2
  86.3 0.9 convert_element_type.29
  87.1 8.4 %collective-permute-start.6 = (f16[8,264,128]{2,1,0:T(8,128)(2,1)}, f16[8,264,128]{2,1,0:T(8,128)(2,1)}, u32[]{:S(2)}, u32[]{:S(2)}) collective-permute-start(f16[8,264,128]{2,1,0:T(8,128)(2,1)} %convert_element_type.29), channel_id=1, source_target_pairs={{0,32},{32,0},{64,96},{96,64},{128,160},{160,128},{192,224},{224,1... | collective-permute-start | bytes 1622024 | tf_op jit(solution)/shard_map/input_grad/ppermute | solution.py:324
  95.6 1.9 %collective-permute-start.7 = (f32[1,128]{1,0:T(1,128)S(1)}, f32[1,128]{1,0:T(1,128)S(1)}, u32[]{:S(2)}, u32[]{:S(2)}) collective-permute-start(f32[1,128]{1,0:T(1,128)S(1)} %get-tuple-element.40), channel_id=1, source_target_pairs={{0,8},{8,0},{16,24},{24,16},{1,9},{9,1},{17,25},{25,17},{2,10},{10... | collective-permute-start | bytes 1544 | tf_op jit(solution)/shard_map/input_grad/ppermute | solution.py:34
  97.5 1.1 collective-permute-done.7
  98.6 4.8 %collective-permute-start.8 = (f32[1,128]{1,0:T(1,128)S(1)}, f32[1,128]{1,0:T(1,128)S(1)}, u32[]{:S(2)}, u32[]{:S(2)}) collective-permute-start(f32[1,128]{1,0:T(1,128)S(1)} %add.35), channel_id=1, source_target_pairs={{0,16},{8,24},{16,0},{24,8},{1,17},{9,25},{17,1},{25,9},{2,18},{10... | collective-permute-start | bytes 1544 | tf_op jit(solution)/shard_map/input_grad/ppermute | solution.py:34
  103.4 2.1 %collective-permute-done.8 = f32[1,128]{1,0:T(1,128)S(1)} collective-permute-done((f32[1,128]{1,0:T(1,128)S(1)}, f32[1,128]{1,0:T(1,128)S(1)}, u32[]{:S(2)}, u32[]{:S(2)}) %collective-permute-start.8) | collective-permute-done | bytes 544 | tf_op jit(solution)/shard_map/input_grad/ppermute | solution.py:34
  105.5 2.0 %collective-permute-start.9 = (f32[1,128]{1,0:T(1,128)S(1)}, f32[1,128]{1,0:T(1,128)S(1)}, u32[]{:S(2)}, u32[]{:S(2)}) collective-permute-start(f32[1,128]{1,0:T(1,128)S(1)} %add.36), channel_id=1, source_target_pairs={{0,32},{32,0},{64,96},{96,64},{128,160},{160,128},{192,224},{224,1... | collective-permute-start | bytes 1544 | tf_op jit(solution)/shard_map/input_grad/ppermute | solution.py:34
  107.5 3.4 %collective-permute-done.9 = f32[1,128]{1,0:T(1,128)S(1)} collective-permute-done((f32[1,128]{1,0:T(1,128)S(1)}, f32[1,128]{1,0:T(1,128)S(1)}, u32[]{:S(2)}, u32[]{:S(2)}) %collective-permute-start.9) | collective-permute-done | bytes 544 | tf_op jit(solution)/shard_map/input_grad/ppermute | solution.py:34
  110.9 1.1 convert_element_type.30.got_ref
  112.1 0.9 input_grad.3.after_ref
  113.0 0.3 copy-done.4
  113.3 2.9 %weight_grad.1 = (f32[256,1024]{1,0:T(8,128)S(1)}, f32[256,1024]{1,0:T(8,128)S(1)}) custom-call(s32[4]{0:T(128)S(1)} %pad_add_fusion.place_ref, bf16[8,2,64,512]{3,2,1,0:T(8,128)(2,1)S(1)} %bitcast.16, bf16[8,2,64,512]{3,2,1,0:T(8,128)(2,1)S(1)} %bitcast.17, bf16[8,528,128]{2,1,0:T(8,128)(2,1)S(1)} %all_to_all.25.g_ref.loss_ref, ...), custom_call_target="tpu_custom_call" | custom-call | flops 1073741824 | bytes 5000000 | tf_op jit(solution)/shard_map/weight_grad/pallas_call | solution.py:343
  116.2 1.0 copy-done.6
  117.2 2.0 %collective-permute-start.10 = (f32[256,1024]{1,0:T(8,128)S(1)}, f32[256,1024]{1,0:T(8,128)}, u32[]{:S(2)}, u32[]{:S(2)}) collective-permute-start(f32[256,1024]{1,0:T(8,128)S(1)} %get-tuple-element.42), channel_id=1, source_target_pairs={{0,8},{8,0},{16,24},{24,16},{1,9},{9,1},{17,25},{25,17},{2,10},{10... | collective-permute-start | bytes 3145736 | tf_op jit(solution)/shard_map/weight_grad/ppermute | solution.py:365
  119.2 0.9 convert_element_type.31
  120.1 8.3 %all-to-all-start.4 = ((f16[8,264,128]{2,1,0:T(8,128)(2,1)}), f16[8,264,128]{2,1,0:T(8,128)(2,1)S(1)}, u32[]{:S(2)}, u32[]{:S(2)}) async-start(f16[8,264,128]{2,1,0:T(8,128)(2,1)} %convert_element_type.31), calls=%async_computation.4 | async-start | bytes 1081344 | tf_op jit(solution)/shard_map/input_grad/all_to_all | solution.py:336
  128.4 1.4 add_convert_fusion
  129.8 4.8 %collective-permute-start.11 = (bf16[256,1024]{1,0:T(8,128)(2,1)S(1)}, bf16[256,1024]{1,0:T(8,128)(2,1)S(1)}, u32[]{:S(2)}, u32[]{:S(2)}) collective-permute-start(bf16[256,1024]{1,0:T(8,128)(2,1)S(1)} %add_convert_fusion), channel_id=1, source_target_pairs={{0,16},{8,24},{16,0},{24,8},{1,17},{9,25},{17,1},{25,9},{2,18},{10... | collective-permute-start | bytes 1572872 | tf_op jit(solution)/shard_map/weight_grad/ppermute | solution.py:366
  134.6 12.6 %collective-permute-done.11 = bf16[256,1024]{1,0:T(8,128)(2,1)S(1)} collective-permute-done((bf16[256,1024]{1,0:T(8,128)(2,1)S(1)}, bf16[256,1024]{1,0:T(8,128)(2,1)S(1)}, u32[]{:S(2)}, u32[]{:S(2)}) %collective-permute-start.11) | collective-permute-done | bytes 524320 | tf_op jit(solution)/shard_map/weight_grad/ppermute | solution.py:366
  147.2 0.2 convert_add_fusion
  147.4 1.9 %collective-permute-start.12 = (f32[256,1024]{1,0:T(8,128)S(1)}, f32[256,1024]{1,0:T(8,128)S(1)}, u32[]{:S(2)}, u32[]{:S(2)}) collective-permute-start(f32[256,1024]{1,0:T(8,128)S(1)} %convert_add_fusion), channel_id=1, source_target_pairs={{0,8},{8,0},{16,24},{24,16},{1,9},{9,1},{17,25},{25,17},{2,10},{10... | collective-permute-start | bytes 3145736 | tf_op jit(solution)/shard_map/weight_grad/ppermute | solution.py:367
  149.3 11.5 %all-to-all-done.4 = f16[8,264,128]{2,1,0:T(8,128)(2,1)S(1)} async-done(((f16[8,264,128]{2,1,0:T(8,128)(2,1)}), f16[8,264,128]{2,1,0:T(8,128)(2,1)S(1)}, u32[]{:S(2)}, u32[]{:S(2)}) %all-to-all-start.4) | async-done | bytes 540704 | tf_op jit(solution)/shard_map/input_grad/all_to_all | solution.py:336
  160.9 0.3 maximum_select_fusion.after_ref
  161.3 0.8 results.1
  162.1 0.5 copy-done
  (27 shorter events, 0.2 us)
Async XLA Ops:
  0.6 12.3 %all-to-all-start.1 = ((bf16[8,8,2048]{2,1,0:T(8,128)(2,1)}), bf16[8,8,2048]{2,1,0:T(8,128)(2,1)S(1)}, u32[]{:S(2)}, u32[]{:S(2)}) async-start(bf16[8,8,2048]{2,1,0:T(8,128)(2,1)} %bitcast.21), calls=%async_computation.1 | async-start | bytes 524288 | tf_op jit(solution)/shard_map/teacher/all_to_all | solution.py:29
  6.5 1.2 copy-start.1
  7.7 1.2 copy-start.3
  13.7 17.9 %collective-permute-start = (bf16[64,640]{1,0:T(8,128)(2,1)S(1)}, bf16[64,640]{1,0:T(8,128)(2,1)S(1)}, u32[]{:S(2)}, u32[]{:S(2)}) collective-permute-start(bf16[64,640]{1,0:T(8,128)(2,1)S(1)} %get-tuple-element.29), channel_id=1, source_target_pairs={{0,32},{32,64},{64,96},{96,128},{128,160},{160,192},{192,224},{224... | collective-permute-start | bytes 245768 | tf_op jit(solution)/shard_map/teacher/ppermute | solution.py:261
  17.5 14.0 %collective-permute-start.1 = (bf16[64,640]{1,0:T(8,128)(2,1)S(1)}, bf16[64,640]{1,0:T(8,128)(2,1)S(1)}, u32[]{:S(2)}, u32[]{:S(2)}) collective-permute-start(bf16[64,640]{1,0:T(8,128)(2,1)S(1)} %get-tuple-element.30), channel_id=1, source_target_pairs={{0,64},{32,96},{64,128},{96,160},{128,192},{160,224},{192,256},{22... | collective-permute-start | bytes 245768 | tf_op jit(solution)/shard_map/teacher/ppermute | solution.py:261
  23.9 7.7 %collective-permute-start.2 = (bf16[64,640]{1,0:T(8,128)(2,1)S(1)}, bf16[64,640]{1,0:T(8,128)(2,1)S(1)}, u32[]{:S(2)}, u32[]{:S(2)}) collective-permute-start(bf16[64,640]{1,0:T(8,128)(2,1)S(1)} %get-tuple-element.31), channel_id=1, source_target_pairs={{0,480},{32,0},{64,32},{96,64},{128,96},{160,128},{192,160},{224,1... | collective-permute-start | bytes 245768 | tf_op jit(solution)/shard_map/teacher/ppermute | solution.py:261
  25.9 30.5 %all-to-all-start = ((f16[8,1032,128]{2,1,0:T(8,128)(2,1)}), f16[8,1032,128]{2,1,0:T(8,128)(2,1)S(1)}, u32[]{:S(2)}, u32[]{:S(2)}) async-start(f16[8,1032,128]{2,1,0:T(8,128)(2,1)} %convert_element_type.27), calls=%async_computation | async-start | bytes 4227072 | tf_op jit(solution)/shard_map/prediction/all_to_all | solution.py:29
  32.2 25.9 %collective-permute-start.3 = (bf16[64,640]{1,0:T(8,128)(2,1)S(1)}, bf16[64,640]{1,0:T(8,128)(2,1)S(1)}, u32[]{:S(2)}, u32[]{:S(2)}) collective-permute-start(bf16[64,640]{1,0:T(8,128)(2,1)S(1)} %get-tuple-element.33), channel_id=1, source_target_pairs={{0,128},{32,160},{64,192},{96,224},{128,256},{160,288},{192,320},{... | collective-permute-start | bytes 245768 | tf_op jit(solution)/shard_map/teacher/ppermute | solution.py:273
  41.3 21.6 %collective-permute-start.4 = (bf16[64,640]{1,0:T(8,128)(2,1)S(1)}, bf16[64,640]{1,0:T(8,128)(2,1)S(1)}, u32[]{:S(2)}, u32[]{:S(2)}) collective-permute-start(bf16[64,640]{1,0:T(8,128)(2,1)S(1)} %get-tuple-element.34), channel_id=1, source_target_pairs={{0,256},{32,288},{64,320},{96,352},{128,384},{160,416},{192,448},{... | collective-permute-start | bytes 245768 | tf_op jit(solution)/shard_map/teacher/ppermute | solution.py:273
  48.4 14.5 %collective-permute-start.5 = (bf16[64,640]{1,0:T(8,128)(2,1)S(1)}, bf16[64,640]{1,0:T(8,128)(2,1)S(1)}, u32[]{:S(2)}, u32[]{:S(2)}) collective-permute-start(bf16[64,640]{1,0:T(8,128)(2,1)S(1)} %get-tuple-element.35), channel_id=1, source_target_pairs={{0,384},{32,416},{64,448},{96,480},{128,0},{160,32},{192,64},{224,... | collective-permute-start | bytes 245768 | tf_op jit(solution)/shard_map/teacher/ppermute | solution.py:273
  64.4 16.2 %copy-start.5 = (bf16[8,512,128]{2,1,0:T(8,128)(2,1)}, bf16[8,512,128]{2,1,0:T(8,128)(2,1)S(1)}, u32[]{:S(2)}) copy-start(bf16[8,512,128]{2,1,0:T(8,128)(2,1)S(1)} %get-tuple-element.36) | copy-start | bytes 3145732
  64.4 21.0 %copy-start.2 = (bf16[512,1024]{1,0:T(8,128)(2,1)S(1)}, bf16[512,1024]{1,0:T(8,128)(2,1)}, u32[]{:S(2)}) copy-start(bf16[512,1024]{1,0:T(8,128)(2,1)} %w_ref.5) | copy-start | bytes 3145732
  80.5 30.4 %all-to-all-start.2 = ((bf16[8,512,128]{2,1,0:T(8,128)(2,1)}), bf16[8,512,128]{2,1,0:T(8,128)(2,1)S(1)}, u32[]{:S(2)}, u32[]{:S(2)}) async-start(bf16[8,512,128]{2,1,0:T(8,128)(2,1)} %copy-done.5), calls=%async_computation.2 | async-start | bytes 2097152 | tf_op jit(solution)/shard_map/gradient/all_to_all | solution.py:29
  87.1 23.8 %collective-permute-start.6 = (f16[8,264,128]{2,1,0:T(8,128)(2,1)}, f16[8,264,128]{2,1,0:T(8,128)(2,1)}, u32[]{:S(2)}, u32[]{:S(2)}) collective-permute-start(f16[8,264,128]{2,1,0:T(8,128)(2,1)} %convert_element_type.29), channel_id=1, source_target_pairs={{0,32},{32,0},{64,96},{96,64},{128,160},{160,128},{192,224},{224,1... | collective-permute-start | bytes 1622024 | tf_op jit(solution)/shard_map/input_grad/ppermute | solution.py:324
  95.6 3.0 %collective-permute-start.7 = (f32[1,128]{1,0:T(1,128)S(1)}, f32[1,128]{1,0:T(1,128)S(1)}, u32[]{:S(2)}, u32[]{:S(2)}) collective-permute-start(f32[1,128]{1,0:T(1,128)S(1)} %get-tuple-element.40), channel_id=1, source_target_pairs={{0,8},{8,0},{16,24},{24,16},{1,9},{9,1},{17,25},{25,17},{2,10},{10... | collective-permute-start | bytes 1544 | tf_op jit(solution)/shard_map/input_grad/ppermute | solution.py:34
  98.6 6.9 %collective-permute-start.8 = (f32[1,128]{1,0:T(1,128)S(1)}, f32[1,128]{1,0:T(1,128)S(1)}, u32[]{:S(2)}, u32[]{:S(2)}) collective-permute-start(f32[1,128]{1,0:T(1,128)S(1)} %add.35), channel_id=1, source_target_pairs={{0,16},{8,24},{16,0},{24,8},{1,17},{9,25},{17,1},{25,9},{2,18},{10... | collective-permute-start | bytes 1544 | tf_op jit(solution)/shard_map/input_grad/ppermute | solution.py:34
  105.5 5.4 %collective-permute-start.9 = (f32[1,128]{1,0:T(1,128)S(1)}, f32[1,128]{1,0:T(1,128)S(1)}, u32[]{:S(2)}, u32[]{:S(2)}) collective-permute-start(f32[1,128]{1,0:T(1,128)S(1)} %add.36), channel_id=1, source_target_pairs={{0,32},{32,0},{64,96},{96,64},{128,160},{160,128},{192,224},{224,1... | collective-permute-start | bytes 1544 | tf_op jit(solution)/shard_map/input_grad/ppermute | solution.py:34
  112.1 1.2 copy-start.4
  116.2 1.0 copy-start.6
  117.2 11.2 %copy-start.7 = (f32[256,1024]{1,0:T(8,128)S(1)}, f32[256,1024]{1,0:T(8,128)}, u32[]{:S(2)}) copy-start(f32[256,1024]{1,0:T(8,128)} %copy-done.6) | copy-start | bytes 3145732
  117.2 11.2 %collective-permute-start.10 = (f32[256,1024]{1,0:T(8,128)S(1)}, f32[256,1024]{1,0:T(8,128)}, u32[]{:S(2)}, u32[]{:S(2)}) collective-permute-start(f32[256,1024]{1,0:T(8,128)S(1)} %get-tuple-element.42), channel_id=1, source_target_pairs={{0,8},{8,0},{16,24},{24,16},{1,9},{9,1},{17,25},{25,17},{2,10},{10... | collective-permute-start | bytes 3145736 | tf_op jit(solution)/shard_map/weight_grad/ppermute | solution.py:365
  120.1 40.8 %all-to-all-start.4 = ((f16[8,264,128]{2,1,0:T(8,128)(2,1)}), f16[8,264,128]{2,1,0:T(8,128)(2,1)S(1)}, u32[]{:S(2)}, u32[]{:S(2)}) async-start(f16[8,264,128]{2,1,0:T(8,128)(2,1)} %convert_element_type.31), calls=%async_computation.4 | async-start | bytes 1081344 | tf_op jit(solution)/shard_map/input_grad/all_to_all | solution.py:336
  129.8 17.4 %collective-permute-start.11 = (bf16[256,1024]{1,0:T(8,128)(2,1)S(1)}, bf16[256,1024]{1,0:T(8,128)(2,1)S(1)}, u32[]{:S(2)}, u32[]{:S(2)}) collective-permute-start(bf16[256,1024]{1,0:T(8,128)(2,1)S(1)} %add_convert_fusion), channel_id=1, source_target_pairs={{0,16},{8,24},{16,0},{24,8},{1,17},{9,25},{17,1},{25,9},{2,18},{10... | collective-permute-start | bytes 1572872 | tf_op jit(solution)/shard_map/weight_grad/ppermute | solution.py:366
  147.4 13.6 %collective-permute-start.12 = (f32[256,1024]{1,0:T(8,128)S(1)}, f32[256,1024]{1,0:T(8,128)S(1)}, u32[]{:S(2)}, u32[]{:S(2)}) collective-permute-start(f32[256,1024]{1,0:T(8,128)S(1)} %convert_add_fusion), channel_id=1, source_target_pairs={{0,8},{8,0},{16,24},{24,16},{1,9},{9,1},{17,25},{25,17},{2,10},{10... | collective-permute-start | bytes 3145736 | tf_op jit(solution)/shard_map/weight_grad/ppermute | solution.py:367
  161.3 1.3 copy-start

commit v7 on v6

--- a/solution.py
+++ b/solution.py
@@ -69,8 +69,8 @@
     partial = jnp.dot(s_ref[...], w_ref[...], preferred_element_type=f32)
     power = exponent_of(jnp.max(jnp.abs(partial), axis=1, keepdims=True))
     scaled = partial * jnp.exp2(TOP - power)
-    rows, width = scaled.shape[0] // 2, scaled.shape[1]
-    for n in range(2):
+    rows, width = scaled.shape[0] // 4, scaled.shape[1]
+    for n in range(4):
         for c in range(width // LANES):
             o_ref[n, c * rows : (c + 1) * rows, :] = scaled[n * rows : (n + 1) * rows, c * LANES : (c + 1) * LANES]
         meta = jnp.transpose(jnp.broadcast_to(power[n * rows : (n + 1) * rows], (rows, LANES)))
@@ -183,7 +183,7 @@
             held[n * half : (n + 1) * half, :] = student.T
 
     def columns(ref):
-        parts = [ref[:, c * part : (c + 1) * part, :].reshape(-1, LANES) for c in range(4)]
+        parts = [ref[:, c * part : (c + 1) * part, :].reshape(-1, LANES) for c in range(8)]
         return jnp.concatenate(parts, axis=1)
 
     grad = jnp.concatenate([columns(g_ref), columns(h_ref)], axis=0)
@@ -229,13 +229,13 @@
             ),
             2 * tokens * width_local * columns,
             6_000_000,
-            grid=(tensor_count // 2,),
+            grid=(tensor_count // 4,),
             in_specs=[
-                pl.BlockSpec((2 * own, width_local), lambda i: (i, 0)),
+                pl.BlockSpec((4 * own, width_local), lambda i: (i, 0)),
                 pl.BlockSpec((width_local, columns), lambda i: (0, 0)),
             ],
             out_specs=(
-                pl.BlockSpec((2, size, LANES), lambda i: (i, 0, 0)),
+                pl.BlockSpec((4, size, LANES), lambda i: (i, 0, 0)),
                 pl.BlockSpec((META, LANES), lambda i: (0, 0)),
             ),
         )(student, proj_weight)
@@ -347,17 +347,17 @@
             5_000_000,
             grid_spec=pltpu.PrefetchScalarGridSpec(
                 num_scalar_prefetch=1,
-                grid=(2,),
+                grid=(1,),
                 in_specs=[
                     pl.BlockSpec((8, 1, 64, width_local), lambda i, p: (0, 1 - p[2], 0, 0)),
                     pl.BlockSpec((8, 1, 64, width_local), lambda i, p: (0, p[2], 0, 0)),
-                    pl.BlockSpec((tensor_count, 2 * own, LANES), lambda i, p: (0, i, 0)),
-                    pl.BlockSpec((tensor_count, 2 * own, LANES), lambda i, p: (0, i, 0)),
+                    pl.BlockSpec((tensor_count, 4 * own, LANES), lambda i, p: (0, i, 0)),
+                    pl.BlockSpec((tensor_count, 4 * own, LANES), lambda i, p: (0, i, 0)),
                     pl.BlockSpec((1, META, LANES), lambda i, p: (0, 256 // META, 0)),
                 ],
                 out_specs=(
-                    pl.BlockSpec((width_local // 2, 4 * LANES), lambda i, p: (0, i)),
-                    pl.BlockSpec((width_local // 2, 4 * LANES), lambda i, p: (0, i)),
+                    pl.BlockSpec((width_local // 2, 8 * LANES), lambda i, p: (0, i)),
+                    pl.BlockSpec((width_local // 2, 8 * LANES), lambda i, p: (0, i)),
                 ),
                 scratch_shapes=[pltpu.VMEM((width_local, tokens), bf16)],
             ),

time: 165 us -> 163 us (0.988)
  transfers between devices with their start and end apart: 17 -> 17, of which waited for: 7 -> 8; matrix products, arithmetic and copies ran while one was open for 4% -> 4% of each run, Pallas kernels for 2% -> 2%
where the time goes in v7:
time: 163 us; the launch traced here: 162 us
  starting transfers between devices  84.3 us (52%)
  waiting for transfers between devices  38.3 us (23%)
  blocking collectives  16.1 us (10%)
  Pallas kernels  9.11 us (6%)
  other arithmetic  8.14 us (5%)
  local copies, waits for them, and re-layouts  4.22 us (3%)
  between operations  2.1 us (1%)
    ppermute x3, starting transfers between devices, body(): target.append(lax.ppermute(packed[m], 'dp', moves))  21.7 us
    all_to_all x3, starting transfers between devices, all_to_all(): return lax.all_to_all(x, axis, 0, 0)  16.3 us
    all_to_all x1, blocking collectives, all_to_all(): return lax.all_to_all(x, axis, 0, 0)  16.1 us
    ppermute x1, waiting for transfers between devices, body(): mine = pair.astype(f32) + lax.ppermute(pair, 'seq', other_y).astype(f32)  12.6 us
    ppermute x3, starting transfers between devices, body(): near.append(lax.ppermute(packed[k], 'dp', moves))  12.1 us
    all_to_all x1, waiting for transfers between devices, body(): lax.all_to_all(term.astype(f16), 'dp', 0, 0, axis_index_groups=same_parity)  11.5 us
    ppermute x3, starting transfers between devices, butterfly(): lax.ppermute(x, axis, [(i, i ^ step) for i in range(lax.axis_size(axis))])  8.69 us
    ppermute x1, starting transfers between devices, body(): got = lax.ppermute(send.astype(f16), 'dp', neighbour)  8.42 us
  transfers between devices with their start and end apart: 17, of which 8 were waited for; matrix products, arithmetic and copies ran while one was open for 4% of the time, Pallas kernels for 2%

profile of v7, /device:TPU:34, one launch (start us, length us, event | category | flops | bytes accessed | tf_op | source)
XLA Modules:
  0.0 162.3 jit_solution(3830674875371717305)
XLA Ops:
  0.6 5.9 %all-to-all-start.1 = ((bf16[8,8,2048]{2,1,0:T(8,128)(2,1)}), bf16[8,8,2048]{2,1,0:T(8,128)(2,1)S(1)}, u32[]{:S(2)}, u32[]{:S(2)}) async-start(bf16[8,8,2048]{2,1,0:T(8,128)(2,1)} %bitcast.21), calls=%async_computation.1 | async-start | bytes 524288 | tf_op jit(solution)/shard_map/teacher/all_to_all | solution.py:29
  6.5 1.2 copy-done.1
  7.7 1.2 copy-done.3
  8.9 1.9 %teacher.3 = (f32[8,1032,128]{2,1,0:T(8,128)S(1)}, f32[8,128]{1,0:T(8,128)S(1)}) custom-call(bf16[1024,512]{1,0:T(8,128)(2,1)S(1)} %bitcast.15, bf16[512,1024]{1,0:T(8,128)(2,1)S(1)} %copy-done.1), custom_call_target="tpu_custom_call" | custom-call | flops 1073741824 | bytes 6000000 | tf_op jit(solution)/shard_map/teacher/pallas_call | solution.py:224
  10.8 1.6 %convert_element_type.27 = f16[8,1032,128]{2,1,0:T(8,128)(2,1)} convert(f32[8,1032,128]{2,1,0:T(8,128)S(1)} %get-tuple-element.24) | non-fusion elementwise | flops 1056768 | bytes 6340608 | tf_op jit(solution)/shard_map/teacher/convert_element_type | solution.py:242
  12.5 0.1 all-to-all-done.1
  12.6 0.8 teacher.4
  13.4 3.8 %collective-permute-start = (bf16[64,640]{1,0:T(8,128)(2,1)S(1)}, bf16[64,640]{1,0:T(8,128)(2,1)S(1)}, u32[]{:S(2)}, u32[]{:S(2)}) collective-permute-start(bf16[64,640]{1,0:T(8,128)(2,1)S(1)} %get-tuple-element.29), channel_id=1, source_target_pairs={{0,32},{32,64},{64,96},{96,128},{128,160},{160,192},{192,224},{224... | collective-permute-start | bytes 245768 | tf_op jit(solution)/shard_map/teacher/ppermute | solution.py:261
  17.2 6.4 %collective-permute-start.1 = (bf16[64,640]{1,0:T(8,128)(2,1)S(1)}, bf16[64,640]{1,0:T(8,128)(2,1)S(1)}, u32[]{:S(2)}, u32[]{:S(2)}) collective-permute-start(bf16[64,640]{1,0:T(8,128)(2,1)S(1)} %get-tuple-element.30), channel_id=1, source_target_pairs={{0,64},{32,96},{64,128},{96,160},{128,192},{160,224},{192,256},{22... | collective-permute-start | bytes 245768 | tf_op jit(solution)/shard_map/teacher/ppermute | solution.py:261
  23.6 1.9 %collective-permute-start.2 = (bf16[64,640]{1,0:T(8,128)(2,1)S(1)}, bf16[64,640]{1,0:T(8,128)(2,1)S(1)}, u32[]{:S(2)}, u32[]{:S(2)}) collective-permute-start(bf16[64,640]{1,0:T(8,128)(2,1)S(1)} %get-tuple-element.31), channel_id=1, source_target_pairs={{0,480},{32,0},{64,32},{96,64},{128,96},{160,128},{192,160},{224,1... | collective-permute-start | bytes 245768 | tf_op jit(solution)/shard_map/teacher/ppermute | solution.py:261
  25.5 5.6 %all-to-all-start = ((f16[8,1032,128]{2,1,0:T(8,128)(2,1)}), f16[8,1032,128]{2,1,0:T(8,128)(2,1)S(1)}, u32[]{:S(2)}, u32[]{:S(2)}) async-start(f16[8,1032,128]{2,1,0:T(8,128)(2,1)} %convert_element_type.27), calls=%async_computation | async-start | bytes 4227072 | tf_op jit(solution)/shard_map/prediction/all_to_all | solution.py:29
  31.2 0.6 teacher.5
  31.8 9.1 %collective-permute-start.3 = (bf16[64,640]{1,0:T(8,128)(2,1)S(1)}, bf16[64,640]{1,0:T(8,128)(2,1)S(1)}, u32[]{:S(2)}, u32[]{:S(2)}) collective-permute-start(bf16[64,640]{1,0:T(8,128)(2,1)S(1)} %get-tuple-element.33), channel_id=1, source_target_pairs={{0,128},{32,160},{64,192},{96,224},{128,256},{160,288},{192,320},{... | collective-permute-start | bytes 245768 | tf_op jit(solution)/shard_map/teacher/ppermute | solution.py:273
  40.9 7.1 %collective-permute-start.4 = (bf16[64,640]{1,0:T(8,128)(2,1)S(1)}, bf16[64,640]{1,0:T(8,128)(2,1)S(1)}, u32[]{:S(2)}, u32[]{:S(2)}) collective-permute-start(bf16[64,640]{1,0:T(8,128)(2,1)S(1)} %get-tuple-element.34), channel_id=1, source_target_pairs={{0,256},{32,288},{64,320},{96,352},{128,384},{160,416},{192,448},{... | collective-permute-start | bytes 245768 | tf_op jit(solution)/shard_map/teacher/ppermute | solution.py:273
  48.0 5.5 %collective-permute-start.5 = (bf16[64,640]{1,0:T(8,128)(2,1)S(1)}, bf16[64,640]{1,0:T(8,128)(2,1)S(1)}, u32[]{:S(2)}, u32[]{:S(2)}) collective-permute-start(bf16[64,640]{1,0:T(8,128)(2,1)S(1)} %get-tuple-element.35), channel_id=1, source_target_pairs={{0,384},{32,416},{64,448},{96,480},{128,0},{160,32},{192,64},{224,... | collective-permute-start | bytes 245768 | tf_op jit(solution)/shard_map/teacher/ppermute | solution.py:273
  53.4 2.5 %all-to-all-done = f16[8,1032,128]{2,1,0:T(8,128)(2,1)S(1)} async-done(((f16[8,1032,128]{2,1,0:T(8,128)(2,1)}), f16[8,1032,128]{2,1,0:T(8,128)(2,1)S(1)}, u32[]{:S(2)}, u32[]{:S(2)}) %all-to-all-start) | async-done | bytes 2113568 | tf_op jit(solution)/shard_map/prediction/all_to_all | solution.py:29
  56.0 0.3 convert_element_type.28
  56.3 1.4 fusion
  57.7 4.8 %collective-permute-done.4.t2_ref = bf16[64,640]{1,0:T(8,128)(2,1)S(1)} collective-permute-done((bf16[64,640]{1,0:T(8,128)(2,1)S(1)}, bf16[64,640]{1,0:T(8,128)(2,1)S(1)}, u32[]{:S(2)}, u32[]{:S(2)}) %collective-permute-start.4) | collective-permute-done | bytes 81952 | tf_op jit(solution)/shard_map/teacher/ppermute | solution.py:273
  62.5 1.4 gradient.1
  64.0 16.1 %all_to_all.25.g_ref.loss_ref = bf16[8,528,128]{2,1,0:T(8,128)(2,1)S(1)} all-to-all(bf16[8,528,128]{2,1,0:T(8,128)(2,1)S(1)} %get-tuple-element.37), channel_id=1, replica_groups=mesh['dp'=16,'seq'=4,'tensor'=8] {'tensor'}, dimensions={0} | all-to-all | bytes 2162688 | tf_op jit(solution)/shard_map/gradient/all_to_all | solution.py:29
  80.1 4.8 %all-to-all-start.2 = ((bf16[8,512,128]{2,1,0:T(8,128)(2,1)}), bf16[8,512,128]{2,1,0:T(8,128)(2,1)S(1)}, u32[]{:S(2)}, u32[]{:S(2)}) async-start(bf16[8,512,128]{2,1,0:T(8,128)(2,1)} %copy-done.5), calls=%async_computation.2 | async-start | bytes 2097152 | tf_op jit(solution)/shard_map/gradient/all_to_all | solution.py:29
  85.0 0.9 input_grad.2
  85.8 0.9 convert_element_type.29
  86.7 8.4 %collective-permute-start.6 = (f16[8,264,128]{2,1,0:T(8,128)(2,1)}, f16[8,264,128]{2,1,0:T(8,128)(2,1)}, u32[]{:S(2)}, u32[]{:S(2)}) collective-permute-start(f16[8,264,128]{2,1,0:T(8,128)(2,1)} %convert_element_type.29), channel_id=1, source_target_pairs={{0,32},{32,0},{64,96},{96,64},{128,160},{160,128},{192,224},{224,1... | collective-permute-start | bytes 1622024 | tf_op jit(solution)/shard_map/input_grad/ppermute | solution.py:324
  95.1 1.9 %collective-permute-start.7 = (f32[1,128]{1,0:T(1,128)S(1)}, f32[1,128]{1,0:T(1,128)S(1)}, u32[]{:S(2)}, u32[]{:S(2)}) collective-permute-start(f32[1,128]{1,0:T(1,128)S(1)} %get-tuple-element.40), channel_id=1, source_target_pairs={{0,8},{8,0},{16,24},{24,16},{1,9},{9,1},{17,25},{25,17},{2,10},{10... | collective-permute-start | bytes 1544 | tf_op jit(solution)/shard_map/input_grad/ppermute | solution.py:34
  97.1 1.1 collective-permute-done.7
  98.2 4.8 %collective-permute-start.8 = (f32[1,128]{1,0:T(1,128)S(1)}, f32[1,128]{1,0:T(1,128)S(1)}, u32[]{:S(2)}, u32[]{:S(2)}) collective-permute-start(f32[1,128]{1,0:T(1,128)S(1)} %add.35), channel_id=1, source_target_pairs={{0,16},{8,24},{16,0},{24,8},{1,17},{9,25},{17,1},{25,9},{2,18},{10... | collective-permute-start | bytes 1544 | tf_op jit(solution)/shard_map/input_grad/ppermute | solution.py:34
  103.0 2.1 %collective-permute-done.8 = f32[1,128]{1,0:T(1,128)S(1)} collective-permute-done((f32[1,128]{1,0:T(1,128)S(1)}, f32[1,128]{1,0:T(1,128)S(1)}, u32[]{:S(2)}, u32[]{:S(2)}) %collective-permute-start.8) | collective-permute-done | bytes 544 | tf_op jit(solution)/shard_map/input_grad/ppermute | solution.py:34
  105.1 2.0 %collective-permute-start.9 = (f32[1,128]{1,0:T(1,128)S(1)}, f32[1,128]{1,0:T(1,128)S(1)}, u32[]{:S(2)}, u32[]{:S(2)}) collective-permute-start(f32[1,128]{1,0:T(1,128)S(1)} %add.36), channel_id=1, source_target_pairs={{0,32},{32,0},{64,96},{96,64},{128,160},{160,128},{192,224},{224,1... | collective-permute-start | bytes 1544 | tf_op jit(solution)/shard_map/input_grad/ppermute | solution.py:34
  107.1 3.4 %collective-permute-done.9 = f32[1,128]{1,0:T(1,128)S(1)} collective-permute-done((f32[1,128]{1,0:T(1,128)S(1)}, f32[1,128]{1,0:T(1,128)S(1)}, u32[]{:S(2)}, u32[]{:S(2)}) %collective-permute-start.9) | collective-permute-done | bytes 544 | tf_op jit(solution)/shard_map/input_grad/ppermute | solution.py:34
  110.5 1.1 convert_element_type.30.got_ref
  111.7 0.9 input_grad.3.after_ref
  112.6 0.3 copy-done.4
  112.9 1.9 %weight_grad.1 = (f32[256,1024]{1,0:T(8,128)S(1)}, f32[256,1024]{1,0:T(8,128)S(1)}) custom-call(s32[4]{0:T(128)S(1)} %pad_add_fusion.place_ref, bf16[8,2,64,512]{3,2,1,0:T(8,128)(2,1)S(1)} %bitcast.16, bf16[8,2,64,512]{3,2,1,0:T(8,128)(2,1)S(1)} %bitcast.17, bf16[8,528,128]{2,1,0:T(8,128)(2,1)S(1)} %all_to_all.25.g_ref.loss_ref, ...), custom_call_target="tpu_custom_call" | custom-call | flops 1073741824 | bytes 5000000 | tf_op jit(solution)/shard_map/weight_grad/pallas_call | solution.py:343
  114.8 1.0 copy-done.6
  115.8 2.0 %collective-permute-start.10 = (f32[256,1024]{1,0:T(8,128)S(1)}, f32[256,1024]{1,0:T(8,128)}, u32[]{:S(2)}, u32[]{:S(2)}) collective-permute-start(f32[256,1024]{1,0:T(8,128)S(1)} %get-tuple-element.42), channel_id=1, source_target_pairs={{0,8},{8,0},{16,24},{24,16},{1,9},{9,1},{17,25},{25,17},{2,10},{10... | collective-permute-start | bytes 3145736 | tf_op jit(solution)/shard_map/weight_grad/ppermute | solution.py:365
  117.8 0.9 convert_element_type.31
  118.7 8.3 %all-to-all-start.4 = ((f16[8,264,128]{2,1,0:T(8,128)(2,1)}), f16[8,264,128]{2,1,0:T(8,128)(2,1)S(1)}, u32[]{:S(2)}, u32[]{:S(2)}) async-start(f16[8,264,128]{2,1,0:T(8,128)(2,1)} %convert_element_type.31), calls=%async_computation.4 | async-start | bytes 1081344 | tf_op jit(solution)/shard_map/input_grad/all_to_all | solution.py:336
  127.0 1.4 add_convert_fusion
  128.3 4.8 %collective-permute-start.11 = (bf16[256,1024]{1,0:T(8,128)(2,1)S(1)}, bf16[256,1024]{1,0:T(8,128)(2,1)S(1)}, u32[]{:S(2)}, u32[]{:S(2)}) collective-permute-start(bf16[256,1024]{1,0:T(8,128)(2,1)S(1)} %add_convert_fusion), channel_id=1, source_target_pairs={{0,16},{8,24},{16,0},{24,8},{1,17},{9,25},{17,1},{25,9},{2,18},{10... | collective-permute-start | bytes 1572872 | tf_op jit(solution)/shard_map/weight_grad/ppermute | solution.py:366
  133.2 12.6 %collective-permute-done.11 = bf16[256,1024]{1,0:T(8,128)(2,1)S(1)} collective-permute-done((bf16[256,1024]{1,0:T(8,128)(2,1)S(1)}, bf16[256,1024]{1,0:T(8,128)(2,1)S(1)}, u32[]{:S(2)}, u32[]{:S(2)}) %collective-permute-start.11) | collective-permute-done | bytes 524320 | tf_op jit(solution)/shard_map/weight_grad/ppermute | solution.py:366
  145.8 0.2 convert_add_fusion
  146.0 1.9 %collective-permute-start.12 = (f32[256,1024]{1,0:T(8,128)S(1)}, f32[256,1024]{1,0:T(8,128)S(1)}, u32[]{:S(2)}, u32[]{:S(2)}) collective-permute-start(f32[256,1024]{1,0:T(8,128)S(1)} %convert_add_fusion), channel_id=1, source_target_pairs={{0,8},{8,0},{16,24},{24,16},{1,9},{9,1},{17,25},{25,17},{2,10},{10... | collective-permute-start | bytes 3145736 | tf_op jit(solution)/shard_map/weight_grad/ppermute | solution.py:367
  147.9 11.5 %all-to-all-done.4 = f16[8,264,128]{2,1,0:T(8,128)(2,1)S(1)} async-done(((f16[8,264,128]{2,1,0:T(8,128)(2,1)}), f16[8,264,128]{2,1,0:T(8,128)(2,1)S(1)}, u32[]{:S(2)}, u32[]{:S(2)}) %all-to-all-start.4) | async-done | bytes 540704 | tf_op jit(solution)/shard_map/input_grad/all_to_all | solution.py:336
  159.5 0.3 maximum_select_fusion.after_ref
  159.8 0.8 results.1
  160.7 0.5 copy-done
  (27 shorter events, 0.2 us)
Async XLA Ops:
  0.6 12.0 %all-to-all-start.1 = ((bf16[8,8,2048]{2,1,0:T(8,128)(2,1)}), bf16[8,8,2048]{2,1,0:T(8,128)(2,1)S(1)}, u32[]{:S(2)}, u32[]{:S(2)}) async-start(bf16[8,8,2048]{2,1,0:T(8,128)(2,1)} %bitcast.21), calls=%async_computation.1 | async-start | bytes 524288 | tf_op jit(solution)/shard_map/teacher/all_to_all | solution.py:29
  6.5 1.2 copy-start.1
  7.7 1.2 copy-start.3
  13.4 17.8 %collective-permute-start = (bf16[64,640]{1,0:T(8,128)(2,1)S(1)}, bf16[64,640]{1,0:T(8,128)(2,1)S(1)}, u32[]{:S(2)}, u32[]{:S(2)}) collective-permute-start(bf16[64,640]{1,0:T(8,128)(2,1)S(1)} %get-tuple-element.29), channel_id=1, source_target_pairs={{0,32},{32,64},{64,96},{96,128},{128,160},{160,192},{192,224},{224... | collective-permute-start | bytes 245768 | tf_op jit(solution)/shard_map/teacher/ppermute | solution.py:261
  17.2 14.0 %collective-permute-start.1 = (bf16[64,640]{1,0:T(8,128)(2,1)S(1)}, bf16[64,640]{1,0:T(8,128)(2,1)S(1)}, u32[]{:S(2)}, u32[]{:S(2)}) collective-permute-start(bf16[64,640]{1,0:T(8,128)(2,1)S(1)} %get-tuple-element.30), channel_id=1, source_target_pairs={{0,64},{32,96},{64,128},{96,160},{128,192},{160,224},{192,256},{22... | collective-permute-start | bytes 245768 | tf_op jit(solution)/shard_map/teacher/ppermute | solution.py:261
  23.6 7.6 %collective-permute-start.2 = (bf16[64,640]{1,0:T(8,128)(2,1)S(1)}, bf16[64,640]{1,0:T(8,128)(2,1)S(1)}, u32[]{:S(2)}, u32[]{:S(2)}) collective-permute-start(bf16[64,640]{1,0:T(8,128)(2,1)S(1)} %get-tuple-element.31), channel_id=1, source_target_pairs={{0,480},{32,0},{64,32},{96,64},{128,96},{160,128},{192,160},{224,1... | collective-permute-start | bytes 245768 | tf_op jit(solution)/shard_map/teacher/ppermute | solution.py:261
  25.5 30.5 %all-to-all-start = ((f16[8,1032,128]{2,1,0:T(8,128)(2,1)}), f16[8,1032,128]{2,1,0:T(8,128)(2,1)S(1)}, u32[]{:S(2)}, u32[]{:S(2)}) async-start(f16[8,1032,128]{2,1,0:T(8,128)(2,1)} %convert_element_type.27), calls=%async_computation | async-start | bytes 4227072 | tf_op jit(solution)/shard_map/prediction/all_to_all | solution.py:29
  31.8 25.9 %collective-permute-start.3 = (bf16[64,640]{1,0:T(8,128)(2,1)S(1)}, bf16[64,640]{1,0:T(8,128)(2,1)S(1)}, u32[]{:S(2)}, u32[]{:S(2)}) collective-permute-start(bf16[64,640]{1,0:T(8,128)(2,1)S(1)} %get-tuple-element.33), channel_id=1, source_target_pairs={{0,128},{32,160},{64,192},{96,224},{128,256},{160,288},{192,320},{... | collective-permute-start | bytes 245768 | tf_op jit(solution)/shard_map/teacher/ppermute | solution.py:273
  40.9 21.6 %collective-permute-start.4 = (bf16[64,640]{1,0:T(8,128)(2,1)S(1)}, bf16[64,640]{1,0:T(8,128)(2,1)S(1)}, u32[]{:S(2)}, u32[]{:S(2)}) collective-permute-start(bf16[64,640]{1,0:T(8,128)(2,1)S(1)} %get-tuple-element.34), channel_id=1, source_target_pairs={{0,256},{32,288},{64,320},{96,352},{128,384},{160,416},{192,448},{... | collective-permute-start | bytes 245768 | tf_op jit(solution)/shard_map/teacher/ppermute | solution.py:273
  48.0 14.5 %collective-permute-start.5 = (bf16[64,640]{1,0:T(8,128)(2,1)S(1)}, bf16[64,640]{1,0:T(8,128)(2,1)S(1)}, u32[]{:S(2)}, u32[]{:S(2)}) collective-permute-start(bf16[64,640]{1,0:T(8,128)(2,1)S(1)} %get-tuple-element.35), channel_id=1, source_target_pairs={{0,384},{32,416},{64,448},{96,480},{128,0},{160,32},{192,64},{224,... | collective-permute-start | bytes 245768 | tf_op jit(solution)/shard_map/teacher/ppermute | solution.py:273
  63.9 16.2 %copy-start.5 = (bf16[8,512,128]{2,1,0:T(8,128)(2,1)}, bf16[8,512,128]{2,1,0:T(8,128)(2,1)S(1)}, u32[]{:S(2)}) copy-start(bf16[8,512,128]{2,1,0:T(8,128)(2,1)S(1)} %get-tuple-element.36) | copy-start | bytes 3145732
  63.9 21.0 %copy-start.2 = (bf16[512,1024]{1,0:T(8,128)(2,1)S(1)}, bf16[512,1024]{1,0:T(8,128)(2,1)}, u32[]{:S(2)}) copy-start(bf16[512,1024]{1,0:T(8,128)(2,1)} %w_ref.5) | copy-start | bytes 3145732
  80.1 30.4 %all-to-all-start.2 = ((bf16[8,512,128]{2,1,0:T(8,128)(2,1)}), bf16[8,512,128]{2,1,0:T(8,128)(2,1)S(1)}, u32[]{:S(2)}, u32[]{:S(2)}) async-start(bf16[8,512,128]{2,1,0:T(8,128)(2,1)} %copy-done.5), calls=%async_computation.2 | async-start | bytes 2097152 | tf_op jit(solution)/shard_map/gradient/all_to_all | solution.py:29
  86.7 23.8 %collective-permute-start.6 = (f16[8,264,128]{2,1,0:T(8,128)(2,1)}, f16[8,264,128]{2,1,0:T(8,128)(2,1)}, u32[]{:S(2)}, u32[]{:S(2)}) collective-permute-start(f16[8,264,128]{2,1,0:T(8,128)(2,1)} %convert_element_type.29), channel_id=1, source_target_pairs={{0,32},{32,0},{64,96},{96,64},{128,160},{160,128},{192,224},{224,1... | collective-permute-start | bytes 1622024 | tf_op jit(solution)/shard_map/input_grad/ppermute | solution.py:324
  95.1 3.0 %collective-permute-start.7 = (f32[1,128]{1,0:T(1,128)S(1)}, f32[1,128]{1,0:T(1,128)S(1)}, u32[]{:S(2)}, u32[]{:S(2)}) collective-permute-start(f32[1,128]{1,0:T(1,128)S(1)} %get-tuple-element.40), channel_id=1, source_target_pairs={{0,8},{8,0},{16,24},{24,16},{1,9},{9,1},{17,25},{25,17},{2,10},{10... | collective-permute-start | bytes 1544 | tf_op jit(solution)/shard_map/input_grad/ppermute | solution.py:34
  98.2 6.9 %collective-permute-start.8 = (f32[1,128]{1,0:T(1,128)S(1)}, f32[1,128]{1,0:T(1,128)S(1)}, u32[]{:S(2)}, u32[]{:S(2)}) collective-permute-start(f32[1,128]{1,0:T(1,128)S(1)} %add.35), channel_id=1, source_target_pairs={{0,16},{8,24},{16,0},{24,8},{1,17},{9,25},{17,1},{25,9},{2,18},{10... | collective-permute-start | bytes 1544 | tf_op jit(solution)/shard_map/input_grad/ppermute | solution.py:34
  105.1 5.4 %collective-permute-start.9 = (f32[1,128]{1,0:T(1,128)S(1)}, f32[1,128]{1,0:T(1,128)S(1)}, u32[]{:S(2)}, u32[]{:S(2)}) collective-permute-start(f32[1,128]{1,0:T(1,128)S(1)} %add.36), channel_id=1, source_target_pairs={{0,32},{32,0},{64,96},{96,64},{128,160},{160,128},{192,224},{224,1... | collective-permute-start | bytes 1544 | tf_op jit(solution)/shard_map/input_grad/ppermute | solution.py:34
  111.6 1.2 copy-start.4
  114.8 1.0 copy-start.6
  115.8 11.2 %copy-start.7 = (f32[256,1024]{1,0:T(8,128)S(1)}, f32[256,1024]{1,0:T(8,128)}, u32[]{:S(2)}) copy-start(f32[256,1024]{1,0:T(8,128)} %copy-done.6) | copy-start | bytes 3145732
  115.8 11.2 %collective-permute-start.10 = (f32[256,1024]{1,0:T(8,128)S(1)}, f32[256,1024]{1,0:T(8,128)}, u32[]{:S(2)}, u32[]{:S(2)}) collective-permute-start(f32[256,1024]{1,0:T(8,128)S(1)} %get-tuple-element.42), channel_id=1, source_target_pairs={{0,8},{8,0},{16,24},{24,16},{1,9},{9,1},{17,25},{25,17},{2,10},{10... | collective-permute-start | bytes 3145736 | tf_op jit(solution)/shard_map/weight_grad/ppermute | solution.py:365
  118.7 40.8 %all-to-all-start.4 = ((f16[8,264,128]{2,1,0:T(8,128)(2,1)}), f16[8,264,128]{2,1,0:T(8,128)(2,1)S(1)}, u32[]{:S(2)}, u32[]{:S(2)}) async-start(f16[8,264,128]{2,1,0:T(8,128)(2,1)} %convert_element_type.31), calls=%async_computation.4 | async-start | bytes 1081344 | tf_op jit(solution)/shard_map/input_grad/all_to_all | solution.py:336
  128.3 17.4 %collective-permute-start.11 = (bf16[256,1024]{1,0:T(8,128)(2,1)S(1)}, bf16[256,1024]{1,0:T(8,128)(2,1)S(1)}, u32[]{:S(2)}, u32[]{:S(2)}) collective-permute-start(bf16[256,1024]{1,0:T(8,128)(2,1)S(1)} %add_convert_fusion), channel_id=1, source_target_pairs={{0,16},{8,24},{16,0},{24,8},{1,17},{9,25},{17,1},{25,9},{2,18},{10... | collective-permute-start | bytes 1572872 | tf_op jit(solution)/shard_map/weight_grad/ppermute | solution.py:366
  146.0 13.6 %collective-permute-start.12 = (f32[256,1024]{1,0:T(8,128)S(1)}, f32[256,1024]{1,0:T(8,128)S(1)}, u32[]{:S(2)}, u32[]{:S(2)}) collective-permute-start(f32[256,1024]{1,0:T(8,128)S(1)} %convert_add_fusion), channel_id=1, source_target_pairs={{0,8},{8,0},{16,24},{24,16},{1,9},{9,1},{17,25},{25,17},{2,10},{10... | collective-permute-start | bytes 3145736 | tf_op jit(solution)/shard_map/weight_grad/ppermute | solution.py:367
  159.8 1.3 copy-start
